TPU v7x, 32 devices: a whole 2x2x4 slice. The times are simulated.
32 devices in a mesh: row: 8 (over y, x, core), col: 4 (over z).
Axes of the slice: x: 2, y: 2, z: 4, core: 2. Of those that a mesh axis runs over, the one named last changes fastest.
Arguments:
- aligned_family_embedding: bfloat16 [256, 384, 256], P('row', 'col'), may hold values from -24 to 24
- aligned_slot_available: int32 [256, 384], P('row', 'col'), may hold values from 0 to 1, as said below
- chain_site_available: int32 [384], replicated, may hold values 0 or 1
- duo_embedding: float32 [384, 384, 128], P('row', 'col'), may hold values from -1.2 to 1.2
- averaging_layernorm_stretch: float32 [256], replicated, may hold values from 0.1 to 1.9
- lineup_layernorm_stretch: float32 [256], replicated, may hold values from 0.1 to 1.9
- duo_layernorm_stretch: float32 [128], replicated, may hold values from 0.1 to 1.9
- lefthand_linear_kernel: bfloat16 [256, 32], replicated, may hold values from -0.375 to 0.375
- righthand_linear_kernel: bfloat16 [256, 32], replicated, may hold values from -0.375 to 0.375
- kronecker_linear_kernel: bfloat16 [1024, 128], replicated, may hold values from -0.1875 to 0.1875
- duo_logit_kernel: bfloat16 [128, 8], replicated, may hold values from -0.75 to 0.75
- asker_lookup_sigmoid_kernel: bfloat16 [256, 1024], replicated, may hold values from -8 to 8
- closing_linear_kernel: bfloat16 [256, 256], replicated, may hold values from -0.375 to 0.375
Outputs:
- refreshed_family_embedding: bfloat16 [256, 384, 256], P('row', 'col')
- duo_after_averaging: float32 [384, 384, 128], P('row', 'col')
Inputs may be any that keep to these rules, and one draw needn't show every extreme that they name: `aligned_slot_available`: 0 or 1; sequence 0 is present at every residue.
All inputs are finite; a program needn't handle non-finite values.
Results may differ from a plain program's by a relative error of at most 0.0052.
Values may be sent and summed in bfloat16 or wider, within the bound.
No kernel may reach another device: no remote copies, remote signals or barrier semaphores. Data moves between devices by JAX's collectives and lax.ppermute only.
A program may use at most 192 MiB of HBM per device.

v0:
```python
import jax
import jax.numpy as jnp
from jax import lax
from jax.sharding import PartitionSpec as P

EPSILON = 1e-05
CONTRACT_FIRST = (((0,), (0,)), ((), ()))


def spread(x, axis, root):
    mine = lax.axis_index(axis) == root
    return lax.psum(jnp.where(mine, x, jnp.zeros_like(x)), axis)


def standardize_features(values):
    average = jnp.mean(values, axis=-1, keepdims=True)
    centred = values - average
    variance = jnp.mean(centred * centred, axis=-1, keepdims=True)
    return centred * lax.rsqrt(variance + EPSILON)


def project_rows(inputs, weight, availability_real):
    projected = jnp.einsum("src,ca->sra", inputs, weight, preferred_element_type=jnp.float32)
    return (projected * availability_real[:, :, None]).astype(jnp.bfloat16)


def attend(queries, gate_pre, keys_all, values_all, key_mask, bias_rows, head_count):
    homolog_number, query_count, inner_width = queries.shape
    key_count = keys_all.shape[1]
    head_dim = inner_width // head_count
    block_rows = 1
    while (
        block_rows < homolog_number
        and block_rows * query_count < 512
        and (homolog_number % (2 * block_rows) == 0)
    ):
        block_rows = 2 * block_rows
    groups = homolog_number // block_rows
    score_scale = head_dim ** (-0.5)
    bias_float = bias_rows.astype(jnp.float32)

    def one_block(group_members):
        block_query, block_gate, block_key, block_value, block_mask = group_members
        query_heads = block_query.reshape(block_rows, query_count, head_count, head_dim)
        key_heads = block_key.reshape(block_rows, key_count, head_count, head_dim)
        value_heads = block_value.reshape(block_rows, key_count, head_count, head_dim)
        scores = jnp.einsum(
            "bqhd,bkhd->bhqk", query_heads, key_heads, preferred_element_type=jnp.float32
        )
        scores = (
            scores * score_scale
            + bias_float[None]
            + 1000000000.0 * (block_mask.astype(jnp.float32)[:, None, None, :] - 1.0)
        )
        highest = jnp.max(scores, axis=-1, keepdims=True)
        exponent = jnp.exp(scores - highest)
        weights = (exponent / jnp.sum(exponent, axis=-1, keepdims=True)).astype(jnp.bfloat16)
        mixed_rows = jnp.einsum(
            "bhqk,bkhd->bqhd", weights, value_heads, preferred_element_type=jnp.float32
        )
        mixed_rows = mixed_rows.reshape(block_rows, query_count, inner_width)
        return (mixed_rows * jax.nn.sigmoid(block_gate.astype(jnp.float32))).astype(jnp.bfloat16)

    def grouped(array):
        return array.reshape((groups, block_rows) + array.shape[1:])

    gated_row_output = lax.map(
        one_block,
        (
            grouped(queries),
            grouped(gate_pre),
            grouped(keys_all),
            grouped(values_all),
            grouped(key_mask),
        ),
    )
    return gated_row_output.reshape(homolog_number, query_count, inner_width)


def shards(
    aligned_family_embedding,
    aligned_slot_available,
    chain_site_available,
    duo_embedding,
    averaging_layernorm_stretch,
    lineup_layernorm_stretch,
    duo_layernorm_stretch,
    lefthand_linear_kernel,
    righthand_linear_kernel,
    kronecker_linear_kernel,
    duo_logit_kernel,
    asker_lookup_sigmoid_kernel,
    closing_linear_kernel,
):
    homolog_number, amino_position_number, discarded_carry = aligned_family_embedding.shape
    res_rows = duo_embedding.shape[0]
    opm_width = lefthand_linear_kernel.shape[1]
    head_count = duo_logit_kernel.shape[1]
    inner_width = closing_linear_kernel.shape[0]
    row_index = lax.axis_index("row")
    col_index = lax.axis_index("col")
    half_index = row_index % 2
    owner_index = row_index // 2
    standardized_features = standardize_features(aligned_family_embedding.astype(jnp.float32))
    availability_real = aligned_slot_available.astype(jnp.float32)
    shrunk_availability = aligned_slot_available.astype(jnp.bfloat16)
    opm_input = (standardized_features * averaging_layernorm_stretch).astype(jnp.bfloat16)
    left_flat = project_rows(opm_input, lefthand_linear_kernel, availability_real).reshape(
        homolog_number, amino_position_number * opm_width
    )
    right_flat = project_rows(opm_input, righthand_linear_kernel, availability_real).reshape(
        homolog_number, amino_position_number * opm_width
    )
    left_all, right_all, mask_all = (
        lax.all_gather(left_flat, "row", axis=0, tiled=True),
        lax.all_gather(right_flat, "row", axis=0, tiled=True),
        lax.all_gather(shrunk_availability, "row", axis=0, tiled=True),
    )
    picked = (
        lax.dynamic_slice_in_dim(
            left_all, half_index * res_rows * opm_width, res_rows * opm_width, 1
        ),
        lax.dynamic_slice_in_dim(mask_all, half_index * res_rows, res_rows, 1),
    )
    left_block, left_mask = (
        spread(picked[0], "col", owner_index),
        spread(picked[1], "col", owner_index),
    )
    outer_sum = lax.dot_general(
        left_block, right_all, CONTRACT_FIRST, preferred_element_type=jnp.float32
    )
    counts = lax.dot_general(
        left_mask, mask_all, CONTRACT_FIRST, preferred_element_type=jnp.float32
    )
    outer_narrow = outer_sum.astype(jnp.bfloat16).reshape(
        res_rows, opm_width, amino_position_number, opm_width
    )
    mixing = kronecker_linear_kernel.reshape(opm_width, opm_width, kronecker_linear_kernel.shape[1])
    update = jnp.einsum("iajb,abk->ijk", outer_narrow, mixing, preferred_element_type=jnp.float32)
    residue_float = chain_site_available.astype(jnp.float32)
    residue_rows = lax.dynamic_slice_in_dim(residue_float, row_index * res_rows, res_rows)
    residue_cols = lax.dynamic_slice_in_dim(
        residue_float, col_index * amino_position_number, amino_position_number
    )
    update = (
        update
        / (counts + 0.001)[:, :, None]
        * (residue_rows[:, None] * residue_cols[None, :])[:, :, None]
    )
    duo_after_averaging = duo_embedding + update
    pair_input = (standardize_features(duo_after_averaging) * duo_layernorm_stretch).astype(
        jnp.bfloat16
    )
    bias_tile = jnp.einsum(
        "ijc,ch->hij", pair_input, duo_logit_kernel, preferred_element_type=jnp.float32
    ).astype(jnp.bfloat16)
    bias_cols = lax.all_gather(bias_tile, "col", axis=2, tiled=True)
    exponential_probabilities = (standardized_features * lineup_layernorm_stretch).astype(
        jnp.bfloat16
    )
    rows_input, rows_mask = (
        lax.all_to_all(exponential_probabilities, "col", split_axis=0, concat_axis=1, tiled=True),
        lax.all_to_all(shrunk_availability, "col", split_axis=0, concat_axis=1, tiled=True),
    )
    bias_whole = lax.all_gather(bias_cols, "row", axis=1, tiled=True)
    projected = jnp.einsum(
        "src,cd->srd", rows_input, asker_lookup_sigmoid_kernel, preferred_element_type=jnp.float32
    ).astype(jnp.bfloat16)
    gated_whole = attend(
        projected[..., :inner_width],
        projected[..., 3 * inner_width :],
        projected[..., inner_width : 2 * inner_width],
        projected[..., 2 * inner_width : 3 * inner_width],
        rows_mask,
        bias_whole,
        head_count,
    )
    gated_local = lax.all_to_all(gated_whole, "col", split_axis=1, concat_axis=0, tiled=True)
    summed_increment = jnp.einsum(
        "sqd,dc->sqc", gated_local, closing_linear_kernel, preferred_element_type=jnp.float32
    )
    refreshed_family_embedding = (
        aligned_family_embedding.astype(jnp.float32) + summed_increment
    ).astype(jnp.bfloat16)
    return (refreshed_family_embedding, duo_after_averaging)


def solution(mesh):
    placed = (
        P("row", "col", None),
        P("row", "col"),
        P(),
        P("row", "col", None),
        P(),
        P(),
        P(),
        P(),
        P(),
        P(),
        P(),
        P(),
        P(),
    )
    return jax.shard_map(
        shards,
        mesh=mesh,
        in_specs=placed,
        out_specs=(P("row", "col", None), P("row", "col", None)),
        check_vma=False,
    )
```

profile of v0, /device:TPU:0, one launch (start us, length us, event | category | flops | bytes accessed | tf_op | source)
XLA Modules:
  0.0 397.9 jit_solution(1644607154977162668)
XLA Ops:
  7.3 2.2 convert_reduce_fusion
  9.5 1.0 fusion.16
  10.5 0.6 fusion.34
  11.1 1.3 fusion.20
  12.4 0.4 copy.54
  12.8 1.5 reshape.145
  14.4 1.3 fusion.21
  15.7 0.4 copy.55
  16.0 1.5 reshape.146
  17.7 25.2 %all-gather.4.cloned.1.call-done = bf16[256,3072]{1,0:T(8,128)(2,1)} async-done(((bf16[32,3072]{1,0:T(8,128)(2,1)}), bf16[256,3072]{1,0:T(8,128)(2,1)}) %all-gather.4.cloned.1.call-update) | async-done | bytes 1572880 | tf_op jit(solution)/shard_map/all_gather | solution.py:115
  42.9 2.1 dynamic-slice_select_fusion
  45.3 9.2 %all_gather.17 = bf16[256,96]{1,0:T(8,128)(2,1)S(1)} all-gather(bf16[32,96]{1,0:T(8,128)(2,1)} %get-tuple-element.162), channel_id=1, replica_groups=mesh['row'=8,'col'=4] {'row'}, dimensions={0}, use_global_device_ids=true | all-gather | bytes 55296 | tf_op jit(solution)/shard_map/all_gather | solution.py:117
  54.5 19.6 %psum.15 = bf16[256,48]{1,0:T(8,128)(2,1)S(1)} all-reduce(bf16[256,48]{1,0:T(8,128)(2,1)S(1)} %dynamic-slice_select_fusion.1), channel_id=1, replica_groups=mesh['row'=8,'col'=4] {'col'}, use_global_device_ids=true, to_apply=%region_3.4 | all-reduce | flops 12288 | bytes 49152 | tf_op jit(solution)/shard_map/psum | solution.py:12
  74.4 43.3 %all-reduce.2.cloned.1.call-done = bf16[256,1536]{1,0:T(8,128)(2,1)} async-done(((bf16[256,1536]{1,0:T(8,128)(2,1)}), bf16[256,1536]{1,0:T(8,128)(2,1)}) %all-reduce.2.cloned.1.call-update) | async-done | bytes 786448 | tf_op jit(solution)/shard_map/psum | solution.py:12
  117.7 7.9 %convolution_convert_fusion = bf16[1536,3072]{1,0:T(8,128)(2,1)} fusion(bf16[256,1536]{1,0:T(8,128)(2,1)} %all-reduce.2.cloned.1.call-done, bf16[256,3072]{1,0:T(8,128)(2,1)} %all-gather.6.cloned.1.call-done), kind=kOutput, calls=%fused_computation.20 | convolution fusion | flops 2420637696 | bytes 11796480 | tf_op jit(solution)/shard_map/dot_general | solution.py:129
  125.7 41.0 %reshape.147 = bf16[48,32,96,32]{3,2,1,0:T(8,128)(2,1)} reshape(bf16[1536,3072]{1,0:T(8,128)(2,1)} %convolution_convert_fusion) | data formatting | bytes 18874368 | tf_op jit(solution)/shard_map/reshape | solution.py:135
  166.6 17.0 %fusion.35 = (f32[48,96]{1,0:T(8,128)S(1)}, f32[48,96,128]{2,1,0:T(8,128)S(1)}) fusion(f32[48,96,128]{2,1,0:T(8,128)} %param.18, f32[48,96]{1,0:T(8,128)S(1)} %broadcast_multiply_fusion.1, f32[48,96]{1,0:T(8,128)S(1)} %convolution_add_fusion, bf16[48,32,96,32]{3,2,1,0:T(8,128)(2,1)} %reshape.147, bf16[32,32,128,1]{2,1,0,3:T(8,128)(2,1)S(1)} %bitcast.92), kind=kOutput, calls=%fused_computation.61 | convolution fusion | flops 1210314240 | bytes 14473216 | tf_op jit(solution)/shard_map/iajb,abk->ijk/dot_general | solution.py:139
  183.7 1.7 multiply_reduce_fusion
  185.4 2.0 fusion.24
  187.6 18.0 %all_gather.18 = bf16[8,48,384]{1,0,2:T(8,128)(2,1)S(1)} all-gather(bf16[8,48,96]{1,0,2:T(8,128)(2,1)S(1)} %copy.57), channel_id=1, replica_groups=mesh['row'=8,'col'=4] {'col'}, dimensions={2}, use_global_device_ids=true | all-gather | bytes 368640 | tf_op jit(solution)/shard_map/all_gather | solution.py:157
  205.6 1.3 copy.58
  206.9 3.3 all-to-all-start.1
  210.3 1.9 fusion.14
  212.1 3.7 all-to-all-done.1
  215.9 4.6 %all-to-all-start = ((bf16[32,96,256]{2,1,0:T(8,128)(2,1)}), bf16[32,96,256]{2,1,0:T(8,128)(2,1)}, u32[]{:S(2)}, u32[]{:S(2)}) async-start(bf16[32,96,256]{2,1,0:T(8,128)(2,1)} %fusion.14), calls=%async_computation | async-start | bytes 3145728 | tf_op jit(solution)/shard_map/all_to_all | solution.py:162
  220.5 33.2 %all-to-all-done = bf16[32,96,256]{2,1,0:T(8,128)(2,1)} async-done(((bf16[32,96,256]{2,1,0:T(8,128)(2,1)}), bf16[32,96,256]{2,1,0:T(8,128)(2,1)}, u32[]{:S(2)}, u32[]{:S(2)}) %all-to-all-start) | async-done | bytes 1572896 | tf_op jit(solution)/shard_map/all_to_all | solution.py:162
  253.7 1.5 copy.53
  255.3 1.8 convolution_convert_fusion.1
  257.1 2.9 fusion.33
  260.0 5.1 %copy.63 = f32[8,384,384]{1,2,0:T(8,128)} copy(bf16[8,384,384]{2,0,1:T(8,128)(2,1)} %all-gather.8.cloned.1.call-done) | data formatting | bytes 7077888 | tf_op jit(solution)/shard_map/while | solution.py:67
  265.1 80.7 %while.12 = (s32[]{:T(128)}, bf16[4,2,384,256]{2,3,1,0:T(8,128)(2,1)}, bf16[4,2,384,256]{3,2,1,0:T(8,128)(2,1)}, bf16[4,2,384,256]{3,2,1,0:T(8,128)(2,1)}, bf16[...) while((s32[]{:T(128)}, ...), condition=%wide.region_9.10_spmd, body=%wide.region_6.9_spmd.sunk | while | flops 319687296 | bytes 33480808 | solution.py:67
  265.1 1.2 constant_dynamic-slice_fusion.8
  266.5 1.2 constant_dynamic-slice_fusion.7
  267.7 0.9 copy.84
  268.6 9.9 %fusion.57 = (f32[2,8,384]{2,1,0:T(8,128)S(1)}, f32[2,8,384,384]{2,3,1,0:T(8,128)}) fusion(f32[2,384]{1,0:T(2,128)S(1)} %multiply_bitcast_fusion.2, f32[8,384,384]{1,2,0:T(8,128)} %get-tuple-element.250, bf16[2,384,8,32]{1,3,2,0:T(8,128)(2,1)S(1)} %bitcast.80, bf16[2,384,8,32]{1,3,2,0:T(8,128)(2,1)} %bitcast.81), kind=kOutput, calls=%fused_computation.58.clone.1 | convolution fusion | flops 162791808 | bytes 14969856 | tf_op jit(solution)/shard_map/while/body/eval_jaxpr/sub | solution.py:56
  278.5 0.9 copy.82
  279.4 4.6 %fusion.58 = f32[2,8,32,384]{3,2,1,0:T(8,128)S(1)} fusion(bf16[2,384,8,32]{1,3,2,0:T(8,128)(2,1)} %bitcast.82, f32[2,8,384,384]{2,3,1,0:T(8,128)} %get-tuple-element.225, f32[2,8,384]{2,1,0:T(8,128)S(1)} %get-tuple-element.226), kind=kOutput, calls=%fused_computation.8.clone.1 | convolution fusion | flops 155713536 | bytes 10641408 | tf_op jit(solution)/shard_map/while/body/eval_jaxpr/bhqk,bkhd->bqhd/dot_general | solution.py:58
  284.3 1.0 constant_dynamic-update-slice_fusion.2
  285.3 1.2 constant_dynamic-slice_fusion.8
  286.6 1.2 constant_dynamic-slice_fusion.7
  287.8 0.9 copy.84
  288.7 9.9 %fusion.57 = (f32[2,8,384]{2,1,0:T(8,128)S(1)}, f32[2,8,384,384]{2,3,1,0:T(8,128)}) fusion(f32[2,384]{1,0:T(2,128)S(1)} %multiply_bitcast_fusion.2, f32[8,384,384]{1,2,0:T(8,128)} %get-tuple-element.250, bf16[2,384,8,32]{1,3,2,0:T(8,128)(2,1)S(1)} %bitcast.80, bf16[2,384,8,32]{1,3,2,0:T(8,128)(2,1)} %bitcast.81), kind=kOutput, calls=%fused_computation.58.clone.1 | convolution fusion | flops 162791808 | bytes 14969856 | tf_op jit(solution)/shard_map/while/body/eval_jaxpr/sub | solution.py:56
  298.7 0.9 copy.82
  299.6 4.6 %fusion.58 = f32[2,8,32,384]{3,2,1,0:T(8,128)S(1)} fusion(bf16[2,384,8,32]{1,3,2,0:T(8,128)(2,1)} %bitcast.82, f32[2,8,384,384]{2,3,1,0:T(8,128)} %get-tuple-element.225, f32[2,8,384]{2,1,0:T(8,128)S(1)} %get-tuple-element.226), kind=kOutput, calls=%fused_computation.8.clone.1 | convolution fusion | flops 155713536 | bytes 10641408 | tf_op jit(solution)/shard_map/while/body/eval_jaxpr/bhqk,bkhd->bqhd/dot_general | solution.py:58
  304.5 1.0 constant_dynamic-update-slice_fusion.2
  305.4 1.2 constant_dynamic-slice_fusion.8
  306.8 1.2 constant_dynamic-slice_fusion.7
  308.0 0.9 copy.84
  308.9 9.9 %fusion.57 = (f32[2,8,384]{2,1,0:T(8,128)S(1)}, f32[2,8,384,384]{2,3,1,0:T(8,128)}) fusion(f32[2,384]{1,0:T(2,128)S(1)} %multiply_bitcast_fusion.2, f32[8,384,384]{1,2,0:T(8,128)} %get-tuple-element.250, bf16[2,384,8,32]{1,3,2,0:T(8,128)(2,1)S(1)} %bitcast.80, bf16[2,384,8,32]{1,3,2,0:T(8,128)(2,1)} %bitcast.81), kind=kOutput, calls=%fused_computation.58.clone.1 | convolution fusion | flops 162791808 | bytes 14969856 | tf_op jit(solution)/shard_map/while/body/eval_jaxpr/sub | solution.py:56
  318.8 0.9 copy.82
  319.8 4.6 %fusion.58 = f32[2,8,32,384]{3,2,1,0:T(8,128)S(1)} fusion(bf16[2,384,8,32]{1,3,2,0:T(8,128)(2,1)} %bitcast.82, f32[2,8,384,384]{2,3,1,0:T(8,128)} %get-tuple-element.225, f32[2,8,384]{2,1,0:T(8,128)S(1)} %get-tuple-element.226), kind=kOutput, calls=%fused_computation.8.clone.1 | convolution fusion | flops 155713536 | bytes 10641408 | tf_op jit(solution)/shard_map/while/body/eval_jaxpr/bhqk,bkhd->bqhd/dot_general | solution.py:58
  324.6 1.0 constant_dynamic-update-slice_fusion.2
  325.6 1.2 constant_dynamic-slice_fusion.8
  327.0 1.2 constant_dynamic-slice_fusion.7
  328.1 0.9 copy.84
  329.1 9.9 %fusion.57 = (f32[2,8,384]{2,1,0:T(8,128)S(1)}, f32[2,8,384,384]{2,3,1,0:T(8,128)}) fusion(f32[2,384]{1,0:T(2,128)S(1)} %multiply_bitcast_fusion.2, f32[8,384,384]{1,2,0:T(8,128)} %get-tuple-element.250, bf16[2,384,8,32]{1,3,2,0:T(8,128)(2,1)S(1)} %bitcast.80, bf16[2,384,8,32]{1,3,2,0:T(8,128)(2,1)} %bitcast.81), kind=kOutput, calls=%fused_computation.58.clone.1 | convolution fusion | flops 162791808 | bytes 14969856 | tf_op jit(solution)/shard_map/while/body/eval_jaxpr/sub | solution.py:56
  339.0 0.9 copy.82
  339.9 4.6 %fusion.58 = f32[2,8,32,384]{3,2,1,0:T(8,128)S(1)} fusion(bf16[2,384,8,32]{1,3,2,0:T(8,128)(2,1)} %bitcast.82, f32[2,8,384,384]{2,3,1,0:T(8,128)} %get-tuple-element.225, f32[2,8,384]{2,1,0:T(8,128)S(1)} %get-tuple-element.226), kind=kOutput, calls=%fused_computation.8.clone.1 | convolution fusion | flops 155713536 | bytes 10641408 | tf_op jit(solution)/shard_map/while/body/eval_jaxpr/bhqk,bkhd->bqhd/dot_general | solution.py:58
  344.8 1.0 constant_dynamic-update-slice_fusion.2
  345.7 3.0 copy.71
  348.7 40.0 %all_to_all.52 = bf16[8,384,256]{2,0,1:T(8,128)(2,1)S(1)} all-to-all(bf16[8,384,256]{2,0,1:T(8,128)(2,1)} %copy.71), channel_id=1, replica_groups=mesh['row'=8,'col'=4] {'col'}, dimensions={1} | all-to-all | bytes 3145728 | tf_op jit(solution)/shard_map/all_to_all | solution.py:178
  388.7 0.4 copy.67
  389.1 0.5 copy-done.4
  389.6 1.7 fusion.17
  (63 shorter events, 2.9 us)
Async XLA Ops:
  7.2 248.1 %copy-start = (bf16[256,1024]{1,0:T(8,128)(2,1)S(1)}, bf16[256,1024]{1,0:T(8,128)(2,1)}, u32[]{:S(2)}) copy-start(bf16[256,1024]{1,0:T(8,128)(2,1)} %param.26) | copy-start | bytes 1572868
  7.2 2.3 copy-start.2
  7.2 3.3 copy-start.5
  7.2 3.9 copy-start.13
  7.2 3.9 copy-start.11
  7.2 35.6 %all-gather.4.cloned.1.call-start = ((), (), s32[]{:S(2)}) async-start(), calls=%async_computation.3 | async-start | bytes 1769472 | tf_op jit(solution)/shard_map/all_gather | solution.py:115
  11.1 3.2 copy-start.12
  14.3 60.1 %all-gather.6.cloned.1.call-start = ((), (), s32[]{:S(2)}) async-start(), calls=%async_computation.5 | async-start | bytes 1769472 | tf_op jit(solution)/shard_map/all_gather | solution.py:116
  15.7 29.4 %copy-start.7 = (s32[384]{0:T(512)S(1)}, s32[384]{0:T(512)}, u32[]{:S(2)}) copy-start(s32[384]{0:T(512)} %param.17) | copy-start | bytes 4612
  17.6 100.1 %all-reduce.2.cloned.1.call-start = ((), (), s32[]{:S(2)}) async-start(), calls=%async_computation.4 | async-start | bytes 1572864 | tf_op jit(solution)/shard_map/psum | solution.py:12
  45.0 214.9 %all-gather.8.cloned.1.call-start = ((), (), s32[]{:S(2)}) async-start(), calls=%async_computation.6 | async-start | bytes 2654208 | tf_op jit(solution)/shard_map/all_gather | solution.py:165
  125.6 41.0 %copy-start.10 = (bf16[1024,128]{1,0:T(8,128)(2,1)S(1)}, bf16[1024,128]{1,0:T(8,128)(2,1)}, u32[]{:S(2)}) copy-start(bf16[1024,128]{1,0:T(8,128)(2,1)} %param.24) | copy-start | bytes 786436
  183.6 1.7 copy-start.3
  183.7 1.7 copy-start.6
  183.7 1.7 copy-start.9
  185.4 24.9 %copy-start.8 = (f32[256]{0:T(256)S(1)}, f32[256]{0:T(256)}, u32[]{:S(2)}) copy-start(f32[256]{0:T(256)} %param.20) | copy-start | bytes 3076
  206.9 8.9 %all-to-all-start.1 = ((bf16[4,8,96]{2,1,0:T(8,128)(2,1)}), bf16[4,8,96]{2,1,0:T(8,128)(2,1)S(1)}, u32[]{:S(2)}, u32[]{:S(2)}) async-start(bf16[4,8,96]{2,1,0:T(8,128)(2,1)} %bitcast.21), calls=%async_computation.1 | async-start | bytes 16384 | tf_op jit(solution)/shard_map/all_to_all | solution.py:163
  215.9 37.9 %all-to-all-start = ((bf16[32,96,256]{2,1,0:T(8,128)(2,1)}), bf16[32,96,256]{2,1,0:T(8,128)(2,1)}, u32[]{:S(2)}, u32[]{:S(2)}) async-start(bf16[32,96,256]{2,1,0:T(8,128)(2,1)} %fusion.14), calls=%async_computation | async-start | bytes 3145728 | tf_op jit(solution)/shard_map/all_to_all | solution.py:162
  388.7 0.9 copy-start.4
  389.1 2.3 copy-start.1
Sparse Core Ops, SparseCore 0:
  14.4 28.3 all-gather.3
  45.3 25.6 all-gather.5
  74.0 43.6 all-reduce.1
  207.1 28.6 all-gather.7
where the time goes:
time: 400 us; the launch traced here: 398 us
  waiting for transfers between devices  105 us (26%)
  matrix products  91.4 us (23%)
  blocking collectives  86.8 us (22%)
  local copies, waits for them, and re-layouts  78.4 us (20%)
  between operations  14.1 us (4%)
  other arithmetic  13.5 us (3%)
  starting transfers between devices  8.06 us (2%)
    psum x1, waiting for transfers between devices, spread(): return lax.psum(jnp.where(mine, x, jnp.zeros_like(x)), axis)  43.3 us
    reshape x1, local copies, waits for them, and re-layouts, shards(): outer_sum.astype(jnp.bfloat16)  41 us
    all_to_all x1, blocking collectives, shards(): lax.all_to_all(gated_whole, 'col', split_axis=1, concat_axis=0, tiled=True)  40 us
    sub x4, matrix products, one_block(): exponent = jnp.exp(scores - highest)  39.7 us
    all_to_all x1, waiting for transfers between devices, shards(): lax.all_to_all(exponential_probabilities, 'col', split_axis=0, concat_axi...  33.2 us
    all_gather x1, waiting for transfers between devices, shards(): lax.all_gather(left_flat, 'row', axis=0, tiled=True)  25.2 us
    psum x1, blocking collectives, spread(): return lax.psum(jnp.where(mine, x, jnp.zeros_like(x)), axis)  19.6 us
    dot_general x4, matrix products, one_block(): jnp.einsum('bhqk,bkhd->bqhd', weights, value_heads, preferred_element_typ...  18.5 us
  transfers between devices with their start and end apart: 6, of which 4 were waited for; matrix products, arithmetic and copies ran while one was open for 4% of the time, Pallas kernels for 0%

commit v1 on v0

v1 whole, which is shorter than its diff:
```python
import math

import jax
import jax.numpy as jnp
from jax import lax
from jax.experimental import pallas as pl
from jax.experimental.pallas import tpu as pltpu
from jax.sharding import PartitionSpec as P

EPSILON = 1e-05
LOG2E = math.log2(math.e)
LANES = 128
ROWS_BY_ROWS = (((1,), (1,)), ((), ()))
CONTRACT_FIRST = (((0,), (0,)), ((), ()))
VMEM = pltpu.CompilerParams(vmem_limit_bytes=56 * 2**20)
SMEM = pl.BlockSpec(memory_space=pltpu.SMEM)
f32 = jnp.float32
bf16 = jnp.bfloat16


def whole(array):
    return pl.BlockSpec(array.shape, lambda step, rank=array.ndim: (0,) * rank)


def standardize(values):
    average = jnp.mean(values, axis=-1, keepdims=True)
    centred = values - average
    variance = jnp.mean(centred * centred, axis=-1, keepdims=True)
    return centred * lax.rsqrt(variance + EPSILON)


def opm_inputs_kernel(half_ref, x_ref, mask_ref, gain_ref, wl_ref, wr_ref, left_ref, right_ref, scratch):
    seqs, residues, channels = x_ref.shape
    width = wr_ref.shape[0]
    per_group = LANES // width
    groups = residues // per_group
    halves, slabs = left_ref.shape[:2]
    half_groups = slabs - 1
    half_residues = residues // halves
    normed = standardize(x_ref[...].reshape(seqs * residues, channels).astype(f32)) * gain_ref[...]
    for piece in range(channels // LANES):
        scratch[piece] = normed[:, piece * LANES : (piece + 1) * LANES]
    narrow = normed.astype(bf16).reshape(seqs, residues, channels)
    mask = mask_ref[...].astype(f32)
    right = [
        lax.dot_general(wr_ref[...], narrow[s], ROWS_BY_ROWS, preferred_element_type=f32) * mask[s : s + 1, :]
        for s in range(seqs)
    ]
    right_ref[:width] = jnp.swapaxes(jnp.stack(right, 0), 0, 1).astype(bf16)
    right_ref[width] = mask.astype(bf16)
    total = None
    for q in range(per_group):
        rows = jnp.concatenate(
            [scratch[piece, pl.ds(q, seqs * groups, stride=per_group), :] for piece in range(channels // LANES)], 1
        ).astype(bf16)
        part = jnp.dot(rows, wl_ref[q], preferred_element_type=f32)
        total = part if total is None else total + part
    left = jnp.swapaxes(total.reshape(seqs, groups, LANES), 0, 1)
    row = lax.broadcasted_iota(jnp.int32, (residues, residues * width), 0) * width
    col = lax.broadcasted_iota(jnp.int32, (residues, residues * width), 1)
    spread = ((col >= row) & (col < row + width)).astype(f32).astype(bf16)
    mask_wide = jnp.dot(mask.astype(bf16), spread, preferred_element_type=f32)
    flip = half_ref[0]
    for g in range(groups):
        half = g // half_groups
        slot = half + flip - 2 * half * flip
        left_ref[slot, g % half_groups] = (left[g] * mask_wide[:, g * LANES : (g + 1) * LANES]).astype(bf16)
    for half in range(halves):
        slot = half + flip - 2 * half * flip
        part = mask[:, half * half_residues : (half + 1) * half_residues]
        left_ref[slot, half_groups] = jnp.concatenate(
            [part, jnp.zeros((seqs, LANES - half_residues), f32)], 1
        ).astype(bf16)


def opm_inputs(flip, x, mask, gain, wl, wr, half_residues, block=16):
    seqs, residues, channels = x.shape
    width = wl.shape[1]
    per_group = LANES // width
    halves = residues // half_residues
    slabs = half_residues // per_group + 1
    wide = jnp.stack([jnp.pad(wl, ((0, 0), (q * width, LANES - (q + 1) * width))) for q in range(per_group)])
    gain = gain.reshape(1, channels)
    return pl.pallas_call(
        opm_inputs_kernel,
        grid=(seqs // block,),
        in_specs=[
            SMEM,
            pl.BlockSpec((block, residues, channels), lambda s: (s, 0, 0)),
            pl.BlockSpec((block, residues), lambda s: (s, 0)),
            whole(gain),
            whole(wide),
            pl.BlockSpec((width, channels), lambda s: (0, 0)),
        ],
        out_specs=[
            pl.BlockSpec((halves, slabs, block, LANES), lambda s: (0, 0, s, 0)),
            pl.BlockSpec((width + 1, block, residues), lambda s: (0, s, 0)),
        ],
        out_shape=[
            jax.ShapeDtypeStruct((halves, slabs, seqs, LANES), bf16),
            jax.ShapeDtypeStruct((width + 1, seqs, residues), bf16),
        ],
        scratch_shapes=[pltpu.VMEM((channels // LANES, block * residues, LANES), f32)],
        compiler_params=VMEM,
        name="opm_inputs",
    )(flip, x, mask, gain, wide, wr.T)


def pair_tile(order, lefts, rights, duo, chain_rows, chain_cols, kernel, gain, logit, block=16):
    rows, residues, channels = duo.shape
    heads = logit.shape[1]
    width = rights[0].shape[0] - 1
    seqs = rights[0].shape[1]
    groups = lefts[0].shape[0] - 1
    parts = len(rights)

    def body(order_ref, *refs):
        left_refs, right_refs = refs[:parts], refs[parts : 2 * parts]
        duo_ref, ci_ref, cj_ref, w_ref, gain_ref, logit_ref, out_ref, bias_ref, rhs, lhs, scale = refs[2 * parts :]
        step = pl.program_id(0)

        @pl.when(step == 0)
        def _():
            counts = jnp.zeros((LANES, residues), f32)
            for n, ref in enumerate(right_refs):
                for b in range(width):
                    rhs[n * seqs : (n + 1) * seqs, b * LANES : b * LANES + residues] = ref[b]
                rhs[n * seqs : (n + 1) * seqs, width * LANES : width * LANES + residues] = ref[width]
            for n, ref in enumerate(left_refs):
                place = pl.ds(pl.multiple_of(order_ref[n] * seqs, seqs), seqs)
                for g in range(groups + 1):
                    lhs[place, g * LANES : (g + 1) * LANES] = ref[g]
            counts = lax.dot_general(
                lhs[:, groups * LANES :], rhs[:, width * LANES :], CONTRACT_FIRST, preferred_element_type=f32
            )[:rows, :residues]
            scale[:, :residues] = ci_ref[...] * cj_ref[...] / (counts + 0.001)

        span = block * width
        picked = lhs[:, pl.ds(pl.multiple_of(step * span, LANES), span)]
        outer = lax.dot_general(
            picked, rhs[:, : width * LANES], CONTRACT_FIRST, preferred_element_type=f32
        ).astype(bf16)
        row_scale = scale[pl.ds(pl.multiple_of(step * block, 8), block), :]
        biases = []
        for first in range(0, block, 2):
            both = [
                jnp.concatenate(
                    [outer[i * width : (i + 1) * width, b * LANES : (b + 1) * LANES] for b in range(width)], 0
                )
                for i in (first, first + 1)
            ]
            update = jnp.dot(w_ref[...], jnp.concatenate(both, 1), preferred_element_type=f32)
            for k, i in enumerate((first, first + 1)):
                mine = (update[:, k * LANES : (k + 1) * LANES] * row_scale[i : i + 1, :]).T[:residues]
                fresh = duo_ref[i] + mine
                out_ref[i] = fresh
                pair_input = (standardize(fresh) * gain_ref[...]).astype(bf16)
                biases.append(
                    lax.dot_general(logit_ref[...], pair_input, ROWS_BY_ROWS, preferred_element_type=f32)
                )
        bias_ref[...] = jnp.swapaxes(jnp.stack(biases, 0), 0, 1).astype(bf16)

    mixing = kernel.reshape(width, width, channels).transpose(2, 1, 0).reshape(channels, width * width)
    operands = [
        *lefts,
        *rights,
        duo,
        chain_rows.reshape(rows, 1),
        chain_cols.reshape(1, residues),
        mixing,
        gain.reshape(1, channels),
        logit.T,
    ]
    specs = [whole(array) for array in operands]
    specs[2 * parts] = pl.BlockSpec((block, residues, channels), lambda s: (s, 0, 0))
    return pl.pallas_call(
        body,
        grid=(rows // block,),
        in_specs=[SMEM, *specs],
        out_specs=[
            pl.BlockSpec((block, residues, channels), lambda s: (s, 0, 0)),
            pl.BlockSpec((heads, block, residues), lambda s: (0, s, 0)),
        ],
        out_shape=[
            jax.ShapeDtypeStruct((rows, residues, channels), f32),
            jax.ShapeDtypeStruct((heads, rows, residues), bf16),
        ],
        scratch_shapes=[
            pltpu.VMEM((parts * seqs, (width + 1) * LANES), bf16),
            pltpu.VMEM((parts * seqs, (groups + 1) * LANES), bf16),
            pltpu.VMEM((rows, LANES), f32),
        ],
        compiler_params=VMEM,
        name="pair_tile",
    )(order, *operands)


def project_kernel(*refs):
    parts = len(refs) - 5
    x_refs = refs[:parts]
    gain_ref, wk_ref, wt_ref, keys_ref, rest_ref = refs[parts:]
    x = jnp.concatenate([ref[0] for ref in x_refs], 0).astype(f32)
    narrow = (standardize(x) * gain_ref[...]).astype(bf16)
    keys_ref[0] = jnp.dot(narrow, wk_ref[...], preferred_element_type=f32).astype(bf16)
    rest_ref[0] = lax.dot_general(wt_ref[...], narrow, ROWS_BY_ROWS, preferred_element_type=f32).astype(bf16)


def project(pieces, gain, kernel):
    seqs, residues, channels = pieces[0].shape
    inner = kernel.shape[1] // 4
    total = residues * len(pieces)
    by_column = jnp.concatenate([kernel[:, :inner], kernel[:, 2 * inner :]], 1).T
    by_row = kernel[:, inner : 2 * inner]
    gain = gain.reshape(1, channels)
    return pl.pallas_call(
        project_kernel,
        grid=(seqs,),
        in_specs=[pl.BlockSpec((1, residues, channels), lambda s: (s, 0, 0))] * len(pieces)
        + [whole(gain), whole(by_row), whole(by_column)],
        out_specs=[
            pl.BlockSpec((1, total, inner), lambda s: (s, 0, 0)),
            pl.BlockSpec((1, 3 * inner, total), lambda s: (s, 0, 0)),
        ],
        out_shape=[
            jax.ShapeDtypeStruct((seqs, total, inner), bf16),
            jax.ShapeDtypeStruct((seqs, 3 * inner, total), bf16),
        ],
        compiler_params=VMEM,
        name="project",
    )(*pieces, gain, by_row, by_column)


def attend(slots, pieces, keys, rest, mask, biases, closing, first, count):
    seqs, residues, channels = pieces[0].shape
    parts = len(pieces)
    blocks = len(biases)
    heads, rows, total = biases[0].shape
    inner = keys.shape[2]
    depth = inner // heads
    head_group = LANES // depth
    scale = depth**-0.5 * LOG2E

    def body(slots_ref, *refs):
        x_refs, refs = refs[:parts], refs[parts:]
        keys_ref, rest_ref, mask_ref, refs = refs[0], refs[1], refs[2], refs[3:]
        bias_refs, refs = refs[:blocks], refs[blocks:]
        closing_ref, out_refs, (raw, bias_t, gated, sems) = refs[0], refs[1 : 1 + parts], refs[1 + parts :]

        @pl.when(pl.program_id(0) == 0)
        def _():
            copies = [
                pltpu.make_async_copy(ref, raw.at[slots_ref[n]], sems.at[n]) for n, ref in enumerate(bias_refs)
            ]
            for copy in copies:
                copy.start()
            for copy in copies:
                copy.wait()
            for h in range(heads):
                bias_t[h] = (raw[:, h].astype(f32) * LOG2E).reshape(total, total).T

        row_mask = (mask_ref[0].astype(f32) - 1.0) * (1e9 * LOG2E)
        tall_mask = jnp.broadcast_to(row_mask, (LANES, total)).T
        tall_mask = jnp.concatenate([tall_mask] * (total // LANES), 1)
        for h in range(heads):
            group, place = h // head_group, h % head_group
            key = keys_ref[0][:, group * LANES : (group + 1) * LANES]
            query = rest_ref[0, h * depth : (h + 1) * depth, :]
            zero = jnp.zeros_like(query)
            alone = jnp.concatenate([query if n == place else zero for n in range(head_group)], 0)
            value = rest_ref[0, inner + h * depth : inner + (h + 1) * depth, :]
            value = jnp.concatenate([value, jnp.ones((16, total), bf16)], 0)
            scores = jnp.dot(key, alone, preferred_element_type=f32) * scale + bias_t[h] + tall_mask
            highest = jnp.max(scores, axis=0, keepdims=True)
            weights = jnp.exp2(scores - highest).astype(bf16)
            mixed = jnp.dot(value, weights, preferred_element_type=f32)
            gate = rest_ref[0, 2 * inner + h * depth : 2 * inner + (h + 1) * depth, :].astype(f32)
            gated[h * depth : (h + 1) * depth, :] = (
                mixed[:depth] / mixed[depth : depth + 1] * jax.nn.sigmoid(gate)
            ).astype(bf16)
        change = lax.dot_general(gated[...], closing_ref[...], CONTRACT_FIRST, preferred_element_type=f32)
        for n in range(parts):
            out_refs[n][0] = (
                x_refs[n][0].astype(f32) + change[n * residues : (n + 1) * residues]
            ).astype(bf16)

    return pl.pallas_call(
        body,
        grid=(count,),
        in_specs=[SMEM]
        + [pl.BlockSpec((1, residues, channels), lambda s: (s + first, 0, 0))] * parts
        + [
            pl.BlockSpec((1, total, inner), lambda s: (s + first, 0, 0)),
            pl.BlockSpec((1, 3 * inner, total), lambda s: (s + first, 0, 0)),
            pl.BlockSpec((1, 1, total), lambda s: (s + first, 0, 0)),
        ]
        + [pl.BlockSpec(memory_space=pl.ANY)] * blocks
        + [whole(closing)],
        out_specs=[pl.BlockSpec((1, residues, channels), lambda s: (s, 0, 0))] * parts,
        out_shape=[jax.ShapeDtypeStruct((count, residues, channels), bf16)] * parts,
        scratch_shapes=[
            pltpu.VMEM((blocks, heads, rows, total), bf16),
            pltpu.VMEM((heads, total, total), f32),
            pltpu.VMEM((inner, total), bf16),
            pltpu.SemaphoreType.DMA((blocks,)),
        ],
        compiler_params=VMEM,
        name="attend",
    )(slots, *pieces, keys, rest, mask, *biases, closing)


def make_shards(mesh):
    n_row, n_col = mesh.shape["row"], mesh.shape["col"]
    halves = n_row // n_col

    def by_row(x, k):
        return lax.ppermute(x, "row", [(r, r ^ k) for r in range(n_row)])

    def by_col(x, k):
        return lax.ppermute(x, "col", [(c, c ^ k) for c in range(n_col)])

    def by_both(x, target):
        pairs = []
        for r in range(n_row):
            for c in range(n_col):
                to_row, to_col = target(r, c)
                pairs.append((r * n_col + c, to_row * n_col + to_col))
        return lax.ppermute(x, ("row", "col"), pairs)

    def gather_rows(x):
        pieces = {0: x}
        for k in range(halves, n_row, halves):
            pieces[k] = by_row(x, k)
        for k in range(0, n_row, halves):
            pieces[k + 1] = by_row(pieces[k], 1)
        return [pieces[k] for k in range(n_row)]

    def shards(
        msa,
        available,
        chain_site_available,
        duo_embedding,
        averaging_gain,
        lineup_gain,
        duo_gain,
        left_kernel,
        right_kernel,
        kronecker_kernel,
        logit_kernel,
        projection_kernel,
        closing_kernel,
    ):
        seqs, residues, channels = msa.shape
        rows = duo_embedding.shape[0]
        r, c = lax.axis_index("row"), lax.axis_index("col")
        share = seqs // n_col

        flip = (r % halves).astype(jnp.int32).reshape(1)
        left, right = opm_inputs(
            flip, msa, available, averaging_gain, left_kernel, right_kernel, rows
        )
        spread = [by_both(left, lambda a, b, u=u: (a, b ^ u ^ (a // halves))) for u in range(n_col)]
        rights = gather_rows(right)
        lefts = [
            by_both(spread[u][v], lambda a, b, u=u, v=v: (a ^ (halves * (b ^ u) + v), b))
            for u in range(n_col)
            for v in range(halves)
        ]
        order = jnp.stack([halves * (c ^ u) + v for u in range(n_col) for v in range(halves)]).astype(jnp.int32)

        mask = available.astype(bf16)
        held = lax.optimization_barrier((msa, *spread))[0]
        x_pieces, mask_pieces = [], []
        for k in range(n_col):
            place = (c ^ k) * share
            x_pieces.append(lax.dynamic_slice_in_dim(held, place, share, 0))
            mask_pieces.append(lax.dynamic_slice_in_dim(mask, place, share, 0))
            if k:
                x_pieces[k] = by_col(x_pieces[k], k)
                mask_pieces[k] = by_col(mask_pieces[k], k)
        rows_mask = jnp.concatenate(mask_pieces, 1)[:, None, :]

        chain = chain_site_available.astype(f32)
        duo_after_averaging, tile = pair_tile(
            order,
            lefts,
            rights,
            duo_embedding,
            lax.dynamic_slice_in_dim(chain, r * rows, rows),
            lax.dynamic_slice_in_dim(chain, c * residues, residues),
            kronecker_kernel,
            duo_gain,
            logit_kernel,
        )
        strip = jnp.concatenate([tile] + [by_col(tile, k) for k in range(1, n_col)], 2)
        biases = gather_rows(strip)
        slots = jnp.stack(
            [halves * (((r ^ w) // halves) ^ c) + (r ^ w) % halves for w in range(n_row)]
        ).astype(jnp.int32)

        keys, rest = project(x_pieces, lineup_gain, projection_kernel)
        chunk = max(share // CHUNKS, 1)
        refreshed = jnp.zeros_like(msa)
        for first in range(0, share, chunk):
            outs = attend(
                slots, x_pieces, keys, rest, rows_mask, biases, closing_kernel, first, chunk
            )
            for k, piece in enumerate(outs):
                if k:
                    piece = by_col(piece, k)
                refreshed = lax.dynamic_update_slice_in_dim(refreshed, piece, (c ^ k) * share + first, 0)
        return refreshed, duo_after_averaging

    return shards


CHUNKS = 4


def solution(mesh):
    split = P("row", "col", None)
    placed = (split, P("row", "col"), P(), split, P(), P(), P(), P(), P(), P(), P(), P(), P())
    return jax.shard_map(
        make_shards(mesh), mesh=mesh, in_specs=placed, out_specs=(split, split), check_vma=False
    )
```

time: 400 us -> 224 us (0.56)
  matrix products: 91.4 us -> 0 us
  blocking collectives: 86.8 us -> 0 us
  Pallas kernels: 0 us -> 80.4 us
  starting transfers between devices: 8.06 us -> 77.2 us
  local copies, waits for them, and re-layouts: 78.4 us -> 15.9 us
  waiting for transfers between devices: 105 us -> 44.3 us
  between operations: 14.1 us -> 1.67 us
  other arithmetic: 13.5 us -> 2.84 us
    pallas_call x0 -> x7, Pallas kernels: none -> 80.4 us  [the longest x4 46.2 us: attend(): pl.pallas_call(body, grid=(count,), in_specs=[SMEM] + [pl.BlockSpec((1, r...]
    ppermute x0 -> x47, starting transfers between devices: none -> 77.2 us  [the longest x12 33.9 us: by_both(): return lax.ppermute(x, ('row', 'col'), pairs)]
    dot_general x12 -> x0, matrix products: 51.7 us -> none  [the longest x4 18.5 us: one_block(): jnp.einsum('bhqk,bkhd->bqhd', weights, value_heads, preferred_element_typ...]
    reshape x5 -> x4, local copies, waits for them, and re-layouts: 47.1 us -> 2.3 us  [the longest x1 0.85 us: pair_tile(): kernel.reshape(width, width, channels).transpose(2, 1, 0)]
    ppermute x0 -> x47, waiting for transfers between devices: none -> 44.3 us  [the longest x21 33.5 us: by_col(): return lax.ppermute(x, 'col', [(c, c ^ k) for c in range(n_col)])]
    psum x1 -> x0, waiting for transfers between devices: 43.3 us -> none  [spread(): return lax.psum(jnp.where(mine, x, jnp.zeros_like(x)), axis)]
    all_to_all x1 -> x0, blocking collectives: 40 us -> none  [shards(): lax.all_to_all(gated_whole, 'col', split_axis=1, concat_axis=0, tiled=True)]
    sub x4 -> x0, matrix products: 39.7 us -> none  [one_block(): exponent = jnp.exp(scores - highest)]
  transfers between devices with their start and end apart: 6 -> 47, of which waited for: 4 -> 11; matrix products, arithmetic and copies ran while one was open for 4% -> 6% of each run, Pallas kernels for 0% -> 29%
where the time goes in v1:
time: 224 us; the launch traced here: 222 us
  Pallas kernels  80.4 us (36%)
  starting transfers between devices  77.2 us (34%)
  waiting for transfers between devices  44.3 us (20%)
  local copies, waits for them, and re-layouts  15.9 us (7%)
  other arithmetic  2.84 us (1%)
    pallas_call x4, Pallas kernels, attend(): pl.pallas_call(body, grid=(count,), in_specs=[SMEM] + [pl.BlockSpec((1, r...  46.2 us
    ppermute x12, starting transfers between devices, by_both(): return lax.ppermute(x, ('row', 'col'), pairs)  33.9 us
    ppermute x21, waiting for transfers between devices, by_col(): return lax.ppermute(x, 'col', [(c, c ^ k) for c in range(n_col)])  33.5 us
    ppermute x21, starting transfers between devices, by_col(): return lax.ppermute(x, 'col', [(c, c ^ k) for c in range(n_col)])  33.2 us
    pallas_call x1, Pallas kernels, pair_tile(): pl.pallas_call(body, grid=(rows // block,), in_specs=[SMEM, *specs], out_...  21.7 us
    ppermute x12, waiting for transfers between devices, by_both(): return lax.ppermute(x, ('row', 'col'), pairs)  10.8 us
    ppermute x14, starting transfers between devices, by_row(): return lax.ppermute(x, 'row', [(r, r ^ k) for r in range(n_row)])  10.1 us
    unnamed x95, local copies, waits for them, and re-layouts  8.7 us
  transfers between devices with their start and end apart: 47, of which 11 were waited for; matrix products, arithmetic and copies ran while one was open for 6% of the time, Pallas kernels for 29%

profile of v1, /device:TPU:0, one launch (start us, length us, event | category | flops | bytes accessed | tf_op | source)
XLA Modules:
  0.0 222.3 jit_solution(4210890751137579368)
XLA Ops:
  0.7 0.9 copy.35
  1.7 0.7 pad_maximum_fusion.1.wl_ref
  2.4 4.2 %opm_inputs.1 = (bf16[2,13,32,128]{3,2,1,0:T(8,128)(2,1)}, bf16[33,32,96]{2,1,0:T(8,128)(2,1)}) custom-call(s32[1]{0:T(128)} %bitcast.8.half_ref, bf16[32,96,256]{2,1,0:T(8,128)(2,1)} %x_ref.1, s32[32,96]{1,0:T(8,128)} %mask_ref.1, f32[1,256]{1,0:T(1,128)} %bitcast.62, bf16[4,256,128]{2,1,0:T(8,128)(2,1)} %pad_maximum_fusion.1.wl_ref, bf16[32,256]{1,0:T(8,128)(2,1)} %bitcast.60), custom_call_target="tpu_custom_call" | custom-call | tf_op jit(solution)/shard_map/opm_inputs/pallas_call | solution.py:84
  6.6 3.0 %collective-permute-start.19 = (bf16[33,32,96]{2,1,0:T(8,128)(2,1)}, bf16[33,32,96]{2,1,0:T(8,128)(2,1)S(1)}, u32[]{:S(2)}, u32[]{:S(2)}) collective-permute-start(bf16[33,32,96]{2,1,0:T(8,128)(2,1)} %get-tuple-element.29.refs_8_), channel_id=1, source_target_pairs={{0,8},{4,12},{8,0},{12,4},{16,24},{20,28},{24,16},{28,20},{1,9},{5... | collective-permute-start | bytes 608264 | tf_op jit(solution)/shard_map/ppermute | solution.py:316
  9.6 1.5 collective-permute-start.21
  11.2 1.6 collective-permute-start
  12.7 3.9 %collective-permute-start.1 = (bf16[2,13,32,128]{3,2,1,0:T(8,128)(2,1)}, bf16[2,13,32,128]{3,2,1,0:T(8,128)(2,1)S(1)}, u32[]{:S(2)}, u32[]{:S(2)}) collective-permute-start(bf16[2,13,32,128]{3,2,1,0:T(8,128)(2,1)} %get-tuple-element.25), channel_id=1, source_target_pairs={{0,1},{1,0},{2,3},{3,2},{4,5},{5,4},{6,7},{7,6},{8,8},{9,9},{10,10... | collective-permute-start | bytes 638984 | tf_op jit(solution)/shard_map/ppermute | solution.py:327
  16.8 0.7 copy.42.refs_17_
  17.7 0.8 copy.43.refs_19_
  18.5 0.6 stack.91.order_ref
  19.1 4.5 %collective-permute-start.2 = (bf16[2,13,32,128]{3,2,1,0:T(8,128)(2,1)}, bf16[2,13,32,128]{3,2,1,0:T(8,128)(2,1)S(1)}, u32[]{:S(2)}, u32[]{:S(2)}) collective-permute-start(bf16[2,13,32,128]{3,2,1,0:T(8,128)(2,1)} %get-tuple-element.25), channel_id=1, source_target_pairs={{0,2},{1,3},{2,0},{3,1},{4,6},{5,7},{6,4},{7,5},{8,11},{9,10},{10,... | collective-permute-start | bytes 638984 | tf_op jit(solution)/shard_map/ppermute | solution.py:327
  23.8 3.2 %collective-permute-start.3 = (bf16[2,13,32,128]{3,2,1,0:T(8,128)(2,1)S(1)}, bf16[2,13,32,128]{3,2,1,0:T(8,128)(2,1)S(1)}, u32[]{:S(2)}, u32[]{:S(2)}) collective-permute-start(bf16[2,13,32,128]{3,2,1,0:T(8,128)(2,1)S(1)} %copy-done.38), channel_id=1, source_target_pairs={{0,3},{1,2},{2,1},{3,0},{4,7},{5,6},{6,5},{7,4},{8,10},{9,11},{10,... | collective-permute-start | bytes 638984 | tf_op jit(solution)/shard_map/ppermute | solution.py:327
  27.0 0.7 collective-permute-start.10
  28.0 4.1 %collective-permute-start.12 = (bf16[13,32,128]{2,1,0:T(8,128)(2,1)S(1)}, bf16[13,32,128]{2,1,0:T(8,128)(2,1)S(1)}, u32[]{:S(2)}, u32[]{:S(2)}) collective-permute-start(bf16[13,32,128]{2,1,0:T(8,128)(2,1)S(1)} %get-tuple-element.59), channel_id=1, source_target_pairs={{0,8},{1,1},{2,26},{3,19},{4,12},{5,5},{6,30},{7,23},{8,0},{9,9},{... | collective-permute-start | bytes 319496 | tf_op jit(solution)/shard_map/ppermute | solution.py:327
  32.2 5.1 %collective-permute-done.2 = bf16[2,13,32,128]{3,2,1,0:T(8,128)(2,1)S(1)} collective-permute-done((bf16[2,13,32,128]{3,2,1,0:T(8,128)(2,1)}, bf16[2,13,32,128]{3,2,1,0:T(8,128)(2,1)S(1)}, u32[]{:S(2)}, u32[]{:S(2)}) %collective-permute-start.2) | collective-permute-done | bytes 213024 | tf_op jit(solution)/shard_map/ppermute | solution.py:327
  38.0 11.3 %collective-permute-start.14 = (bf16[13,32,128]{2,1,0:T(8,128)(2,1)S(1)}, bf16[13,32,128]{2,1,0:T(8,128)(2,1)S(1)}, u32[]{:S(2)}, u32[]{:S(2)}) collective-permute-start(bf16[13,32,128]{2,1,0:T(8,128)(2,1)S(1)} %get-tuple-element.57), channel_id=1, source_target_pairs={{0,16},{1,25},{2,2},{3,11},{4,20},{5,29},{6,6},{7,15},{8,24},{9,17... | collective-permute-start | bytes 319496 | tf_op jit(solution)/shard_map/ppermute | solution.py:327
  49.5 2.8 %collective-permute-done.14.refs_4_ = bf16[13,32,128]{2,1,0:T(8,128)(2,1)S(1)} collective-permute-done((bf16[13,32,128]{2,1,0:T(8,128)(2,1)S(1)}, bf16[13,32,128]{2,1,0:T(8,128)(2,1)S(1)}, u32[]{:S(2)}, u32[]{:S(2)}) %collective-permute-start.14) | collective-permute-done | bytes 106528 | tf_op jit(solution)/shard_map/ppermute | solution.py:327
  52.2 4.1 %collective-permute-start.16 = (bf16[13,32,128]{2,1,0:T(8,128)(2,1)S(1)}, bf16[13,32,128]{2,1,0:T(8,128)(2,1)S(1)}, u32[]{:S(2)}, u32[]{:S(2)}) collective-permute-start(bf16[13,32,128]{2,1,0:T(8,128)(2,1)S(1)} %get-tuple-element.55), channel_id=1, source_target_pairs={{0,24},{1,17},{2,10},{3,3},{4,28},{5,21},{6,14},{7,7},{8,16},{9,25... | collective-permute-start | bytes 319496 | tf_op jit(solution)/shard_map/ppermute | solution.py:327
  56.4 0.7 dynamic-slice_bitcast_fusion.refs_18_
  57.1 2.6 %collective-permute-done.16.refs_6_ = bf16[13,32,128]{2,1,0:T(8,128)(2,1)S(1)} collective-permute-done((bf16[13,32,128]{2,1,0:T(8,128)(2,1)S(1)}, bf16[13,32,128]{2,1,0:T(8,128)(2,1)S(1)}, u32[]{:S(2)}, u32[]{:S(2)}) %collective-permute-start.16) | collective-permute-done | bytes 106528 | tf_op jit(solution)/shard_map/ppermute | solution.py:327
  59.7 2.0 collective-permute-start.7
  62.0 0.7 collective-permute-start.8
  62.9 0.6 copy-done.19
  63.6 21.7 %pair_tile.1 = (f32[48,96,128]{2,1,0:T(8,128)}, bf16[8,48,96]{2,1,0:T(8,128)(2,1)}) custom-call(s32[8]{0:T(128)} %stack.91.order_ref, bf16[13,32,128]{2,1,0:T(8,128)(2,1)} %copy-done.23, bf16[13,32,128]{2,1,0:T(8,128)(2,1)} %copy-done.24, bf16[13,32,128]{2,1,0:T(8,128)(2,1)} %copy-done.25, bf16[13,32,128]{2,1,0:T(8,128)(2,1)} %copy-done.26, ...), custom_call_target="tpu_custom_call" | custom-call | tf_op jit(solution)/shard_map/pair_tile/pallas_call | solution.py:176
  85.4 1.0 collective-permute-start.25
  86.3 2.9 %collective-permute-start.26 = (bf16[8,48,96]{2,1,0:T(8,128)(2,1)}, bf16[8,48,96]{2,1,0:T(8,128)(2,1)S(1)}, u32[]{:S(2)}, u32[]{:S(2)}) collective-permute-start(bf16[8,48,96]{2,1,0:T(8,128)(2,1)} %get-tuple-element.30), channel_id=1, source_target_pairs={{0,2},{1,3},{2,0},{3,1},{4,6},{5,7},{6,4},{7,5},{8,10},{9,11},{10,... | collective-permute-start | bytes 221192 | tf_op jit(solution)/shard_map/ppermute | solution.py:319
  89.2 0.6 collective-permute-start.27
  89.8 1.0 constant_dynamic-slice_fusion.4
  90.8 0.6 collective-permute-done.25
  91.5 2.6 %collective-permute-start.9 = (bf16[8,96]{1,0:T(8,128)(2,1)S(1)}, bf16[8,96]{1,0:T(8,128)(2,1)S(1)}, u32[]{:S(2)}, u32[]{:S(2)}) collective-permute-start(bf16[8,96]{1,0:T(8,128)(2,1)S(1)} %get-tuple-element.67), channel_id=1, source_target_pairs={{0,3},{1,2},{2,1},{3,0},{4,7},{5,6},{6,5},{7,4},{8,11},{9,10},{10,... | collective-permute-start | bytes 4616 | tf_op jit(solution)/shard_map/ppermute | solution.py:319
  94.0 2.6 %collective-permute-done.26 = bf16[8,48,96]{2,1,0:T(8,128)(2,1)S(1)} collective-permute-done((bf16[8,48,96]{2,1,0:T(8,128)(2,1)}, bf16[8,48,96]{2,1,0:T(8,128)(2,1)S(1)}, u32[]{:S(2)}, u32[]{:S(2)}) %collective-permute-start.26) | collective-permute-done | bytes 73760 | tf_op jit(solution)/shard_map/ppermute | solution.py:319
  96.7 3.0 %collective-permute-start.5 = (bf16[8,96,256]{2,1,0:T(8,128)(2,1)S(1)}, bf16[8,96,256]{2,1,0:T(8,128)(2,1)S(1)}, u32[]{:S(2)}, u32[]{:S(2)}) collective-permute-start(bf16[8,96,256]{2,1,0:T(8,128)(2,1)S(1)} %get-tuple-element.49), channel_id=1, source_target_pairs={{0,2},{1,3},{2,0},{3,1},{4,6},{5,7},{6,4},{7,5},{8,10},{9,11},{10,... | collective-permute-start | bytes 1179656 | tf_op jit(solution)/shard_map/ppermute | solution.py:319
  100.5 2.2 collective-permute-start.31
  102.6 1.1 collective-permute-start.33
  103.7 6.8 %collective-permute-done.4.refs_1_ = bf16[8,96,256]{2,1,0:T(8,128)(2,1)S(1)} collective-permute-done((bf16[8,96,256]{2,1,0:T(8,128)(2,1)S(1)}, bf16[8,96,256]{2,1,0:T(8,128)(2,1)S(1)}, u32[]{:S(2)}, u32[]{:S(2)}) %collective-permute-start.4) | collective-permute-done | bytes 393248 | tf_op jit(solution)/shard_map/ppermute | solution.py:319
  110.5 2.2 %collective-permute-start.6 = (bf16[8,96,256]{2,1,0:T(8,128)(2,1)}, bf16[8,96,256]{2,1,0:T(8,128)(2,1)S(1)}, u32[]{:S(2)}, u32[]{:S(2)}) collective-permute-start(bf16[8,96,256]{2,1,0:T(8,128)(2,1)} %get-tuple-element.48), channel_id=1, source_target_pairs={{0,3},{1,2},{2,1},{3,0},{4,7},{5,6},{6,5},{7,4},{8,11},{9,10},{10,... | collective-permute-start | bytes 1179656 | tf_op jit(solution)/shard_map/ppermute | solution.py:319
  112.8 12.9 %collective-permute-done.5.refs_2_ = bf16[8,96,256]{2,1,0:T(8,128)(2,1)S(1)} collective-permute-done((bf16[8,96,256]{2,1,0:T(8,128)(2,1)S(1)}, bf16[8,96,256]{2,1,0:T(8,128)(2,1)S(1)}, u32[]{:S(2)}, u32[]{:S(2)}) %collective-permute-start.5) | collective-permute-done | bytes 393248 | tf_op jit(solution)/shard_map/ppermute | solution.py:319
  126.7 0.7 fusion
  127.4 0.7 slice.35
  128.1 1.7 copy.48
  129.8 1.8 copy.49
  131.6 0.6 stack.77.slots_ref
  132.2 1.8 maximum_bitcast_fusion.refs_6_
  134.1 0.6 copy.44.refs_6_
  134.7 0.7 copy-done.2
  135.5 8.3 %project.1 = (bf16[8,384,256]{2,1,0:T(8,128)(2,1)}, bf16[8,768,384]{2,1,0:T(8,128)(2,1)}) custom-call(bf16[8,96,256]{2,1,0:T(8,128)(2,1)} %get-tuple-element.51.refs_0_, bf16[8,96,256]{2,1,0:T(8,128)(2,1)} %copy-done, bf16[8,96,256]{2,1,0:T(8,128)(2,1)} %copy-done.1, bf16[8,96,256]{2,1,0:T(8,128)(2,1)} %copy-done.2, f32[1,256]{1,0:T(1,128)} %bitcast.63, ...), custom_call_target="tpu_custom_call" | custom-call | tf_op jit(solution)/shard_map/project/pallas_call | solution.py:215
  143.9 0.7 copy-done.8
  144.8 11.5 %attend.4 = (bf16[2,96,256]{2,1,0:T(8,128)(2,1)}, bf16[2,96,256]{2,1,0:T(8,128)(2,1)}, bf16[2,96,256]{2,1,0:T(8,128)(2,1)}, bf16[2,96,256]{2,1,0:T(8,128)(2,1)}) custom-call(s32[8]{0:T(128)} %stack.77.slots_ref, bf16[8,96,256]{2,1,0:T(8,128)(2,1)} %get-tuple-element.51.refs_0_, bf16[8,96,256]{2,1,0:T(8,128)(2,1)} %copy-done, bf16[8,96,256]{2,1,0:T(8,128)(2,1)} %copy-done.1, ...), custom_call_target="tpu_custom_call" | custom-call | tf_op jit(solution)/shard_map/attend/pallas_call | solution.py:286
  156.4 2.6 %collective-permute-start.36 = (bf16[2,96,256]{2,1,0:T(8,128)(2,1)}, bf16[2,96,256]{2,1,0:T(8,128)(2,1)S(1)}, u32[]{:S(2)}, u32[]{:S(2)}) collective-permute-start(bf16[2,96,256]{2,1,0:T(8,128)(2,1)} %get-tuple-element.33), channel_id=1, source_target_pairs={{0,2},{1,3},{2,0},{3,1},{4,6},{5,7},{6,4},{7,5},{8,10},{9,11},{10,... | collective-permute-start | bytes 294920 | tf_op jit(solution)/shard_map/ppermute | solution.py:319
  159.0 1.8 collective-permute-start.37
  160.8 11.7 %attend.5 = (bf16[2,96,256]{2,1,0:T(8,128)(2,1)}, bf16[2,96,256]{2,1,0:T(8,128)(2,1)}, bf16[2,96,256]{2,1,0:T(8,128)(2,1)}, bf16[2,96,256]{2,1,0:T(8,128)(2,1)}) custom-call(s32[8]{0:T(128)} %stack.77.slots_ref, bf16[8,96,256]{2,1,0:T(8,128)(2,1)} %get-tuple-element.51.refs_0_, bf16[8,96,256]{2,1,0:T(8,128)(2,1)} %copy-done, bf16[8,96,256]{2,1,0:T(8,128)(2,1)} %copy-done.1, ...), custom_call_target="tpu_custom_call" | custom-call | tf_op jit(solution)/shard_map/attend/pallas_call | solution.py:286
  172.6 2.6 %collective-permute-start.39 = (bf16[2,96,256]{2,1,0:T(8,128)(2,1)}, bf16[2,96,256]{2,1,0:T(8,128)(2,1)S(1)}, u32[]{:S(2)}, u32[]{:S(2)}) collective-permute-start(bf16[2,96,256]{2,1,0:T(8,128)(2,1)} %get-tuple-element.37), channel_id=1, source_target_pairs={{0,2},{1,3},{2,0},{3,1},{4,6},{5,7},{6,4},{7,5},{8,10},{9,11},{10,... | collective-permute-start | bytes 294920 | tf_op jit(solution)/shard_map/ppermute | solution.py:319
  175.2 11.5 %attend.7 = (bf16[2,96,256]{2,1,0:T(8,128)(2,1)}, bf16[2,96,256]{2,1,0:T(8,128)(2,1)}, bf16[2,96,256]{2,1,0:T(8,128)(2,1)}, bf16[2,96,256]{2,1,0:T(8,128)(2,1)}) custom-call(s32[8]{0:T(128)} %stack.77.slots_ref, bf16[8,96,256]{2,1,0:T(8,128)(2,1)} %get-tuple-element.51.refs_0_, bf16[8,96,256]{2,1,0:T(8,128)(2,1)} %copy-done, bf16[8,96,256]{2,1,0:T(8,128)(2,1)} %copy-done.1, ...), custom_call_target="tpu_custom_call" | custom-call | tf_op jit(solution)/shard_map/attend/pallas_call | solution.py:286
  186.7 11.5 %attend.6 = (bf16[2,96,256]{2,1,0:T(8,128)(2,1)}, bf16[2,96,256]{2,1,0:T(8,128)(2,1)}, bf16[2,96,256]{2,1,0:T(8,128)(2,1)}, bf16[2,96,256]{2,1,0:T(8,128)(2,1)}) custom-call(s32[8]{0:T(128)} %stack.77.slots_ref, bf16[8,96,256]{2,1,0:T(8,128)(2,1)} %get-tuple-element.51.refs_0_, bf16[8,96,256]{2,1,0:T(8,128)(2,1)} %copy-done, bf16[8,96,256]{2,1,0:T(8,128)(2,1)} %copy-done.1, ...), custom_call_target="tpu_custom_call" | custom-call | tf_op jit(solution)/shard_map/attend/pallas_call | solution.py:286
  198.5 0.6 copy-done.34
  199.2 1.8 collective-permute-start.40
  201.1 2.7 %collective-permute-start.42 = (bf16[2,96,256]{2,1,0:T(8,128)(2,1)S(1)}, bf16[2,96,256]{2,1,0:T(8,128)(2,1)S(1)}, u32[]{:S(2)}, u32[]{:S(2)}) collective-permute-start(bf16[2,96,256]{2,1,0:T(8,128)(2,1)S(1)} %copy-done.43), channel_id=1, source_target_pairs={{0,2},{1,3},{2,0},{3,1},{4,6},{5,7},{6,4},{7,5},{8,10},{9,11},{10,... | collective-permute-start | bytes 294920 | tf_op jit(solution)/shard_map/ppermute | solution.py:319
  203.9 1.8 collective-permute-start.43
  205.8 1.1 collective-permute-done.40
  206.9 2.1 collective-permute-start.45
  209.1 2.6 %collective-permute-start.46 = (bf16[2,96,256]{2,1,0:T(8,128)(2,1)S(1)}, bf16[2,96,256]{2,1,0:T(8,128)(2,1)S(1)}, u32[]{:S(2)}, u32[]{:S(2)}) collective-permute-start(bf16[2,96,256]{2,1,0:T(8,128)(2,1)S(1)} %copy-done.39), channel_id=1, source_target_pairs={{0,3},{1,2},{2,1},{3,0},{4,7},{5,6},{6,5},{7,4},{8,11},{9,10},{10,... | collective-permute-start | bytes 294920 | tf_op jit(solution)/shard_map/ppermute | solution.py:319
  211.6 3.0 %collective-permute-done.42 = bf16[2,96,256]{2,1,0:T(8,128)(2,1)S(1)} collective-permute-done((bf16[2,96,256]{2,1,0:T(8,128)(2,1)S(1)}, bf16[2,96,256]{2,1,0:T(8,128)(2,1)S(1)}, u32[]{:S(2)}, u32[]{:S(2)}) %collective-permute-start.42) | collective-permute-done | bytes 98336 | tf_op jit(solution)/shard_map/ppermute | solution.py:319
  214.8 6.3 %collective-permute-done.45 = bf16[2,96,256]{2,1,0:T(8,128)(2,1)S(1)} collective-permute-done((bf16[2,96,256]{2,1,0:T(8,128)(2,1)S(1)}, bf16[2,96,256]{2,1,0:T(8,128)(2,1)S(1)}, u32[]{:S(2)}, u32[]{:S(2)}) %collective-permute-start.45) | collective-permute-done | bytes 98336 | tf_op jit(solution)/shard_map/ppermute | solution.py:319
  221.2 1.1 copy-done.12
  (172 shorter events, 5.1 us)
Async XLA Ops:
  0.7 16.9 %copy-start.22 = (bf16[1024,128]{1,0:T(8,128)(2,1)S(1)}, bf16[1024,128]{1,0:T(8,128)(2,1)}, u32[]{:S(2)}) copy-start(bf16[1024,128]{1,0:T(8,128)(2,1)} %param.22) | copy-start | bytes 786436
  6.6 17.0 %copy-start.14 = (bf16[33,32,96]{2,1,0:T(8,128)(2,1)S(1)}, bf16[33,32,96]{2,1,0:T(8,128)(2,1)}, u32[]{:S(2)}) copy-start(bf16[33,32,96]{2,1,0:T(8,128)(2,1)} %get-tuple-element.29.refs_8_) | copy-start | bytes 608260
  6.6 17.1 %copy-start.38 = (bf16[2,13,32,128]{3,2,1,0:T(8,128)(2,1)S(1)}, bf16[2,13,32,128]{3,2,1,0:T(8,128)(2,1)}, u32[]{:S(2)}) copy-start(bf16[2,13,32,128]{3,2,1,0:T(8,128)(2,1)} %get-tuple-element.25) | copy-start | bytes 638980
  6.6 17.1 %collective-permute-start.19 = (bf16[33,32,96]{2,1,0:T(8,128)(2,1)}, bf16[33,32,96]{2,1,0:T(8,128)(2,1)S(1)}, u32[]{:S(2)}, u32[]{:S(2)}) collective-permute-start(bf16[33,32,96]{2,1,0:T(8,128)(2,1)} %get-tuple-element.29.refs_8_), channel_id=1, source_target_pairs={{0,8},{4,12},{8,0},{12,4},{16,24},{20,28},{24,16},{28,20},{1,9},{5... | collective-permute-start | bytes 608264 | tf_op jit(solution)/shard_map/ppermute | solution.py:316
  9.6 17.4 %collective-permute-start.21 = (bf16[33,32,96]{2,1,0:T(8,128)(2,1)}, bf16[33,32,96]{2,1,0:T(8,128)(2,1)S(1)}, u32[]{:S(2)}, u32[]{:S(2)}) collective-permute-start(bf16[33,32,96]{2,1,0:T(8,128)(2,1)} %get-tuple-element.29.refs_8_), channel_id=1, source_target_pairs={{0,16},{4,20},{8,24},{12,28},{16,0},{20,4},{24,8},{28,12},{1,17},{... | collective-permute-start | bytes 608264 | tf_op jit(solution)/shard_map/ppermute | solution.py:316
  11.1 16.6 %collective-permute-start.23 = (bf16[33,32,96]{2,1,0:T(8,128)(2,1)}, bf16[33,32,96]{2,1,0:T(8,128)(2,1)S(1)}, u32[]{:S(2)}, u32[]{:S(2)}) collective-permute-start(bf16[33,32,96]{2,1,0:T(8,128)(2,1)} %get-tuple-element.29.refs_8_), channel_id=1, source_target_pairs={{0,24},{4,28},{8,16},{12,20},{16,8},{20,12},{24,0},{28,4},{1,25},{... | collective-permute-start | bytes 608264 | tf_op jit(solution)/shard_map/ppermute | solution.py:316
  11.2 7.9 %collective-permute-start = (bf16[2,13,32,128]{3,2,1,0:T(8,128)(2,1)}, bf16[2,13,32,128]{3,2,1,0:T(8,128)(2,1)S(1)}, u32[]{:S(2)}, u32[]{:S(2)}) collective-permute-start(bf16[2,13,32,128]{3,2,1,0:T(8,128)(2,1)} %get-tuple-element.25), channel_id=1, source_target_pairs={{0,0},{1,1},{2,2},{3,3},{4,4},{5,5},{6,6},{7,7},{8,9},{9,8},{10,11... | collective-permute-start | bytes 638984 | tf_op jit(solution)/shard_map/ppermute | solution.py:327
  12.7 10.9 %collective-permute-start.1 = (bf16[2,13,32,128]{3,2,1,0:T(8,128)(2,1)}, bf16[2,13,32,128]{3,2,1,0:T(8,128)(2,1)S(1)}, u32[]{:S(2)}, u32[]{:S(2)}) collective-permute-start(bf16[2,13,32,128]{3,2,1,0:T(8,128)(2,1)} %get-tuple-element.25), channel_id=1, source_target_pairs={{0,1},{1,0},{2,3},{3,2},{4,5},{5,4},{6,7},{7,6},{8,8},{9,9},{10,10... | collective-permute-start | bytes 638984 | tf_op jit(solution)/shard_map/ppermute | solution.py:327
  19.1 18.2 %collective-permute-start.2 = (bf16[2,13,32,128]{3,2,1,0:T(8,128)(2,1)}, bf16[2,13,32,128]{3,2,1,0:T(8,128)(2,1)S(1)}, u32[]{:S(2)}, u32[]{:S(2)}) collective-permute-start(bf16[2,13,32,128]{3,2,1,0:T(8,128)(2,1)} %get-tuple-element.25), channel_id=1, source_target_pairs={{0,2},{1,3},{2,0},{3,1},{4,6},{5,7},{6,4},{7,5},{8,11},{9,10},{10,... | collective-permute-start | bytes 638984 | tf_op jit(solution)/shard_map/ppermute | solution.py:327
  23.6 4.4 %collective-permute-start.18 = (bf16[33,32,96]{2,1,0:T(8,128)(2,1)S(1)}, bf16[33,32,96]{2,1,0:T(8,128)(2,1)S(1)}, u32[]{:S(2)}, u32[]{:S(2)}) collective-permute-start(bf16[33,32,96]{2,1,0:T(8,128)(2,1)S(1)} %copy-done.14), channel_id=1, source_target_pairs={{0,4},{4,0},{8,12},{12,8},{16,20},{20,16},{24,28},{28,24},{1,5},{5... | collective-permute-start | bytes 608264 | tf_op jit(solution)/shard_map/ppermute | solution.py:316
  23.8 39.0 %copy-start.15 = (bf16[33,32,96]{2,1,0:T(8,128)(2,1)}, bf16[33,32,96]{2,1,0:T(8,128)(2,1)S(1)}, u32[]{:S(2)}) copy-start(bf16[33,32,96]{2,1,0:T(8,128)(2,1)S(1)} %collective-permute-done.19.refs_10_) | copy-start | bytes 608260
  23.8 13.5 %collective-permute-start.3 = (bf16[2,13,32,128]{3,2,1,0:T(8,128)(2,1)S(1)}, bf16[2,13,32,128]{3,2,1,0:T(8,128)(2,1)S(1)}, u32[]{:S(2)}, u32[]{:S(2)}) collective-permute-start(bf16[2,13,32,128]{3,2,1,0:T(8,128)(2,1)S(1)} %copy-done.38), channel_id=1, source_target_pairs={{0,3},{1,2},{2,1},{3,0},{4,7},{5,6},{6,5},{7,4},{8,10},{9,11},{10,... | collective-permute-start | bytes 638984 | tf_op jit(solution)/shard_map/ppermute | solution.py:327
  27.0 35.8 %copy-start.16 = (bf16[33,32,96]{2,1,0:T(8,128)(2,1)}, bf16[33,32,96]{2,1,0:T(8,128)(2,1)S(1)}, u32[]{:S(2)}) copy-start(bf16[33,32,96]{2,1,0:T(8,128)(2,1)S(1)} %collective-permute-done.21.refs_12_) | copy-start | bytes 608260
  27.0 10.3 %collective-permute-start.10 = (bf16[13,32,128]{2,1,0:T(8,128)(2,1)S(1)}, bf16[13,32,128]{2,1,0:T(8,128)(2,1)S(1)}, u32[]{:S(2)}, u32[]{:S(2)}) collective-permute-start(bf16[13,32,128]{2,1,0:T(8,128)(2,1)S(1)} %get-tuple-element.61), channel_id=1, source_target_pairs={{0,0},{1,9},{2,18},{3,27},{4,4},{5,13},{6,22},{7,31},{8,8},{9,1},{... | collective-permute-start | bytes 319496 | tf_op jit(solution)/shard_map/ppermute | solution.py:327
  27.7 35.1 %copy-start.17 = (bf16[33,32,96]{2,1,0:T(8,128)(2,1)}, bf16[33,32,96]{2,1,0:T(8,128)(2,1)S(1)}, u32[]{:S(2)}) copy-start(bf16[33,32,96]{2,1,0:T(8,128)(2,1)S(1)} %collective-permute-done.23.refs_14_) | copy-start | bytes 608260
  27.7 10.1 %collective-permute-start.11 = (bf16[13,32,128]{2,1,0:T(8,128)(2,1)S(1)}, bf16[13,32,128]{2,1,0:T(8,128)(2,1)S(1)}, u32[]{:S(2)}, u32[]{:S(2)}) collective-permute-start(bf16[13,32,128]{2,1,0:T(8,128)(2,1)S(1)} %get-tuple-element.60), channel_id=1, source_target_pairs={{0,4},{1,13},{2,22},{3,31},{4,0},{5,9},{6,18},{7,27},{8,12},{9,5},... | collective-permute-start | bytes 319496 | tf_op jit(solution)/shard_map/ppermute | solution.py:327
  28.0 34.8 %copy-start.18 = (bf16[33,32,96]{2,1,0:T(8,128)(2,1)}, bf16[33,32,96]{2,1,0:T(8,128)(2,1)S(1)}, u32[]{:S(2)}) copy-start(bf16[33,32,96]{2,1,0:T(8,128)(2,1)S(1)} %collective-permute-done.18.refs_9_) | copy-start | bytes 608260
  28.0 9.9 %collective-permute-start.12 = (bf16[13,32,128]{2,1,0:T(8,128)(2,1)S(1)}, bf16[13,32,128]{2,1,0:T(8,128)(2,1)S(1)}, u32[]{:S(2)}, u32[]{:S(2)}) collective-permute-start(bf16[13,32,128]{2,1,0:T(8,128)(2,1)S(1)} %get-tuple-element.59), channel_id=1, source_target_pairs={{0,8},{1,1},{2,26},{3,19},{4,12},{5,5},{6,30},{7,23},{8,0},{9,9},{... | collective-permute-start | bytes 319496 | tf_op jit(solution)/shard_map/ppermute | solution.py:327
  37.3 12.1 %collective-permute-start.13 = (bf16[13,32,128]{2,1,0:T(8,128)(2,1)S(1)}, bf16[13,32,128]{2,1,0:T(8,128)(2,1)S(1)}, u32[]{:S(2)}, u32[]{:S(2)}) collective-permute-start(bf16[13,32,128]{2,1,0:T(8,128)(2,1)S(1)} %get-tuple-element.58), channel_id=1, source_target_pairs={{0,12},{1,5},{2,30},{3,23},{4,8},{5,1},{6,26},{7,19},{8,4},{9,13},... | collective-permute-start | bytes 319496 | tf_op jit(solution)/shard_map/ppermute | solution.py:327
  37.3 25.4 %collective-permute-start.20 = (bf16[33,32,96]{2,1,0:T(8,128)(2,1)S(1)}, bf16[33,32,96]{2,1,0:T(8,128)(2,1)S(1)}, u32[]{:S(2)}, u32[]{:S(2)}) collective-permute-start(bf16[33,32,96]{2,1,0:T(8,128)(2,1)S(1)} %collective-permute-done.19.refs_10_), channel_id=1, source_target_pairs={{0,4},{4,0},{8,12},{12,8},{16,20},{20,16},{24,28},{28,24},{1,5},{5... | collective-permute-start | bytes 608264 | tf_op jit(solution)/shard_map/ppermute | solution.py:316
  37.4 25.4 %copy-start.23 = (bf16[13,32,128]{2,1,0:T(8,128)(2,1)}, bf16[13,32,128]{2,1,0:T(8,128)(2,1)S(1)}, u32[]{:S(2)}) copy-start(bf16[13,32,128]{2,1,0:T(8,128)(2,1)S(1)} %collective-permute-done.10.refs_0_) | copy-start | bytes 319492
  37.4 25.4 %collective-permute-start.22 = (bf16[33,32,96]{2,1,0:T(8,128)(2,1)S(1)}, bf16[33,32,96]{2,1,0:T(8,128)(2,1)S(1)}, u32[]{:S(2)}, u32[]{:S(2)}) collective-permute-start(bf16[33,32,96]{2,1,0:T(8,128)(2,1)S(1)} %collective-permute-done.21.refs_12_), channel_id=1, source_target_pairs={{0,4},{4,0},{8,12},{12,8},{16,20},{20,16},{24,28},{28,24},{1,5},{5... | collective-permute-start | bytes 608264 | tf_op jit(solution)/shard_map/ppermute | solution.py:316
  37.9 25.0 %copy-start.24 = (bf16[13,32,128]{2,1,0:T(8,128)(2,1)}, bf16[13,32,128]{2,1,0:T(8,128)(2,1)S(1)}, u32[]{:S(2)}) copy-start(bf16[13,32,128]{2,1,0:T(8,128)(2,1)S(1)} %collective-permute-done.11.refs_1_) | copy-start | bytes 319492
  37.9 24.9 %collective-permute-start.24 = (bf16[33,32,96]{2,1,0:T(8,128)(2,1)S(1)}, bf16[33,32,96]{2,1,0:T(8,128)(2,1)S(1)}, u32[]{:S(2)}, u32[]{:S(2)}) collective-permute-start(bf16[33,32,96]{2,1,0:T(8,128)(2,1)S(1)} %collective-permute-done.23.refs_14_), channel_id=1, source_target_pairs={{0,4},{4,0},{8,12},{12,8},{16,20},{20,16},{24,28},{28,24},{1,5},{5... | collective-permute-start | bytes 608264 | tf_op jit(solution)/shard_map/ppermute | solution.py:316
  38.0 24.9 %copy-start.25 = (bf16[13,32,128]{2,1,0:T(8,128)(2,1)}, bf16[13,32,128]{2,1,0:T(8,128)(2,1)S(1)}, u32[]{:S(2)}) copy-start(bf16[13,32,128]{2,1,0:T(8,128)(2,1)S(1)} %collective-permute-done.12.refs_2_) | copy-start | bytes 319492
  38.0 14.2 %collective-permute-start.14 = (bf16[13,32,128]{2,1,0:T(8,128)(2,1)S(1)}, bf16[13,32,128]{2,1,0:T(8,128)(2,1)S(1)}, u32[]{:S(2)}, u32[]{:S(2)}) collective-permute-start(bf16[13,32,128]{2,1,0:T(8,128)(2,1)S(1)} %get-tuple-element.57), channel_id=1, source_target_pairs={{0,16},{1,25},{2,2},{3,11},{4,20},{5,29},{6,6},{7,15},{8,24},{9,17... | collective-permute-start | bytes 319496 | tf_op jit(solution)/shard_map/ppermute | solution.py:327
  49.3 7.0 %collective-permute-start.15 = (bf16[13,32,128]{2,1,0:T(8,128)(2,1)S(1)}, bf16[13,32,128]{2,1,0:T(8,128)(2,1)S(1)}, u32[]{:S(2)}, u32[]{:S(2)}) collective-permute-start(bf16[13,32,128]{2,1,0:T(8,128)(2,1)S(1)} %get-tuple-element.56), channel_id=1, source_target_pairs={{0,20},{1,29},{2,6},{3,15},{4,16},{5,25},{6,2},{7,11},{8,28},{9,21... | collective-permute-start | bytes 319496 | tf_op jit(solution)/shard_map/ppermute | solution.py:327
  52.2 7.5 %collective-permute-start.16 = (bf16[13,32,128]{2,1,0:T(8,128)(2,1)S(1)}, bf16[13,32,128]{2,1,0:T(8,128)(2,1)S(1)}, u32[]{:S(2)}, u32[]{:S(2)}) collective-permute-start(bf16[13,32,128]{2,1,0:T(8,128)(2,1)S(1)} %get-tuple-element.55), channel_id=1, source_target_pairs={{0,24},{1,17},{2,10},{3,3},{4,28},{5,21},{6,14},{7,7},{8,16},{9,25... | collective-permute-start | bytes 319496 | tf_op jit(solution)/shard_map/ppermute | solution.py:327
  56.3 5.6 %collective-permute-start.17 = (bf16[13,32,128]{2,1,0:T(8,128)(2,1)S(1)}, bf16[13,32,128]{2,1,0:T(8,128)(2,1)S(1)}, u32[]{:S(2)}, u32[]{:S(2)}) collective-permute-start(bf16[13,32,128]{2,1,0:T(8,128)(2,1)S(1)} %get-tuple-element.54), channel_id=1, source_target_pairs={{0,28},{1,21},{2,14},{3,7},{4,24},{5,17},{6,10},{7,3},{8,20},{9,29... | collective-permute-start | bytes 319496 | tf_op jit(solution)/shard_map/ppermute | solution.py:327
  59.7 40.2 %collective-permute-start.7 = (bf16[8,96]{1,0:T(8,128)(2,1)S(1)}, bf16[8,96]{1,0:T(8,128)(2,1)S(1)}, u32[]{:S(2)}, u32[]{:S(2)}) collective-permute-start(bf16[8,96]{1,0:T(8,128)(2,1)S(1)} %get-tuple-element.69), channel_id=1, source_target_pairs={{0,1},{1,0},{2,3},{3,2},{4,5},{5,4},{6,7},{7,6},{8,9},{9,8},{10,11... | collective-permute-start | bytes 4616 | tf_op jit(solution)/shard_map/ppermute | solution.py:319
  62.0 38.5 %collective-permute-start.8 = (bf16[8,96]{1,0:T(8,128)(2,1)S(1)}, bf16[8,96]{1,0:T(8,128)(2,1)S(1)}, u32[]{:S(2)}, u32[]{:S(2)}) collective-permute-start(bf16[8,96]{1,0:T(8,128)(2,1)S(1)} %get-tuple-element.68), channel_id=1, source_target_pairs={{0,2},{1,3},{2,0},{3,1},{4,6},{5,7},{6,4},{7,5},{8,10},{9,11},{10,... | collective-permute-start | bytes 4616 | tf_op jit(solution)/shard_map/ppermute | solution.py:319
  63.6 26.2 %copy-start.4 = (bf16[32,96,256]{2,1,0:T(8,128)(2,1)S(1)}, bf16[32,96,256]{2,1,0:T(8,128)(2,1)}, u32[]{:S(2)}) copy-start(bf16[32,96,256]{2,1,0:T(8,128)(2,1)} %x_ref.1) | copy-start | bytes 4718596
  85.3 41.4 %copy-start.13 = (bf16[256,1024]{1,0:T(8,128)(2,1)S(1)}, bf16[256,1024]{1,0:T(8,128)(2,1)}, u32[]{:S(2)}) copy-start(bf16[256,1024]{1,0:T(8,128)(2,1)} %param.24) | copy-start | bytes 1572868
  85.4 6.1 %collective-permute-start.25 = (bf16[8,48,96]{2,1,0:T(8,128)(2,1)}, bf16[8,48,96]{2,1,0:T(8,128)(2,1)S(1)}, u32[]{:S(2)}, u32[]{:S(2)}) collective-permute-start(bf16[8,48,96]{2,1,0:T(8,128)(2,1)} %get-tuple-element.30), channel_id=1, source_target_pairs={{0,1},{1,0},{2,3},{3,2},{4,5},{5,4},{6,7},{7,6},{8,9},{9,8},{10,11... | collective-permute-start | bytes 221192 | tf_op jit(solution)/shard_map/ppermute | solution.py:319
  86.3 10.4 %collective-permute-start.26 = (bf16[8,48,96]{2,1,0:T(8,128)(2,1)}, bf16[8,48,96]{2,1,0:T(8,128)(2,1)S(1)}, u32[]{:S(2)}, u32[]{:S(2)}) collective-permute-start(bf16[8,48,96]{2,1,0:T(8,128)(2,1)} %get-tuple-element.30), channel_id=1, source_target_pairs={{0,2},{1,3},{2,0},{3,1},{4,6},{5,7},{6,4},{7,5},{8,10},{9,11},{10,... | collective-permute-start | bytes 221192 | tf_op jit(solution)/shard_map/ppermute | solution.py:319
  89.2 7.5 %collective-permute-start.27 = (bf16[8,48,96]{2,1,0:T(8,128)(2,1)}, bf16[8,48,96]{2,1,0:T(8,128)(2,1)S(1)}, u32[]{:S(2)}, u32[]{:S(2)}) collective-permute-start(bf16[8,48,96]{2,1,0:T(8,128)(2,1)} %get-tuple-element.30), channel_id=1, source_target_pairs={{0,3},{1,2},{2,1},{3,0},{4,7},{5,6},{6,5},{7,4},{8,11},{9,10},{10,... | collective-permute-start | bytes 221192 | tf_op jit(solution)/shard_map/ppermute | solution.py:319
  91.5 11.2 %collective-permute-start.9 = (bf16[8,96]{1,0:T(8,128)(2,1)S(1)}, bf16[8,96]{1,0:T(8,128)(2,1)S(1)}, u32[]{:S(2)}, u32[]{:S(2)}) collective-permute-start(bf16[8,96]{1,0:T(8,128)(2,1)S(1)} %get-tuple-element.67), channel_id=1, source_target_pairs={{0,3},{1,2},{2,1},{3,0},{4,7},{5,6},{6,5},{7,4},{8,11},{9,10},{10,... | collective-permute-start | bytes 4616 | tf_op jit(solution)/shard_map/ppermute | solution.py:319
  96.7 13.9 %collective-permute-start.4 = (bf16[8,96,256]{2,1,0:T(8,128)(2,1)S(1)}, bf16[8,96,256]{2,1,0:T(8,128)(2,1)S(1)}, u32[]{:S(2)}, u32[]{:S(2)}) collective-permute-start(bf16[8,96,256]{2,1,0:T(8,128)(2,1)S(1)} %get-tuple-element.50), channel_id=1, source_target_pairs={{0,1},{1,0},{2,3},{3,2},{4,5},{5,4},{6,7},{7,6},{8,9},{9,8},{10,11... | collective-permute-start | bytes 1179656 | tf_op jit(solution)/shard_map/ppermute | solution.py:319
  96.7 29.0 %collective-permute-start.5 = (bf16[8,96,256]{2,1,0:T(8,128)(2,1)S(1)}, bf16[8,96,256]{2,1,0:T(8,128)(2,1)S(1)}, u32[]{:S(2)}, u32[]{:S(2)}) collective-permute-start(bf16[8,96,256]{2,1,0:T(8,128)(2,1)S(1)} %get-tuple-element.49), channel_id=1, source_target_pairs={{0,2},{1,3},{2,0},{3,1},{4,6},{5,7},{6,4},{7,5},{8,10},{9,11},{10,... | collective-permute-start | bytes 1179656 | tf_op jit(solution)/shard_map/ppermute | solution.py:319
  99.9 43.9 %copy-start.3 = (bf16[8,48,384]{2,1,0:T(8,128)(2,1)}, bf16[8,48,384]{2,1,0:T(8,128)(2,1)S(1)}, u32[]{:S(2)}) copy-start(bf16[8,48,384]{2,1,0:T(8,128)(2,1)S(1)} %pad_maximum_fusion.refs_7_) | copy-start | bytes 884740
  99.9 25.8 %collective-permute-start.29 = (bf16[8,48,384]{2,1,0:T(8,128)(2,1)S(1)}, bf16[8,48,384]{2,1,0:T(8,128)(2,1)S(1)}, u32[]{:S(2)}, u32[]{:S(2)}) collective-permute-start(bf16[8,48,384]{2,1,0:T(8,128)(2,1)S(1)} %pad_maximum_fusion.refs_7_), channel_id=1, source_target_pairs={{0,8},{4,12},{8,0},{12,4},{16,24},{20,28},{24,16},{28,20},{1,9},{5... | collective-permute-start | bytes 884744 | tf_op jit(solution)/shard_map/ppermute | solution.py:316
  100.5 25.7 %collective-permute-start.31 = (bf16[8,48,384]{2,1,0:T(8,128)(2,1)S(1)}, bf16[8,48,384]{2,1,0:T(8,128)(2,1)S(1)}, u32[]{:S(2)}, u32[]{:S(2)}) collective-permute-start(bf16[8,48,384]{2,1,0:T(8,128)(2,1)S(1)} %pad_maximum_fusion.refs_7_), channel_id=1, source_target_pairs={{0,16},{4,20},{8,24},{12,28},{16,0},{20,4},{24,8},{28,12},{1,17},{... | collective-permute-start | bytes 884744 | tf_op jit(solution)/shard_map/ppermute | solution.py:316
  102.6 23.7 %collective-permute-start.33 = (bf16[8,48,384]{2,1,0:T(8,128)(2,1)S(1)}, bf16[8,48,384]{2,1,0:T(8,128)(2,1)S(1)}, u32[]{:S(2)}, u32[]{:S(2)}) collective-permute-start(bf16[8,48,384]{2,1,0:T(8,128)(2,1)S(1)} %pad_maximum_fusion.refs_7_), channel_id=1, source_target_pairs={{0,24},{4,28},{8,16},{12,20},{16,8},{20,12},{24,0},{28,4},{1,25},{... | collective-permute-start | bytes 884744 | tf_op jit(solution)/shard_map/ppermute | solution.py:316
  110.5 24.2 %copy-start = (bf16[8,96,256]{2,1,0:T(8,128)(2,1)}, bf16[8,96,256]{2,1,0:T(8,128)(2,1)S(1)}, u32[]{:S(2)}) copy-start(bf16[8,96,256]{2,1,0:T(8,128)(2,1)S(1)} %collective-permute-done.4.refs_1_) | copy-start | bytes 1179652
  110.5 24.2 %collective-permute-start.6 = (bf16[8,96,256]{2,1,0:T(8,128)(2,1)}, bf16[8,96,256]{2,1,0:T(8,128)(2,1)S(1)}, u32[]{:S(2)}, u32[]{:S(2)}) collective-permute-start(bf16[8,96,256]{2,1,0:T(8,128)(2,1)} %get-tuple-element.48), channel_id=1, source_target_pairs={{0,3},{1,2},{2,1},{3,0},{4,7},{5,6},{6,5},{7,4},{8,11},{9,10},{10,... | collective-permute-start | bytes 1179656 | tf_op jit(solution)/shard_map/ppermute | solution.py:319
  125.7 18.1 %collective-permute-start.28 = (bf16[8,48,384]{2,1,0:T(8,128)(2,1)S(1)}, bf16[8,48,384]{2,1,0:T(8,128)(2,1)S(1)}, u32[]{:S(2)}, u32[]{:S(2)}) collective-permute-start(bf16[8,48,384]{2,1,0:T(8,128)(2,1)S(1)} %pad_maximum_fusion.refs_7_), channel_id=1, source_target_pairs={{0,4},{4,0},{8,12},{12,8},{16,20},{20,16},{24,28},{28,24},{1,5},{5... | collective-permute-start | bytes 884744 | tf_op jit(solution)/shard_map/ppermute | solution.py:316
  125.7 18.1 %copy-start.5 = (bf16[8,48,384]{2,1,0:T(8,128)(2,1)}, bf16[8,48,384]{2,1,0:T(8,128)(2,1)S(1)}, u32[]{:S(2)}) copy-start(bf16[8,48,384]{2,1,0:T(8,128)(2,1)S(1)} %collective-permute-done.29.refs_9_) | copy-start | bytes 884740
  125.7 18.1 %collective-permute-start.30 = (bf16[8,48,384]{2,1,0:T(8,128)(2,1)S(1)}, bf16[8,48,384]{2,1,0:T(8,128)(2,1)S(1)}, u32[]{:S(2)}, u32[]{:S(2)}) collective-permute-start(bf16[8,48,384]{2,1,0:T(8,128)(2,1)S(1)} %collective-permute-done.29.refs_9_), channel_id=1, source_target_pairs={{0,4},{4,0},{8,12},{12,8},{16,20},{20,16},{24,28},{28,24},{1,5},{5... | collective-permute-start | bytes 884744 | tf_op jit(solution)/shard_map/ppermute | solution.py:316
  126.2 17.6 %copy-start.6 = (bf16[8,48,384]{2,1,0:T(8,128)(2,1)}, bf16[8,48,384]{2,1,0:T(8,128)(2,1)S(1)}, u32[]{:S(2)}) copy-start(bf16[8,48,384]{2,1,0:T(8,128)(2,1)S(1)} %collective-permute-done.31.refs_11_) | copy-start | bytes 884740
  126.2 17.7 %collective-permute-start.32 = (bf16[8,48,384]{2,1,0:T(8,128)(2,1)S(1)}, bf16[8,48,384]{2,1,0:T(8,128)(2,1)S(1)}, u32[]{:S(2)}, u32[]{:S(2)}) collective-permute-start(bf16[8,48,384]{2,1,0:T(8,128)(2,1)S(1)} %collective-permute-done.31.refs_11_), channel_id=1, source_target_pairs={{0,4},{4,0},{8,12},{12,8},{16,20},{20,16},{24,28},{28,24},{1,5},{5... | collective-permute-start | bytes 884744 | tf_op jit(solution)/shard_map/ppermute | solution.py:316
  126.3 17.5 %copy-start.7 = (bf16[8,48,384]{2,1,0:T(8,128)(2,1)}, bf16[8,48,384]{2,1,0:T(8,128)(2,1)S(1)}, u32[]{:S(2)}) copy-start(bf16[8,48,384]{2,1,0:T(8,128)(2,1)S(1)} %collective-permute-done.33.refs_13_) | copy-start | bytes 884740
  126.3 17.6 %collective-permute-start.34 = (bf16[8,48,384]{2,1,0:T(8,128)(2,1)S(1)}, bf16[8,48,384]{2,1,0:T(8,128)(2,1)S(1)}, u32[]{:S(2)}, u32[]{:S(2)}) collective-permute-start(bf16[8,48,384]{2,1,0:T(8,128)(2,1)S(1)} %collective-permute-done.33.refs_13_), channel_id=1, source_target_pairs={{0,4},{4,0},{8,12},{12,8},{16,20},{20,16},{24,28},{28,24},{1,5},{5... | collective-permute-start | bytes 884744 | tf_op jit(solution)/shard_map/ppermute | solution.py:316
  156.3 42.8 %collective-permute-start.35 = (bf16[2,96,256]{2,1,0:T(8,128)(2,1)}, bf16[2,96,256]{2,1,0:T(8,128)(2,1)S(1)}, u32[]{:S(2)}, u32[]{:S(2)}) collective-permute-start(bf16[2,96,256]{2,1,0:T(8,128)(2,1)} %get-tuple-element.32), channel_id=1, source_target_pairs={{0,1},{1,0},{2,3},{3,2},{4,5},{5,4},{6,7},{7,6},{8,9},{9,8},{10,11... | collective-permute-start | bytes 294920 | tf_op jit(solution)/shard_map/ppermute | solution.py:319
  156.4 44.6 %collective-permute-start.36 = (bf16[2,96,256]{2,1,0:T(8,128)(2,1)}, bf16[2,96,256]{2,1,0:T(8,128)(2,1)S(1)}, u32[]{:S(2)}, u32[]{:S(2)}) collective-permute-start(bf16[2,96,256]{2,1,0:T(8,128)(2,1)} %get-tuple-element.33), channel_id=1, source_target_pairs={{0,2},{1,3},{2,0},{3,1},{4,6},{5,7},{6,4},{7,5},{8,10},{9,11},{10,... | collective-permute-start | bytes 294920 | tf_op jit(solution)/shard_map/ppermute | solution.py:319
  159.0 42.1 %collective-permute-start.37 = (bf16[2,96,256]{2,1,0:T(8,128)(2,1)}, bf16[2,96,256]{2,1,0:T(8,128)(2,1)S(1)}, u32[]{:S(2)}, u32[]{:S(2)}) collective-permute-start(bf16[2,96,256]{2,1,0:T(8,128)(2,1)} %get-tuple-element.34), channel_id=1, source_target_pairs={{0,3},{1,2},{2,1},{3,0},{4,7},{5,6},{6,5},{7,4},{8,11},{9,10},{10,... | collective-permute-start | bytes 294920 | tf_op jit(solution)/shard_map/ppermute | solution.py:319
  172.5 31.4 %collective-permute-start.38 = (bf16[2,96,256]{2,1,0:T(8,128)(2,1)}, bf16[2,96,256]{2,1,0:T(8,128)(2,1)S(1)}, u32[]{:S(2)}, u32[]{:S(2)}) collective-permute-start(bf16[2,96,256]{2,1,0:T(8,128)(2,1)} %get-tuple-element.36), channel_id=1, source_target_pairs={{0,1},{1,0},{2,3},{3,2},{4,5},{5,4},{6,7},{7,6},{8,9},{9,8},{10,11... | collective-permute-start | bytes 294920 | tf_op jit(solution)/shard_map/ppermute | solution.py:319
  172.6 33.1 %collective-permute-start.39 = (bf16[2,96,256]{2,1,0:T(8,128)(2,1)}, bf16[2,96,256]{2,1,0:T(8,128)(2,1)S(1)}, u32[]{:S(2)}, u32[]{:S(2)}) collective-permute-start(bf16[2,96,256]{2,1,0:T(8,128)(2,1)} %get-tuple-element.37), channel_id=1, source_target_pairs={{0,2},{1,3},{2,0},{3,1},{4,6},{5,7},{6,4},{7,5},{8,10},{9,11},{10,... | collective-permute-start | bytes 294920 | tf_op jit(solution)/shard_map/ppermute | solution.py:319
  199.2 7.7 %collective-permute-start.40 = (bf16[2,96,256]{2,1,0:T(8,128)(2,1)S(1)}, bf16[2,96,256]{2,1,0:T(8,128)(2,1)S(1)}, u32[]{:S(2)}, u32[]{:S(2)}) collective-permute-start(bf16[2,96,256]{2,1,0:T(8,128)(2,1)S(1)} %copy-done.45), channel_id=1, source_target_pairs={{0,3},{1,2},{2,1},{3,0},{4,7},{5,6},{6,5},{7,4},{8,11},{9,10},{10,... | collective-permute-start | bytes 294920 | tf_op jit(solution)/shard_map/ppermute | solution.py:319
  201.0 8.1 %collective-permute-start.41 = (bf16[2,96,256]{2,1,0:T(8,128)(2,1)S(1)}, bf16[2,96,256]{2,1,0:T(8,128)(2,1)S(1)}, u32[]{:S(2)}, u32[]{:S(2)}) collective-permute-start(bf16[2,96,256]{2,1,0:T(8,128)(2,1)S(1)} %copy-done.44), channel_id=1, source_target_pairs={{0,1},{1,0},{2,3},{3,2},{4,5},{5,4},{6,7},{7,6},{8,9},{9,8},{10,11... | collective-permute-start | bytes 294920 | tf_op jit(solution)/shard_map/ppermute | solution.py:319
  201.1 13.5 %collective-permute-start.42 = (bf16[2,96,256]{2,1,0:T(8,128)(2,1)S(1)}, bf16[2,96,256]{2,1,0:T(8,128)(2,1)S(1)}, u32[]{:S(2)}, u32[]{:S(2)}) collective-permute-start(bf16[2,96,256]{2,1,0:T(8,128)(2,1)S(1)} %copy-done.43), channel_id=1, source_target_pairs={{0,2},{1,3},{2,0},{3,1},{4,6},{5,7},{6,4},{7,5},{8,10},{9,11},{10,... | collective-permute-start | bytes 294920 | tf_op jit(solution)/shard_map/ppermute | solution.py:319
  203.9 10.8 %collective-permute-start.43 = (bf16[2,96,256]{2,1,0:T(8,128)(2,1)S(1)}, bf16[2,96,256]{2,1,0:T(8,128)(2,1)S(1)}, u32[]{:S(2)}, u32[]{:S(2)}) collective-permute-start(bf16[2,96,256]{2,1,0:T(8,128)(2,1)S(1)} %copy-done.42), channel_id=1, source_target_pairs={{0,3},{1,2},{2,1},{3,0},{4,7},{5,6},{6,5},{7,4},{8,11},{9,10},{10,... | collective-permute-start | bytes 294920 | tf_op jit(solution)/shard_map/ppermute | solution.py:319
  205.7 9.0 %collective-permute-start.44 = (bf16[2,96,256]{2,1,0:T(8,128)(2,1)S(1)}, bf16[2,96,256]{2,1,0:T(8,128)(2,1)S(1)}, u32[]{:S(2)}, u32[]{:S(2)}) collective-permute-start(bf16[2,96,256]{2,1,0:T(8,128)(2,1)S(1)} %copy-done.41), channel_id=1, source_target_pairs={{0,1},{1,0},{2,3},{3,2},{4,5},{5,4},{6,7},{7,6},{8,9},{9,8},{10,11... | collective-permute-start | bytes 294920 | tf_op jit(solution)/shard_map/ppermute | solution.py:319
  206.9 14.2 %collective-permute-start.45 = (bf16[2,96,256]{2,1,0:T(8,128)(2,1)S(1)}, bf16[2,96,256]{2,1,0:T(8,128)(2,1)S(1)}, u32[]{:S(2)}, u32[]{:S(2)}) collective-permute-start(bf16[2,96,256]{2,1,0:T(8,128)(2,1)S(1)} %copy-done.40), channel_id=1, source_target_pairs={{0,2},{1,3},{2,0},{3,1},{4,6},{5,7},{6,4},{7,5},{8,10},{9,11},{10,... | collective-permute-start | bytes 294920 | tf_op jit(solution)/shard_map/ppermute | solution.py:319
  209.1 12.1 %collective-permute-start.46 = (bf16[2,96,256]{2,1,0:T(8,128)(2,1)S(1)}, bf16[2,96,256]{2,1,0:T(8,128)(2,1)S(1)}, u32[]{:S(2)}, u32[]{:S(2)}) collective-permute-start(bf16[2,96,256]{2,1,0:T(8,128)(2,1)S(1)} %copy-done.39), channel_id=1, source_target_pairs={{0,3},{1,2},{2,1},{3,0},{4,7},{5,6},{6,5},{7,4},{8,11},{9,10},{10,... | collective-permute-start | bytes 294920 | tf_op jit(solution)/shard_map/ppermute | solution.py:319
  (29 other events, 169.7 us)

commit v2 on v1

v2 whole, which is shorter than its diff:
```python
import math

import jax
import jax.numpy as jnp
from jax import lax
from jax.experimental import pallas as pl
from jax.experimental.pallas import tpu as pltpu
from jax.sharding import PartitionSpec as P

EPSILON = 1e-05
LOG2E = math.log2(math.e)
LANES = 128
ROWS_BY_ROWS = (((1,), (1,)), ((), ()))
CONTRACT_FIRST = (((0,), (0,)), ((), ()))
VMEM = pltpu.CompilerParams(vmem_limit_bytes=56 * 2**20)
SMEM = pl.BlockSpec(memory_space=pltpu.SMEM)
f32 = jnp.float32
bf16 = jnp.bfloat16


def whole(array):
    return pl.BlockSpec(array.shape, lambda step, rank=array.ndim: (0,) * rank)


def standardize(values):
    average = jnp.mean(values, axis=-1, keepdims=True)
    centred = values - average
    variance = jnp.mean(centred * centred, axis=-1, keepdims=True)
    return centred * lax.rsqrt(variance + EPSILON)


def opm_inputs_kernel(x_ref, mask_ref, gain_ref, wl_ref, wr_ref, left_ref, right_ref, scratch):
    seqs, residues, channels = x_ref.shape
    width = wr_ref.shape[0]
    per_group = LANES // width
    left_weight = wl_ref[...].astype(f32).T
    groups = residues // per_group
    halves, slabs = left_ref.shape[:2]
    half_groups = slabs - 1
    half_residues = residues // halves
    normed = standardize(x_ref[...].reshape(seqs * residues, channels).astype(f32)) * gain_ref[...]
    for piece in range(channels // LANES):
        scratch[piece] = normed[:, piece * LANES : (piece + 1) * LANES]
    narrow = normed.astype(bf16).reshape(seqs, residues, channels)
    mask = mask_ref[...].astype(f32)
    right = [
        lax.dot_general(wr_ref[...], narrow[s], ROWS_BY_ROWS, preferred_element_type=f32) * mask[s : s + 1, :]
        for s in range(seqs)
    ]
    right_ref[:width] = jnp.swapaxes(jnp.stack(right, 0), 0, 1).astype(bf16)
    right_ref[width] = mask.astype(bf16)
    total = None
    for q in range(per_group):
        rows = jnp.concatenate(
            [scratch[piece, pl.ds(q, seqs * groups, stride=per_group), :] for piece in range(channels // LANES)], 1
        ).astype(bf16)
        sides = [jnp.zeros((channels, q * width), f32), jnp.zeros((channels, LANES - (q + 1) * width), f32)]
        placed = jnp.concatenate([a for a in (sides[0], left_weight, sides[1]) if a.shape[1]], 1).astype(bf16)
        part = jnp.dot(rows, placed, preferred_element_type=f32)
        total = part if total is None else total + part
    left = jnp.swapaxes(total.reshape(seqs, groups, LANES), 0, 1)
    row = lax.broadcasted_iota(jnp.int32, (residues, residues * width), 0) * width
    col = lax.broadcasted_iota(jnp.int32, (residues, residues * width), 1)
    spread = ((col >= row) & (col < row + width)).astype(f32).astype(bf16)
    mask_wide = jnp.dot(mask.astype(bf16), spread, preferred_element_type=f32)
    for g in range(groups):
        left_ref[g // half_groups, g % half_groups] = (left[g] * mask_wide[:, g * LANES : (g + 1) * LANES]).astype(bf16)
    for half in range(halves):
        part = mask[:, half * half_residues : (half + 1) * half_residues]
        left_ref[half, half_groups] = jnp.concatenate(
            [part, jnp.zeros((seqs, LANES - half_residues), f32)], 1
        ).astype(bf16)


def opm_inputs(x, mask, gain, wl, wr, half_residues, block=16):
    seqs, residues, channels = x.shape
    width = wl.shape[1]
    per_group = LANES // width
    halves = residues // half_residues
    slabs = half_residues // per_group + 1
    gain = gain.reshape(1, channels)
    return pl.pallas_call(
        opm_inputs_kernel,
        grid=(seqs // block,),
        in_specs=[
            pl.BlockSpec((block, residues, channels), lambda s: (s, 0, 0)),
            pl.BlockSpec((block, residues), lambda s: (s, 0)),
            whole(gain),
            whole(wl.T),
            whole(wr.T),
        ],
        out_specs=[
            pl.BlockSpec((halves, slabs, block, LANES), lambda s: (0, 0, s, 0)),
            pl.BlockSpec((width + 1, block, residues), lambda s: (0, s, 0)),
        ],
        out_shape=[
            jax.ShapeDtypeStruct((halves, slabs, seqs, LANES), bf16),
            jax.ShapeDtypeStruct((width + 1, seqs, residues), bf16),
        ],
        scratch_shapes=[pltpu.VMEM((channels // LANES, block * residues, LANES), f32)],
        compiler_params=VMEM,
        name="opm_inputs",
    )(x, mask, gain, wl.T, wr.T)


def pair_tile(mine, left, right, duo, chain, kernel, gain, logit, block=16):
    rows, residues, channels = duo.shape
    heads = logit.shape[1]
    parts, slabs, seqs = left.shape[:3]
    groups = slabs - 1
    width = right.shape[1] - 1

    def body(mine_ref, left_ref, right_ref, *refs):
        duo_ref, chain_ref, kernel_ref, gain_ref, logit_ref, out_ref, bias_ref, rhs, lhs, scale, w_ref = refs
        step = pl.program_id(0)

        @pl.when(step == 0)
        def _():
            for n in range(parts):
                for b in range(width + 1):
                    rhs[n * seqs : (n + 1) * seqs, b * LANES : b * LANES + residues] = right_ref[n, b]
                for g in range(slabs):
                    lhs[n * seqs : (n + 1) * seqs, g * LANES : (g + 1) * LANES] = left_ref[n, g]
            counts = lax.dot_general(
                lhs[:, groups * LANES :], rhs[:, width * LANES :], CONTRACT_FIRST, preferred_element_type=f32
            )[:rows, :residues]
            flags = chain_ref[...].astype(f32)
            both_flags = []
            for size, at in ((rows, mine_ref[0] * rows), (residues, mine_ref[1] * residues)):
                place = lax.broadcasted_iota(jnp.int32, (chain.shape[1], size), 0)
                pick = place == lax.broadcasted_iota(jnp.int32, (chain.shape[1], size), 1) + at
                both_flags.append(jnp.dot(flags, pick.astype(f32), preferred_element_type=f32))
            present = lax.dot_general(*both_flags, CONTRACT_FIRST, preferred_element_type=f32)
            scale[:, :residues] = present / (counts + 0.001)
            mixing = jnp.swapaxes(kernel_ref[...].astype(f32).reshape(width, width, channels), 0, 1)
            w_ref[...] = mixing.reshape(width * width, channels).T.astype(bf16)

        span = block * width
        picked = lhs[:, pl.ds(pl.multiple_of(step * span, LANES), span)]
        outer = lax.dot_general(
            picked, rhs[:, : width * LANES], CONTRACT_FIRST, preferred_element_type=f32
        ).astype(bf16)
        row_scale = scale[pl.ds(pl.multiple_of(step * block, 8), block), :]
        biases = []
        for first in range(0, block, 2):
            both = [
                jnp.concatenate(
                    [outer[i * width : (i + 1) * width, b * LANES : (b + 1) * LANES] for b in range(width)], 0
                )
                for i in (first, first + 1)
            ]
            update = jnp.dot(w_ref[...], jnp.concatenate(both, 1), preferred_element_type=f32)
            for k, i in enumerate((first, first + 1)):
                fresh = duo_ref[i] + (update[:, k * LANES : (k + 1) * LANES] * row_scale[i : i + 1, :]).T[:residues]
                out_ref[i] = fresh
                pair_input = (standardize(fresh) * gain_ref[...]).astype(bf16)
                biases.append(
                    lax.dot_general(logit_ref[...], pair_input, ROWS_BY_ROWS, preferred_element_type=f32)
                )
        bias_ref[...] = jnp.swapaxes(jnp.stack(biases, 0), 0, 1).astype(bf16)

    operands = [
        left,
        right,
        duo,
        chain,
        kernel,
        gain.reshape(1, channels),
        logit.T,
    ]
    specs = [whole(array) for array in operands]
    specs[2] = pl.BlockSpec((block, residues, channels), lambda s: (s, 0, 0))
    return pl.pallas_call(
        body,
        grid=(rows // block,),
        in_specs=[SMEM, *specs],
        out_specs=[
            pl.BlockSpec((block, residues, channels), lambda s: (s, 0, 0)),
            pl.BlockSpec((heads, block, residues), lambda s: (0, s, 0)),
        ],
        out_shape=[
            jax.ShapeDtypeStruct((rows, residues, channels), f32),
            jax.ShapeDtypeStruct((heads, rows, residues), bf16),
        ],
        scratch_shapes=[
            pltpu.VMEM((parts * seqs, (width + 1) * LANES), bf16),
            pltpu.VMEM((parts * seqs, slabs * LANES), bf16),
            pltpu.VMEM((rows, LANES), f32),
            pltpu.VMEM((channels, width * width), bf16),
        ],
        compiler_params=VMEM,
        name="pair_tile",
    )(mine, *operands)


def attend(mine, pieces, gain, kernel, mask, low, high, closing, first, count):
    cols = len(pieces)
    residues, channels = pieces[0].shape[1:]
    arrays = [array for array, offsets in (*low, *high)]
    lists = [offsets for array, offsets in (*low, *high)]
    per_half, side, total = arrays[0].shape[1:]
    heads = 2 * per_half
    inner = closing.shape[0]
    depth = inner // heads
    gain = gain.reshape(1, channels)
    group = LANES // depth
    scale = depth**-0.5 * LOG2E

    def body(mine_ref, gain_ref, kernel_ref, mask_ref, closing_ref, *refs):
        x_refs, refs = refs[:cols], refs[cols:]
        bias_refs, out_refs = refs[: len(arrays)], refs[len(arrays) : -2]
        bias, turned = refs[-2:]

        @pl.when(pl.program_id(0) == 0)
        def _():
            for n, (ref, offsets) in enumerate(zip(bias_refs, lists)):
                start = n // len(low) * per_half
                for e, offset in enumerate(offsets):
                    place = pl.ds(pl.multiple_of((offset ^ mine_ref[2]) * side, 8), side)
                    for h in range(per_half):
                        bias[start + h, place, :] = ref[e, h].astype(f32) * LOG2E
            turned[...] = kernel_ref[:, inner : 2 * inner].T

        row_mask = (mask_ref[0].astype(f32) - 1.0) * (1e9 * LOG2E)
        head_of = lax.broadcasted_iota(jnp.int32, (total, LANES), 1) // depth
        zero = jnp.zeros((depth, total), bf16)
        x = jnp.concatenate([ref[0] for ref in x_refs], 0).astype(f32)
        narrow = (standardize(x) * gain_ref[...]).astype(bf16)
        keys = lax.dot_general(turned[...], narrow, ROWS_BY_ROWS, preferred_element_type=f32).astype(bf16)
        queries, all_values, gates = [
            jnp.dot(narrow, kernel_ref[:, n * inner : (n + 1) * inner], preferred_element_type=f32).astype(bf16)
            for n in (0, 2, 3)
        ]
        gated = []
        for first_lane in range(0, inner, LANES):
            span = slice(first_lane, first_lane + LANES)
            key = keys[span, :]
            value = all_values[:, span]
            alone, values = [], []
            for h in range(group):
                mine_rows = key[h * depth : (h + 1) * depth]
                alone.append(jnp.concatenate([mine_rows if n == h else zero for n in range(group)], 0))
                here = head_of == h
                values.append(
                    jnp.concatenate(
                        [jnp.where(here, value, jnp.zeros_like(value)), here.astype(f32).astype(bf16)], 1
                    )
                )
            scores = jnp.dot(queries[:, span], jnp.concatenate(alone, 1), preferred_element_type=f32)
            weights = []
            for h in range(group):
                own = scores[:, h * total : (h + 1) * total] * scale
                own = own + bias[first_lane // depth + h] + row_mask
                highest = jnp.max(own, axis=1, keepdims=True)
                weights.append(jnp.exp2(own - highest).astype(bf16))
            mixed = jnp.dot(
                jnp.concatenate(weights, 1), jnp.concatenate(values, 0), preferred_element_type=f32
            )
            gate = gates[:, span].astype(f32)
            gated.append((mixed[:, :LANES] / mixed[:, LANES:] * jax.nn.sigmoid(gate)).astype(bf16))
        change = jnp.dot(jnp.concatenate(gated, 1), closing_ref[...], preferred_element_type=f32)
        for k in range(cols):
            own = x[k * residues : (k + 1) * residues] + change[k * residues : (k + 1) * residues]
            out_refs[k][0] = own.astype(bf16)

    return pl.pallas_call(
        body,
        grid=(count,),
        in_specs=[
            SMEM,
            whole(gain),
            whole(kernel),
            pl.BlockSpec((1, 1, total), lambda s: (s + first, 0, 0)),
            whole(closing),
        ]
        + [pl.BlockSpec((1, residues, channels), lambda s: (s + first, 0, 0))] * cols
        + [whole(array) for array in arrays],
        out_specs=[pl.BlockSpec((1, residues, channels), lambda s: (s, 0, 0))] * cols,
        out_shape=[jax.ShapeDtypeStruct((count, residues, channels), bf16)] * cols,
        scratch_shapes=[pltpu.VMEM((heads, total, total), f32), pltpu.VMEM((inner, channels), bf16)],
        compiler_params=VMEM,
        name="attend",
    )(mine, gain, kernel, mask, closing, *pieces, *arrays)


def make_shards(mesh):
    n_row, n_col = mesh.shape["row"], mesh.shape["col"]
    halves = n_row // n_col

    def by_row(x, k):
        return lax.ppermute(x, "row", [(r, r ^ k) for r in range(n_row)])

    def by_col(x, k):
        return lax.ppermute(x, "col", [(c, c ^ k) for c in range(n_col)])

    def gather_rows(first, second):
        bits = []
        k = 2
        while k < n_row:
            bits.append(k)
            k *= 2
        held = [(first[None], [0]), (second[None], [0])]
        for step in range(len(bits)):
            got = []
            for part, k in ((0, bits[step]), (1, bits[-1 - step])):
                array, offsets = held[part]
                got.append(
                    (jnp.concatenate([array, by_row(array, k)], 0), offsets + [o ^ k for o in offsets])
                )
            held = got
        return [
            [(array, offsets), (by_row(array, 1), [o ^ 1 for o in offsets])] for array, offsets in held
        ]

    def shards(
        msa,
        available,
        chain_site_available,
        duo_embedding,
        averaging_gain,
        lineup_gain,
        duo_gain,
        left_kernel,
        right_kernel,
        kronecker_kernel,
        logit_kernel,
        projection_kernel,
        closing_kernel,
    ):
        seqs, residues, channels = msa.shape
        rows = duo_embedding.shape[0]
        r, c = lax.axis_index("row"), lax.axis_index("col")
        share = seqs // n_col
        mine = jnp.stack([r, c, r ^ (halves * c)]).astype(jnp.int32)

        left, right = opm_inputs(msa, available, averaging_gain, left_kernel, right_kernel, rows)
        rights = lax.all_gather(right, "row", axis=0)
        spread = lax.all_gather(left, "col", axis=0, tiled=True)
        left_rows = lax.all_to_all(spread, "row", 0, 0, tiled=True)

        msa_late, spread_late = lax.optimization_barrier((msa, spread))
        x = [lax.dynamic_slice_in_dim(msa_late, (c ^ k) * share, share, 0) for k in range(n_col)]
        x = [by_col(piece, k) if k else piece for k, piece in enumerate(x)]
        mask = lax.dynamic_slice_in_dim(spread_late[:, -1, :, :rows], c * share, share, 1)
        mask = mask.reshape(n_col, halves, share, rows)
        mask = jnp.stack([lax.dynamic_index_in_dim(mask, c ^ k, 0, keepdims=False) for k in range(n_col)])
        rows_mask = mask.transpose(2, 0, 1, 3).reshape(share, 1, residues * n_col)

        duo_after_averaging, tile = pair_tile(
            mine,
            left_rows,
            rights,
            duo_embedding,
            chain_site_available.reshape(1, -1),
            kronecker_kernel,
            duo_gain,
            logit_kernel,
        )
        tile, x[1:] = lax.optimization_barrier((tile, x[1:]))
        tiles = [tile] + [by_col(tile, k) for k in range(1, n_col)]
        cut = tile.shape[0] // 2
        low, high = gather_rows(
            jnp.concatenate([t[:cut] for t in tiles], 2), jnp.concatenate([t[cut:] for t in tiles], 2)
        )
        sent = []
        first = 0
        for count in chunks(share):
            held = rows_mask
            if len(sent) > 1:
                held, sent[-2] = lax.optimization_barrier((rows_mask, sent[-2]))
            outs = attend(
                mine, x, lineup_gain, projection_kernel, held, low, high, closing_kernel, first, count
            )
            sent.append([by_col(piece, k) if k else piece for k, piece in enumerate(outs)])
            first += count
        refreshed = jnp.zeros_like(msa)
        first = 0
        for count, parts in zip(chunks(share), sent):
            for k, piece in enumerate(parts):
                refreshed = lax.dynamic_update_slice_in_dim(refreshed, piece, (c ^ k) * share + first, 0)
            first += count
        return refreshed, duo_after_averaging

    return shards


def chunks(share):
    most = max(-(-3 * share // 8), 1)
    counts = []
    while sum(counts) < share:
        counts.append(min(most, share - sum(counts)))
    return counts


def solution(mesh):
    split = P("row", "col", None)
    placed = (split, P("row", "col"), P(), split, P(), P(), P(), P(), P(), P(), P(), P(), P())
    return jax.shard_map(
        make_shards(mesh), mesh=mesh, in_specs=placed, out_specs=(split, split), check_vma=False
    )
```

time: 224 us -> 165 us (0.74)
  starting transfers between devices: 77.2 us -> 33.7 us
  Pallas kernels: 80.4 us -> 56 us
  blocking collectives: 0 us -> 23.4 us
  waiting for transfers between devices: 44.3 us -> 28.2 us
  between operations: 1.67 us -> 14.6 us
  local copies, waits for them, and re-layouts: 15.9 us -> 7.76 us
    ppermute x12 -> x0, starting transfers between devices: 33.9 us -> none  [by_both(): return lax.ppermute(x, ('row', 'col'), pairs)]
    pallas_call x6 -> x4, Pallas kernels: 58.7 us -> 34.3 us  [the longest x3 30.1 us: attend(): pl.pallas_call(body, grid=(count,), in_specs=[SMEM, whole(gain), whole(ke...]
    all_gather x0 -> x1, blocking collectives: none -> 23.4 us  [shards(): spread = lax.all_gather(left, 'col', axis=0, tiled=True)]
    ppermute x21 -> x15, waiting for transfers between devices: 33.5 us -> 11.8 us  [by_col(): return lax.ppermute(x, 'col', [(c, c ^ k) for c in range(n_col)])]
    ppermute x12 -> x0, waiting for transfers between devices: 10.8 us -> none  [by_both(): return lax.ppermute(x, ('row', 'col'), pairs)]
    ppermute x14 -> x6, waiting for transfers between devices: 0.04 us -> 9.72 us  [by_row(): return lax.ppermute(x, 'row', [(r, r ^ k) for r in range(n_row)])]
    ppermute x21 -> x15, starting transfers between devices: 33.2 us -> 24.4 us  [by_col(): return lax.ppermute(x, 'col', [(c, c ^ k) for c in range(n_col)])]
    all_to_all x0 -> x1, waiting for transfers between devices: none -> 6.64 us  [shards(): left_rows = lax.all_to_all(spread, 'row', 0, 0, tiled=True)]
  transfers between devices with their start and end apart: 47 -> 23, of which waited for: 11 -> 9; matrix products, arithmetic and copies ran while one was open for 6% -> 4% of each run, Pallas kernels for 29% -> 25%
where the time goes in v2:
time: 165 us
  Pallas kernels  56 us (34%)
  starting transfers between devices  33.7 us (20%)
  waiting for transfers between devices  28.2 us (17%)
  blocking collectives  23.4 us (14%)
  between operations  14.6 us (9%)
  local copies, waits for them, and re-layouts  7.76 us (5%)
    pallas_call x3, Pallas kernels, attend(): pl.pallas_call(body, grid=(count,), in_specs=[SMEM, whole(gain), whole(ke...  30.1 us
    ppermute x15, starting transfers between devices, by_col(): return lax.ppermute(x, 'col', [(c, c ^ k) for c in range(n_col)])  24.4 us
    all_gather x1, blocking collectives, shards(): spread = lax.all_gather(left, 'col', axis=0, tiled=True)  23.4 us
    pallas_call x1, Pallas kernels, pair_tile(): pl.pallas_call(body, grid=(rows // block,), in_specs=[SMEM, *specs], out_...  21.7 us
    ppermute x15, waiting for transfers between devices, by_col(): return lax.ppermute(x, 'col', [(c, c ^ k) for c in range(n_col)])  11.8 us
    ppermute x6, waiting for transfers between devices, by_row(): return lax.ppermute(x, 'row', [(r, r ^ k) for r in range(n_row)])  9.72 us
    all_to_all x1, waiting for transfers between devices, shards(): left_rows = lax.all_to_all(spread, 'row', 0, 0, tiled=True)  6.64 us
    ppermute x6, starting transfers between devices, by_row(): return lax.ppermute(x, 'row', [(r, r ^ k) for r in range(n_row)])  5.05 us
  transfers between devices with their start and end apart: 23, of which 9 were waited for; matrix products, arithmetic and copies ran while one was open for 4% of the time, Pallas kernels for 25%

profile of v2, /device:TPU:0, one launch (start us, length us, event | category | flops | bytes accessed | tf_op | source)
XLA Modules:
  0.0 164.7 jit_solution(3328899743043891997)
XLA Ops:
  7.2 0.0 all-gather.3.cloned.1.call-start
  7.2 4.2 %opm_inputs.1 = (bf16[2,13,32,128]{3,2,1,0:T(8,128)(2,1)}, bf16[33,32,96]{2,1,0:T(8,128)(2,1)}) custom-call(bf16[32,96,256]{2,1,0:T(8,128)(2,1)} %x_ref.1, s32[32,96]{1,0:T(8,128)} %mask_ref.1, f32[1,256]{1,0:T(1,128)} %bitcast.25, bf16[32,256]{1,0:T(8,128)(2,1)} %bitcast.19, bf16[32,256]{1,0:T(8,128)(2,1)} %bitcast.20), custom_call_target="tpu_custom_call" | custom-call | tf_op jit(solution)/shard_map/opm_inputs/pallas_call | solution.py:82
  11.4 0.0 all-gather.3.cloned.1.call-update
  11.5 23.4 %all_gather.9 = bf16[8,13,32,128]{3,2,1,0:T(8,128)(2,1)} all-gather(bf16[2,13,32,128]{3,2,1,0:T(8,128)(2,1)} %get-tuple-element.29), channel_id=1, replica_groups=mesh['row'=8,'col'=4] {'col'}, dimensions={0}, use_global_device_ids=true | all-gather | bytes 1064960 | tf_op jit(solution)/shard_map/all_gather | solution.py:338
  34.9 4.2 %all-to-all-start = ((bf16[8,13,32,128]{3,2,1,0:T(8,128)(2,1)}), bf16[8,13,32,128]{3,2,1,0:T(8,128)(2,1)}, u32[]{:S(2)}, u32[]{:S(2)}) async-start(bf16[8,13,32,128]{3,2,1,0:T(8,128)(2,1)} %all_gather.9), calls=%async_computation | async-start | bytes 1703936 | tf_op jit(solution)/shard_map/all_to_all | solution.py:339
  39.1 0.0 copy-start.12
  39.2 1.0 constant_dynamic-slice_fusion
  40.2 2.4 %collective-permute-start.1 = (bf16[8,96,256]{2,1,0:T(8,128)(2,1)S(1)}, bf16[8,96,256]{2,1,0:T(8,128)(2,1)S(1)}, u32[]{:S(2)}, u32[]{:S(2)}) collective-permute-start(bf16[8,96,256]{2,1,0:T(8,128)(2,1)S(1)} %get-tuple-element.57), channel_id=1, source_target_pairs={{0,2},{1,3},{2,0},{3,1},{4,6},{5,7},{6,4},{7,5},{8,10},{9,11},{10,... | collective-permute-start | bytes 1179656 | tf_op jit(solution)/shard_map/ppermute | solution.py:294
  42.6 2.0 %collective-permute-start.2 = (bf16[8,96,256]{2,1,0:T(8,128)(2,1)S(1)}, bf16[8,96,256]{2,1,0:T(8,128)(2,1)S(1)}, u32[]{:S(2)}, u32[]{:S(2)}) collective-permute-start(bf16[8,96,256]{2,1,0:T(8,128)(2,1)S(1)} %get-tuple-element.56), channel_id=1, source_target_pairs={{0,3},{1,2},{2,1},{3,0},{4,7},{5,6},{6,5},{7,4},{8,11},{9,10},{10,... | collective-permute-start | bytes 1179656 | tf_op jit(solution)/shard_map/ppermute | solution.py:294
  44.6 0.6 reshape.30.refs_1_
  45.2 0.6 pad_add_fusion.mine_ref
  45.8 6.6 %all-to-all-done.left_ref = bf16[8,13,32,128]{3,2,1,0:T(8,128)(2,1)} async-done(((bf16[8,13,32,128]{3,2,1,0:T(8,128)(2,1)}), bf16[8,13,32,128]{3,2,1,0:T(8,128)(2,1)}, u32[]{:S(2)}, u32[]{:S(2)}) %all-to-all-start) | async-done | bytes 852000 | tf_op jit(solution)/shard_map/all_to_all | solution.py:339
  52.4 21.7 %pair_tile.1 = (f32[48,96,128]{2,1,0:T(8,128)}, bf16[8,48,96]{2,1,0:T(8,128)(2,1)}) custom-call(s32[3]{0:T(128)} %pad_add_fusion.mine_ref, bf16[8,13,32,128]{3,2,1,0:T(8,128)(2,1)} %all-to-all-done.left_ref, bf16[8,33,32,96]{3,2,1,0:T(8,128)(2,1)} %bitcast.17, f32[48,96,128]{2,1,0:T(8,128)} %refs_0_.1, s32[1,384]{1,0:T(1,128)} %reshape.30.refs_1_, ...), custom_call_target="tpu_custom_call" | custom-call | tf_op jit(solution)/shard_map/pair_tile/pallas_call | solution.py:173
  74.1 0.0 collective-permute-done.refs_1_
  74.1 0.0 collective-permute-done.2.refs_3_
  74.1 4.2 %collective-permute-start.3 = (bf16[8,48,96]{2,1,0:T(8,128)(2,1)}, bf16[8,48,96]{2,1,0:T(8,128)(2,1)S(1)}, u32[]{:S(2)}, u32[]{:S(2)}) collective-permute-start(bf16[8,48,96]{2,1,0:T(8,128)(2,1)} %get-tuple-element.37), channel_id=1, source_target_pairs={{0,1},{1,0},{2,3},{3,2},{4,5},{5,4},{6,7},{7,6},{8,9},{9,8},{10,11... | collective-permute-start | bytes 221192 | tf_op jit(solution)/shard_map/ppermute | solution.py:294
  78.3 0.6 collective-permute-start.4
  78.9 1.8 %collective-permute-start.5 = (bf16[8,48,96]{2,1,0:T(8,128)(2,1)}, bf16[8,48,96]{2,1,0:T(8,128)(2,1)S(1)}, u32[]{:S(2)}, u32[]{:S(2)}) collective-permute-start(bf16[8,48,96]{2,1,0:T(8,128)(2,1)} %get-tuple-element.37), channel_id=1, source_target_pairs={{0,3},{1,2},{2,1},{3,0},{4,7},{5,6},{6,5},{7,4},{8,11},{9,10},{10,... | collective-permute-start | bytes 221192 | tf_op jit(solution)/shard_map/ppermute | solution.py:294
  80.7 0.8 fusion
  81.6 0.4 collective-permute-done.3
  81.9 6.3 %collective-permute-done.4 = bf16[8,48,96]{2,1,0:T(8,128)(2,1)S(1)} collective-permute-done((bf16[8,48,96]{2,1,0:T(8,128)(2,1)}, bf16[8,48,96]{2,1,0:T(8,128)(2,1)S(1)}, u32[]{:S(2)}, u32[]{:S(2)}) %collective-permute-start.4) | collective-permute-done | bytes 73760 | tf_op jit(solution)/shard_map/ppermute | solution.py:294
  88.2 0.0 collective-permute-done.5
  88.2 0.1 maximum_bitcast_fusion.1
  88.4 1.6 collective-permute-start.9
  90.0 0.1 maximum_bitcast_fusion
  90.1 1.5 collective-permute-start.6
  91.7 1.9 %collective-permute-done.9 = bf16[1,4,48,384]{3,2,1,0:T(8,128)(2,1)S(1)} collective-permute-done((bf16[1,4,48,384]{3,2,1,0:T(8,128)(2,1)S(1)}, bf16[1,4,48,384]{3,2,1,0:T(8,128)(2,1)S(1)}, u32[]{:S(2)}, u32[]{:S(2)}) %collective-permute-start.9) | collective-permute-done | bytes 147488 | tf_op jit(solution)/shard_map/ppermute | solution.py:291
  93.6 1.6 collective-permute-start.10
  95.2 1.4 collective-permute-done.6
  96.6 0.2 collective-permute-start.7
  96.8 4.8 %collective-permute-done.10 = bf16[2,4,48,384]{3,2,1,0:T(8,128)(2,1)S(1)} collective-permute-done((bf16[2,4,48,384]{3,2,1,0:T(8,128)(2,1)S(1)}, bf16[2,4,48,384]{3,2,1,0:T(8,128)(2,1)S(1)}, u32[]{:S(2)}, u32[]{:S(2)}) %collective-permute-start.10) | collective-permute-done | bytes 294944 | tf_op jit(solution)/shard_map/ppermute | solution.py:291
  101.7 0.1 pad_maximum_fusion.1.refs_6_
  101.8 0.1 collective-permute-start.11
  101.8 1.6 collective-permute-done.7
  103.4 0.1 pad_maximum_fusion.refs_4_
  103.5 0.0 copy-start.1
  103.5 0.1 collective-permute-start.8
  103.6 1.4 copy.19
  105.1 0.1 reshape.28
  105.2 0.6 copy.21.mask_ref
  105.8 0.8 copy-done.3
  106.6 0.2 copy-done.4
  106.9 10.8 %attend.3 = (bf16[3,96,256]{2,1,0:T(8,128)(2,1)}, bf16[3,96,256]{2,1,0:T(8,128)(2,1)}, bf16[3,96,256]{2,1,0:T(8,128)(2,1)}, bf16[3,96,256]{2,1,0:T(8,128)(2,1)}) custom-call(s32[3]{0:T(128)} %pad_add_fusion.mine_ref, f32[1,256]{1,0:T(1,128)} %bitcast.21, bf16[256,1024]{1,0:T(8,128)(2,1)} %kernel_ref.5, bf16[8,1,384]{2,1,0:T(2,128)(2,1)} %copy.21.mask_ref, ...), custom_call_target="tpu_custom_call" | custom-call | tf_op jit(solution)/shard_map/attend/pallas_call | solution.py:266
  117.7 1.3 collective-permute-start.12
  119.0 1.5 collective-permute-start.13
  120.5 1.7 %collective-permute-start.14 = (bf16[3,96,256]{2,1,0:T(8,128)(2,1)}, bf16[3,96,256]{2,1,0:T(8,128)(2,1)S(1)}, u32[]{:S(2)}, u32[]{:S(2)}) collective-permute-start(bf16[3,96,256]{2,1,0:T(8,128)(2,1)} %get-tuple-element.41), channel_id=1, source_target_pairs={{0,3},{1,2},{2,1},{3,0},{4,7},{5,6},{6,5},{7,4},{8,11},{9,10},{10,... | collective-permute-start | bytes 442376 | tf_op jit(solution)/shard_map/ppermute | solution.py:294
  122.2 11.0 %attend.4 = (bf16[3,96,256]{2,1,0:T(8,128)(2,1)}, bf16[3,96,256]{2,1,0:T(8,128)(2,1)}, bf16[3,96,256]{2,1,0:T(8,128)(2,1)}, bf16[3,96,256]{2,1,0:T(8,128)(2,1)}) custom-call(s32[3]{0:T(128)} %pad_add_fusion.mine_ref, f32[1,256]{1,0:T(1,128)} %bitcast.22, bf16[256,1024]{1,0:T(8,128)(2,1)} %kernel_ref.5, bf16[8,1,384]{2,1,0:T(2,128)(2,1)} %copy.21.mask_ref, ...), custom_call_target="tpu_custom_call" | custom-call | tf_op jit(solution)/shard_map/attend/pallas_call | solution.py:266
  133.2 0.4 collective-permute-start.15
  133.6 2.4 %collective-permute-start.16 = (bf16[3,96,256]{2,1,0:T(8,128)(2,1)}, bf16[3,96,256]{2,1,0:T(8,128)(2,1)S(1)}, u32[]{:S(2)}, u32[]{:S(2)}) collective-permute-start(bf16[3,96,256]{2,1,0:T(8,128)(2,1)} %get-tuple-element.48), channel_id=1, source_target_pairs={{0,2},{1,3},{2,0},{3,1},{4,6},{5,7},{6,4},{7,5},{8,10},{9,11},{10,... | collective-permute-start | bytes 442376 | tf_op jit(solution)/shard_map/ppermute | solution.py:294
  136.0 0.0 collective-permute-done.12
  136.0 1.7 %collective-permute-start.17 = (bf16[3,96,256]{2,1,0:T(8,128)(2,1)}, bf16[3,96,256]{2,1,0:T(8,128)(2,1)S(1)}, u32[]{:S(2)}, u32[]{:S(2)}) collective-permute-start(bf16[3,96,256]{2,1,0:T(8,128)(2,1)} %get-tuple-element.49), channel_id=1, source_target_pairs={{0,3},{1,2},{2,1},{3,0},{4,7},{5,6},{6,5},{7,4},{8,11},{9,10},{10,... | collective-permute-start | bytes 442376 | tf_op jit(solution)/shard_map/ppermute | solution.py:294
  137.7 0.6 copy.23.mask_ref
  138.3 8.2 %attend.5 = (bf16[2,96,256]{2,1,0:T(8,128)(2,1)}, bf16[2,96,256]{2,1,0:T(8,128)(2,1)}, bf16[2,96,256]{2,1,0:T(8,128)(2,1)}, bf16[2,96,256]{2,1,0:T(8,128)(2,1)}) custom-call(s32[3]{0:T(128)} %pad_add_fusion.mine_ref, f32[1,256]{1,0:T(1,128)} %bitcast.23, bf16[256,1024]{1,0:T(8,128)(2,1)} %kernel_ref.5, bf16[8,1,384]{2,1,0:T(2,128)(2,1)} %copy.23.mask_ref, ...), custom_call_target="tpu_custom_call" | custom-call | tf_op jit(solution)/shard_map/attend/pallas_call | solution.py:266
  146.5 0.1 collective-permute-start.18
  146.6 2.7 %collective-permute-start.19 = (bf16[2,96,256]{2,1,0:T(8,128)(2,1)}, bf16[2,96,256]{2,1,0:T(8,128)(2,1)S(1)}, u32[]{:S(2)}, u32[]{:S(2)}) collective-permute-start(bf16[2,96,256]{2,1,0:T(8,128)(2,1)} %get-tuple-element.53), channel_id=1, source_target_pairs={{0,2},{1,3},{2,0},{3,1},{4,6},{5,7},{6,4},{7,5},{8,10},{9,11},{10,... | collective-permute-start | bytes 294920 | tf_op jit(solution)/shard_map/ppermute | solution.py:294
  149.3 0.2 broadcast_in_dim.9
  149.6 0.0 collective-permute-done.15
  149.6 1.7 %collective-permute-start.20 = (bf16[2,96,256]{2,1,0:T(8,128)(2,1)S(1)}, bf16[2,96,256]{2,1,0:T(8,128)(2,1)S(1)}, u32[]{:S(2)}, u32[]{:S(2)}) collective-permute-start(bf16[2,96,256]{2,1,0:T(8,128)(2,1)S(1)} %copy-done.13), channel_id=1, source_target_pairs={{0,3},{1,2},{2,1},{3,0},{4,7},{5,6},{6,5},{7,4},{8,11},{9,10},{10,... | collective-permute-start | bytes 294920 | tf_op jit(solution)/shard_map/ppermute | solution.py:294
  151.4 0.0 collective-permute-done.17
  151.5 0.1 collective-permute-done.18
  151.6 5.1 %collective-permute-done.19 = bf16[2,96,256]{2,1,0:T(8,128)(2,1)S(1)} collective-permute-done((bf16[2,96,256]{2,1,0:T(8,128)(2,1)}, bf16[2,96,256]{2,1,0:T(8,128)(2,1)S(1)}, u32[]{:S(2)}, u32[]{:S(2)}) %collective-permute-start.19) | collective-permute-done | bytes 98336 | tf_op jit(solution)/shard_map/ppermute | solution.py:294
  156.7 0.0 collective-permute-done.20
  156.7 0.0 copy-start.8
  156.7 1.1 copy-done.8
  (52 shorter events, 0.4 us)
Async XLA Ops:
  7.2 45.3 %all-gather.3.cloned.1.call-start = ((), (), s32[]{:S(2)}) async-start(), calls=%async_computation.1 | async-start | bytes 2433024 | tf_op jit(solution)/shard_map/all_gather | solution.py:337
  11.4 27.7 %copy-start.2 = (bf16[32,96,256]{2,1,0:T(8,128)(2,1)S(1)}, bf16[32,96,256]{2,1,0:T(8,128)(2,1)}, u32[]{:S(2)}) copy-start(bf16[32,96,256]{2,1,0:T(8,128)(2,1)} %x_ref.1) | copy-start | bytes 4718596
  34.9 17.5 %all-to-all-start = ((bf16[8,13,32,128]{3,2,1,0:T(8,128)(2,1)}), bf16[8,13,32,128]{3,2,1,0:T(8,128)(2,1)}, u32[]{:S(2)}, u32[]{:S(2)}) async-start(bf16[8,13,32,128]{3,2,1,0:T(8,128)(2,1)} %all_gather.9), calls=%async_computation | async-start | bytes 1703936 | tf_op jit(solution)/shard_map/all_to_all | solution.py:339
  39.1 5.4 %copy-start.12 = (s32[384]{0:T(512)S(1)}, s32[384]{0:T(512)}, u32[]{:S(2)}) copy-start(s32[384]{0:T(512)} %param.15) | copy-start | bytes 4612
  40.2 33.9 %collective-permute-start = (bf16[8,96,256]{2,1,0:T(8,128)(2,1)}, bf16[8,96,256]{2,1,0:T(8,128)(2,1)S(1)}, u32[]{:S(2)}, u32[]{:S(2)}) collective-permute-start(bf16[8,96,256]{2,1,0:T(8,128)(2,1)} %get-tuple-element.58), channel_id=1, source_target_pairs={{0,1},{1,0},{2,3},{3,2},{4,5},{5,4},{6,7},{7,6},{8,9},{9,8},{10,11... | collective-permute-start | bytes 1179656 | tf_op jit(solution)/shard_map/ppermute | solution.py:294
  40.2 33.9 %collective-permute-start.1 = (bf16[8,96,256]{2,1,0:T(8,128)(2,1)S(1)}, bf16[8,96,256]{2,1,0:T(8,128)(2,1)S(1)}, u32[]{:S(2)}, u32[]{:S(2)}) collective-permute-start(bf16[8,96,256]{2,1,0:T(8,128)(2,1)S(1)} %get-tuple-element.57), channel_id=1, source_target_pairs={{0,2},{1,3},{2,0},{3,1},{4,6},{5,7},{6,4},{7,5},{8,10},{9,11},{10,... | collective-permute-start | bytes 1179656 | tf_op jit(solution)/shard_map/ppermute | solution.py:294
  42.6 31.5 %collective-permute-start.2 = (bf16[8,96,256]{2,1,0:T(8,128)(2,1)S(1)}, bf16[8,96,256]{2,1,0:T(8,128)(2,1)S(1)}, u32[]{:S(2)}, u32[]{:S(2)}) collective-permute-start(bf16[8,96,256]{2,1,0:T(8,128)(2,1)S(1)} %get-tuple-element.56), channel_id=1, source_target_pairs={{0,3},{1,2},{2,1},{3,0},{4,7},{5,6},{6,5},{7,4},{8,11},{9,10},{10,... | collective-permute-start | bytes 1179656 | tf_op jit(solution)/shard_map/ppermute | solution.py:294
  74.1 27.6 %copy-start.5 = (bf16[8,96,256]{2,1,0:T(8,128)(2,1)}, bf16[8,96,256]{2,1,0:T(8,128)(2,1)S(1)}, u32[]{:S(2)}) copy-start(bf16[8,96,256]{2,1,0:T(8,128)(2,1)S(1)} %collective-permute-done.refs_1_) | copy-start | bytes 1179652
  74.1 27.6 %copy-start.6 = (bf16[8,96,256]{2,1,0:T(8,128)(2,1)}, bf16[8,96,256]{2,1,0:T(8,128)(2,1)S(1)}, u32[]{:S(2)}) copy-start(bf16[8,96,256]{2,1,0:T(8,128)(2,1)S(1)} %collective-permute-done.1.refs_2_) | copy-start | bytes 1179652
  74.1 27.6 %copy-start.7 = (bf16[8,96,256]{2,1,0:T(8,128)(2,1)}, bf16[8,96,256]{2,1,0:T(8,128)(2,1)S(1)}, u32[]{:S(2)}) copy-start(bf16[8,96,256]{2,1,0:T(8,128)(2,1)S(1)} %collective-permute-done.2.refs_3_) | copy-start | bytes 1179652
  74.1 7.8 %collective-permute-start.3 = (bf16[8,48,96]{2,1,0:T(8,128)(2,1)}, bf16[8,48,96]{2,1,0:T(8,128)(2,1)S(1)}, u32[]{:S(2)}, u32[]{:S(2)}) collective-permute-start(bf16[8,48,96]{2,1,0:T(8,128)(2,1)} %get-tuple-element.37), channel_id=1, source_target_pairs={{0,1},{1,0},{2,3},{3,2},{4,5},{5,4},{6,7},{7,6},{8,9},{9,8},{10,11... | collective-permute-start | bytes 221192 | tf_op jit(solution)/shard_map/ppermute | solution.py:294
  78.3 9.9 %collective-permute-start.4 = (bf16[8,48,96]{2,1,0:T(8,128)(2,1)}, bf16[8,48,96]{2,1,0:T(8,128)(2,1)S(1)}, u32[]{:S(2)}, u32[]{:S(2)}) collective-permute-start(bf16[8,48,96]{2,1,0:T(8,128)(2,1)} %get-tuple-element.37), channel_id=1, source_target_pairs={{0,2},{1,3},{2,0},{3,1},{4,6},{5,7},{6,4},{7,5},{8,10},{9,11},{10,... | collective-permute-start | bytes 221192 | tf_op jit(solution)/shard_map/ppermute | solution.py:294
  78.9 9.3 %collective-permute-start.5 = (bf16[8,48,96]{2,1,0:T(8,128)(2,1)}, bf16[8,48,96]{2,1,0:T(8,128)(2,1)S(1)}, u32[]{:S(2)}, u32[]{:S(2)}) collective-permute-start(bf16[8,48,96]{2,1,0:T(8,128)(2,1)} %get-tuple-element.37), channel_id=1, source_target_pairs={{0,3},{1,2},{2,1},{3,0},{4,7},{5,6},{6,5},{7,4},{8,11},{9,10},{10,... | collective-permute-start | bytes 221192 | tf_op jit(solution)/shard_map/ppermute | solution.py:294
  88.4 5.2 %collective-permute-start.9 = (bf16[1,4,48,384]{3,2,1,0:T(8,128)(2,1)S(1)}, bf16[1,4,48,384]{3,2,1,0:T(8,128)(2,1)S(1)}, u32[]{:S(2)}, u32[]{:S(2)}) collective-permute-start(bf16[1,4,48,384]{3,2,1,0:T(8,128)(2,1)S(1)} %maximum_bitcast_fusion.1), channel_id=1, source_target_pairs={{0,16},{4,20},{8,24},{12,28},{16,0},{20,4},{24,8},{28,12},{1,17},{... | collective-permute-start | bytes 442376 | tf_op jit(solution)/shard_map/ppermute | solution.py:291
  90.1 6.5 %collective-permute-start.6 = (bf16[1,4,48,384]{3,2,1,0:T(8,128)(2,1)S(1)}, bf16[1,4,48,384]{3,2,1,0:T(8,128)(2,1)S(1)}, u32[]{:S(2)}, u32[]{:S(2)}) collective-permute-start(bf16[1,4,48,384]{3,2,1,0:T(8,128)(2,1)S(1)} %maximum_bitcast_fusion), channel_id=1, source_target_pairs={{0,8},{4,12},{8,0},{12,4},{16,24},{20,28},{24,16},{28,20},{1,9},{5... | collective-permute-start | bytes 442376 | tf_op jit(solution)/shard_map/ppermute | solution.py:291
  93.6 8.0 %collective-permute-start.10 = (bf16[2,4,48,384]{3,2,1,0:T(8,128)(2,1)S(1)}, bf16[2,4,48,384]{3,2,1,0:T(8,128)(2,1)S(1)}, u32[]{:S(2)}, u32[]{:S(2)}) collective-permute-start(bf16[2,4,48,384]{3,2,1,0:T(8,128)(2,1)S(1)} %pad_maximum_fusion.3), channel_id=1, source_target_pairs={{0,8},{4,12},{8,0},{12,4},{16,24},{20,28},{24,16},{28,20},{1,9},{5... | collective-permute-start | bytes 884744 | tf_op jit(solution)/shard_map/ppermute | solution.py:291
  96.6 6.8 %collective-permute-start.7 = (bf16[2,4,48,384]{3,2,1,0:T(8,128)(2,1)S(1)}, bf16[2,4,48,384]{3,2,1,0:T(8,128)(2,1)S(1)}, u32[]{:S(2)}, u32[]{:S(2)}) collective-permute-start(bf16[2,4,48,384]{3,2,1,0:T(8,128)(2,1)S(1)} %pad_maximum_fusion.2), channel_id=1, source_target_pairs={{0,16},{4,20},{8,24},{12,28},{16,0},{20,4},{24,8},{28,12},{1,17},{... | collective-permute-start | bytes 884744 | tf_op jit(solution)/shard_map/ppermute | solution.py:291
  101.8 3.3 %copy-start = (bf16[4,4,48,384]{3,2,1,0:T(8,128)(2,1)}, bf16[4,4,48,384]{3,2,1,0:T(8,128)(2,1)S(1)}, u32[]{:S(2)}) copy-start(bf16[4,4,48,384]{3,2,1,0:T(8,128)(2,1)S(1)} %pad_maximum_fusion.1.refs_6_) | copy-start | bytes 1769476
  101.8 4.0 %collective-permute-start.11 = (bf16[4,4,48,384]{3,2,1,0:T(8,128)(2,1)S(1)}, bf16[4,4,48,384]{3,2,1,0:T(8,128)(2,1)S(1)}, u32[]{:S(2)}, u32[]{:S(2)}) collective-permute-start(bf16[4,4,48,384]{3,2,1,0:T(8,128)(2,1)S(1)} %pad_maximum_fusion.1.refs_6_), channel_id=1, source_target_pairs={{0,4},{4,0},{8,12},{12,8},{16,20},{20,16},{24,28},{28,24},{1,5},{5... | collective-permute-start | bytes 1769480 | tf_op jit(solution)/shard_map/ppermute | solution.py:291
  103.5 2.3 %copy-start.1 = (bf16[4,4,48,384]{3,2,1,0:T(8,128)(2,1)}, bf16[4,4,48,384]{3,2,1,0:T(8,128)(2,1)S(1)}, u32[]{:S(2)}) copy-start(bf16[4,4,48,384]{3,2,1,0:T(8,128)(2,1)S(1)} %pad_maximum_fusion.refs_4_) | copy-start | bytes 1769476
  103.5 2.3 %collective-permute-start.8 = (bf16[4,4,48,384]{3,2,1,0:T(8,128)(2,1)S(1)}, bf16[4,4,48,384]{3,2,1,0:T(8,128)(2,1)S(1)}, u32[]{:S(2)}, u32[]{:S(2)}) collective-permute-start(bf16[4,4,48,384]{3,2,1,0:T(8,128)(2,1)S(1)} %pad_maximum_fusion.refs_4_), channel_id=1, source_target_pairs={{0,4},{4,0},{8,12},{12,8},{16,20},{20,16},{24,28},{28,24},{1,5},{5... | collective-permute-start | bytes 1769480 | tf_op jit(solution)/shard_map/ppermute | solution.py:291
  105.8 0.8 copy-start.3
  105.8 1.0 copy-start.4
  117.7 18.3 %collective-permute-start.12 = (bf16[3,96,256]{2,1,0:T(8,128)(2,1)}, bf16[3,96,256]{2,1,0:T(8,128)(2,1)S(1)}, u32[]{:S(2)}, u32[]{:S(2)}) collective-permute-start(bf16[3,96,256]{2,1,0:T(8,128)(2,1)} %get-tuple-element.39), channel_id=1, source_target_pairs={{0,1},{1,0},{2,3},{3,2},{4,5},{5,4},{6,7},{7,6},{8,9},{9,8},{10,11... | collective-permute-start | bytes 442376 | tf_op jit(solution)/shard_map/ppermute | solution.py:294
  119.0 18.6 %collective-permute-start.13 = (bf16[3,96,256]{2,1,0:T(8,128)(2,1)}, bf16[3,96,256]{2,1,0:T(8,128)(2,1)S(1)}, u32[]{:S(2)}, u32[]{:S(2)}) collective-permute-start(bf16[3,96,256]{2,1,0:T(8,128)(2,1)} %get-tuple-element.40), channel_id=1, source_target_pairs={{0,2},{1,3},{2,0},{3,1},{4,6},{5,7},{6,4},{7,5},{8,10},{9,11},{10,... | collective-permute-start | bytes 442376 | tf_op jit(solution)/shard_map/ppermute | solution.py:294
  120.5 17.2 %collective-permute-start.14 = (bf16[3,96,256]{2,1,0:T(8,128)(2,1)}, bf16[3,96,256]{2,1,0:T(8,128)(2,1)S(1)}, u32[]{:S(2)}, u32[]{:S(2)}) collective-permute-start(bf16[3,96,256]{2,1,0:T(8,128)(2,1)} %get-tuple-element.41), channel_id=1, source_target_pairs={{0,3},{1,2},{2,1},{3,0},{4,7},{5,6},{6,5},{7,4},{8,11},{9,10},{10,... | collective-permute-start | bytes 442376 | tf_op jit(solution)/shard_map/ppermute | solution.py:294
  133.2 16.4 %collective-permute-start.15 = (bf16[3,96,256]{2,1,0:T(8,128)(2,1)}, bf16[3,96,256]{2,1,0:T(8,128)(2,1)S(1)}, u32[]{:S(2)}, u32[]{:S(2)}) collective-permute-start(bf16[3,96,256]{2,1,0:T(8,128)(2,1)} %get-tuple-element.47), channel_id=1, source_target_pairs={{0,1},{1,0},{2,3},{3,2},{4,5},{5,4},{6,7},{7,6},{8,9},{9,8},{10,11... | collective-permute-start | bytes 442376 | tf_op jit(solution)/shard_map/ppermute | solution.py:294
  133.6 17.8 %collective-permute-start.16 = (bf16[3,96,256]{2,1,0:T(8,128)(2,1)}, bf16[3,96,256]{2,1,0:T(8,128)(2,1)S(1)}, u32[]{:S(2)}, u32[]{:S(2)}) collective-permute-start(bf16[3,96,256]{2,1,0:T(8,128)(2,1)} %get-tuple-element.48), channel_id=1, source_target_pairs={{0,2},{1,3},{2,0},{3,1},{4,6},{5,7},{6,4},{7,5},{8,10},{9,11},{10,... | collective-permute-start | bytes 442376 | tf_op jit(solution)/shard_map/ppermute | solution.py:294
  136.0 15.5 %collective-permute-start.17 = (bf16[3,96,256]{2,1,0:T(8,128)(2,1)}, bf16[3,96,256]{2,1,0:T(8,128)(2,1)S(1)}, u32[]{:S(2)}, u32[]{:S(2)}) collective-permute-start(bf16[3,96,256]{2,1,0:T(8,128)(2,1)} %get-tuple-element.49), channel_id=1, source_target_pairs={{0,3},{1,2},{2,1},{3,0},{4,7},{5,6},{6,5},{7,4},{8,11},{9,10},{10,... | collective-permute-start | bytes 442376 | tf_op jit(solution)/shard_map/ppermute | solution.py:294
  146.5 3.0 %copy-start.9 = (bf16[3,96,256]{2,1,0:T(8,128)(2,1)S(1)}, bf16[3,96,256]{2,1,0:T(8,128)(2,1)}, u32[]{:S(2)}) copy-start(bf16[3,96,256]{2,1,0:T(8,128)(2,1)} %get-tuple-element.42) | copy-start | bytes 442372
  146.5 3.1 %copy-start.10 = (bf16[3,96,256]{2,1,0:T(8,128)(2,1)S(1)}, bf16[3,96,256]{2,1,0:T(8,128)(2,1)}, u32[]{:S(2)}) copy-start(bf16[3,96,256]{2,1,0:T(8,128)(2,1)} %get-tuple-element.46) | copy-start | bytes 442372
  146.5 3.1 %copy-start.13 = (bf16[2,96,256]{2,1,0:T(8,128)(2,1)S(1)}, bf16[2,96,256]{2,1,0:T(8,128)(2,1)}, u32[]{:S(2)}) copy-start(bf16[2,96,256]{2,1,0:T(8,128)(2,1)} %get-tuple-element.54) | copy-start | bytes 294916
  146.5 5.1 %collective-permute-start.18 = (bf16[2,96,256]{2,1,0:T(8,128)(2,1)}, bf16[2,96,256]{2,1,0:T(8,128)(2,1)S(1)}, u32[]{:S(2)}, u32[]{:S(2)}) collective-permute-start(bf16[2,96,256]{2,1,0:T(8,128)(2,1)} %get-tuple-element.52), channel_id=1, source_target_pairs={{0,1},{1,0},{2,3},{3,2},{4,5},{5,4},{6,7},{7,6},{8,9},{9,8},{10,11... | collective-permute-start | bytes 294920 | tf_op jit(solution)/shard_map/ppermute | solution.py:294
  146.6 10.1 %collective-permute-start.19 = (bf16[2,96,256]{2,1,0:T(8,128)(2,1)}, bf16[2,96,256]{2,1,0:T(8,128)(2,1)S(1)}, u32[]{:S(2)}, u32[]{:S(2)}) collective-permute-start(bf16[2,96,256]{2,1,0:T(8,128)(2,1)} %get-tuple-element.53), channel_id=1, source_target_pairs={{0,2},{1,3},{2,0},{3,1},{4,6},{5,7},{6,4},{7,5},{8,10},{9,11},{10,... | collective-permute-start | bytes 294920 | tf_op jit(solution)/shard_map/ppermute | solution.py:294
  149.5 2.0 %copy-start.11 = (bf16[2,96,256]{2,1,0:T(8,128)(2,1)S(1)}, bf16[2,96,256]{2,1,0:T(8,128)(2,1)}, u32[]{:S(2)}) copy-start(bf16[2,96,256]{2,1,0:T(8,128)(2,1)} %get-tuple-element.51) | copy-start | bytes 294916
  149.6 7.1 %collective-permute-start.20 = (bf16[2,96,256]{2,1,0:T(8,128)(2,1)S(1)}, bf16[2,96,256]{2,1,0:T(8,128)(2,1)S(1)}, u32[]{:S(2)}, u32[]{:S(2)}) collective-permute-start(bf16[2,96,256]{2,1,0:T(8,128)(2,1)S(1)} %copy-done.13), channel_id=1, source_target_pairs={{0,3},{1,2},{2,1},{3,0},{4,7},{5,6},{6,5},{7,4},{8,11},{9,10},{10,... | collective-permute-start | bytes 294920 | tf_op jit(solution)/shard_map/ppermute | solution.py:294
  156.7 1.1 copy-start.8
Sparse Core Ops, SparseCore 0:
  11.6 30.8 all-gather.2

commit v3 on v2

--- a/solution.py
+++ b/solution.py
@@ -142,21 +142,22 @@
         ).astype(bf16)
         row_scale = scale[pl.ds(pl.multiple_of(step * block, 8), block), :]
         biases = []
-        for first in range(0, block, 2):
-            both = [
-                jnp.concatenate(
-                    [outer[i * width : (i + 1) * width, b * LANES : (b + 1) * LANES] for b in range(width)], 0
-                )
-                for i in (first, first + 1)
-            ]
-            update = jnp.dot(w_ref[...], jnp.concatenate(both, 1), preferred_element_type=f32)
-            for k, i in enumerate((first, first + 1)):
-                fresh = duo_ref[i] + (update[:, k * LANES : (k + 1) * LANES] * row_scale[i : i + 1, :]).T[:residues]
-                out_ref[i] = fresh
-                pair_input = (standardize(fresh) * gain_ref[...]).astype(bf16)
-                biases.append(
-                    lax.dot_general(logit_ref[...], pair_input, ROWS_BY_ROWS, preferred_element_type=f32)
-                )
+        every = [
+            jnp.concatenate(
+                [outer[i * width : (i + 1) * width, b * LANES : (b + 1) * LANES] for b in range(width)], 0
+            )
+            for i in range(block)
+        ]
+        update = jnp.dot(w_ref[...], jnp.concatenate(every, 1), preferred_element_type=f32)
+        fresh = []
+        for i in range(block):
+            mine = (update[:, i * LANES : (i + 1) * LANES] * row_scale[i : i + 1, :]).T[:residues]
+            fresh.append(duo_ref[i] + mine)
+            out_ref[i] = fresh[-1]
+        pair_input = (standardize(jnp.concatenate(fresh, 0)) * gain_ref[...]).astype(bf16)
+        for i in range(block):
+            own = pair_input[i * residues : (i + 1) * residues]
+            biases.append(lax.dot_general(logit_ref[...], own, ROWS_BY_ROWS, preferred_element_type=f32))
         bias_ref[...] = jnp.swapaxes(jnp.stack(biases, 0), 0, 1).astype(bf16)
 
     operands = [
@@ -231,12 +232,11 @@
             jnp.dot(narrow, kernel_ref[:, n * inner : (n + 1) * inner], preferred_element_type=f32).astype(bf16)
             for n in (0, 2, 3)
         ]
-        gated = []
-        for first_lane in range(0, inner, LANES):
-            span = slice(first_lane, first_lane + LANES)
-            key = keys[span, :]
-            value = all_values[:, span]
-            alone, values = [], []
+        spans = [slice(lane, lane + LANES) for lane in range(0, inner, LANES)]
+        scores, values = [], []
+        for span in spans:
+            key, value = keys[span, :], all_values[:, span]
+            alone = []
             for h in range(group):
                 mine_rows = key[h * depth : (h + 1) * depth]
                 alone.append(jnp.concatenate([mine_rows if n == h else zero for n in range(group)], 0))
@@ -246,18 +246,21 @@
                         [jnp.where(here, value, jnp.zeros_like(value)), here.astype(f32).astype(bf16)], 1
                     )
                 )
-            scores = jnp.dot(queries[:, span], jnp.concatenate(alone, 1), preferred_element_type=f32)
-            weights = []
-            for h in range(group):
-                own = scores[:, h * total : (h + 1) * total] * scale
-                own = own + bias[first_lane // depth + h] + row_mask
-                highest = jnp.max(own, axis=1, keepdims=True)
-                weights.append(jnp.exp2(own - highest).astype(bf16))
+            scores.append(jnp.dot(queries[:, span], jnp.concatenate(alone, 1), preferred_element_type=f32))
+        weights = []
+        for h in range(heads):
+            at = h % group * total
+            own = scores[h // group][:, at : at + total] * scale + bias[h] + row_mask
+            highest = jnp.max(own, axis=1, keepdims=True)
+            weights.append(jnp.exp2(own - highest).astype(bf16))
+        gated = []
+        for n, span in enumerate(spans):
+            here = slice(n * group, (n + 1) * group)
             mixed = jnp.dot(
-                jnp.concatenate(weights, 1), jnp.concatenate(values, 0), preferred_element_type=f32
+                jnp.concatenate(weights[here], 1), jnp.concatenate(values[here], 0), preferred_element_type=f32
             )
-            gate = gates[:, span].astype(f32)
-            gated.append((mixed[:, :LANES] / mixed[:, LANES:] * jax.nn.sigmoid(gate)).astype(bf16))
+            gate = jax.nn.sigmoid(gates[:, span].astype(f32))
+            gated.append((mixed[:, :LANES] / mixed[:, LANES:] * gate).astype(bf16))
         change = jnp.dot(jnp.concatenate(gated, 1), closing_ref[...], preferred_element_type=f32)
         for k in range(cols):
             own = x[k * residues : (k + 1) * residues] + change[k * residues : (k + 1) * residues]
@@ -293,7 +296,7 @@
     def by_col(x, k):
         return lax.ppermute(x, "col", [(c, c ^ k) for c in range(n_col)])
 
-    def gather_rows(first, second):
+    def gather_rows(first, second, others):
         bits = []
         k = 2
         while k < n_row:
@@ -308,9 +311,12 @@
                     (jnp.concatenate([array, by_row(array, k)], 0), offsets + [o ^ k for o in offsets])
                 )
             held = got
-        return [
-            [(array, offsets), (by_row(array, 1), [o ^ 1 for o in offsets])] for array, offsets in held
+        arrays, others = lax.optimization_barrier(([array for array, offsets in held], others))
+        sides = [
+            [(array, offsets), (by_row(array, 1), [o ^ 1 for o in offsets])]
+            for array, (_, offsets) in zip(arrays, held)
         ]
+        return (*sides, others)
 
     def shards(
         msa,
@@ -338,14 +344,16 @@
         spread = lax.all_gather(left, "col", axis=0, tiled=True)
         left_rows = lax.all_to_all(spread, "row", 0, 0, tiled=True)
 
-        msa_late, spread_late = lax.optimization_barrier((msa, spread))
-        x = [lax.dynamic_slice_in_dim(msa_late, (c ^ k) * share, share, 0) for k in range(n_col)]
-        x = [by_col(piece, k) if k else piece for k, piece in enumerate(x)]
+        x = [lax.dynamic_slice_in_dim(msa, (c ^ k) * share, share, 0) for k in range(n_col)]
+        x, spread_late = lax.optimization_barrier((x, spread))
+        soon = max(n_col - 1, 2)
+        x = [by_col(piece, k) if 0 < k < soon else piece for k, piece in enumerate(x)]
         mask = lax.dynamic_slice_in_dim(spread_late[:, -1, :, :rows], c * share, share, 1)
         mask = mask.reshape(n_col, halves, share, rows)
         mask = jnp.stack([lax.dynamic_index_in_dim(mask, c ^ k, 0, keepdims=False) for k in range(n_col)])
         rows_mask = mask.transpose(2, 0, 1, 3).reshape(share, 1, residues * n_col)
 
+        left_rows, rows_mask = lax.optimization_barrier((left_rows, rows_mask))
         duo_after_averaging, tile = pair_tile(
             mine,
             left_rows,
@@ -356,11 +364,13 @@
             duo_gain,
             logit_kernel,
         )
-        tile, x[1:] = lax.optimization_barrier((tile, x[1:]))
+        tile, x[1:soon] = lax.optimization_barrier((tile, x[1:soon]))
         tiles = [tile] + [by_col(tile, k) for k in range(1, n_col)]
         cut = tile.shape[0] // 2
-        low, high = gather_rows(
-            jnp.concatenate([t[:cut] for t in tiles], 2), jnp.concatenate([t[cut:] for t in tiles], 2)
+        tiles, x[soon:] = lax.optimization_barrier((tiles, x[soon:]))
+        x[soon:] = [by_col(piece, k) for k, piece in enumerate(x[soon:], soon)]
+        low, high, x[soon:] = gather_rows(
+            jnp.concatenate([t[:cut] for t in tiles], 2), jnp.concatenate([t[cut:] for t in tiles], 2), x[soon:]
         )
         sent = []
         first = 0

time: 165 us -> 161 us (0.976)
  Pallas kernels: 56 us -> 45.1 us
  starting transfers between devices: 33.7 us -> 39.8 us
    pallas_call x1, Pallas kernels: 21.7 us -> 11.8 us  [pair_tile(): pl.pallas_call(body, grid=(rows // block,), in_specs=[SMEM, *specs], out_...]
    ppermute x15, starting transfers between devices: 24.4 us -> 27.9 us  [by_col(): return lax.ppermute(x, 'col', [(c, c ^ k) for c in range(n_col)])]
    ppermute x6, waiting for transfers between devices: 9.72 us -> 6.63 us  [by_row(): return lax.ppermute(x, 'row', [(r, r ^ k) for r in range(n_row)])]
    ppermute x15, waiting for transfers between devices: 11.8 us -> 14.9 us  [by_col(): return lax.ppermute(x, 'col', [(c, c ^ k) for c in range(n_col)])]
    ppermute x6, starting transfers between devices: 5.05 us -> 7.6 us  [by_row(): return lax.ppermute(x, 'row', [(r, r ^ k) for r in range(n_row)])]
  transfers between devices with their start and end apart: 23 -> 23, of which waited for: 9 -> 11; matrix products, arithmetic and copies ran while one was open for 4% -> 3% of each run, Pallas kernels for 25% -> 19%
where the time goes in v3:
time: 161 us; the launch traced here: 160 us
  Pallas kernels  45.1 us (28%)
  starting transfers between devices  39.8 us (25%)
  waiting for transfers between devices  28.9 us (18%)
  blocking collectives  23.4 us (15%)
  between operations  14.5 us (9%)
  local copies, waits for them, and re-layouts  7.21 us (4%)
    pallas_call x3, Pallas kernels, attend(): pl.pallas_call(body, grid=(count,), in_specs=[SMEM, whole(gain), whole(ke...  29.1 us
    ppermute x15, starting transfers between devices, by_col(): return lax.ppermute(x, 'col', [(c, c ^ k) for c in range(n_col)])  27.9 us
    all_gather x1, blocking collectives, shards(): spread = lax.all_gather(left, 'col', axis=0, tiled=True)  23.4 us
    ppermute x15, waiting for transfers between devices, by_col(): return lax.ppermute(x, 'col', [(c, c ^ k) for c in range(n_col)])  14.9 us
    pallas_call x1, Pallas kernels, pair_tile(): pl.pallas_call(body, grid=(rows // block,), in_specs=[SMEM, *specs], out_...  11.8 us
    ppermute x6, starting transfers between devices, by_row(): return lax.ppermute(x, 'row', [(r, r ^ k) for r in range(n_row)])  7.6 us
    all_to_all x1, waiting for transfers between devices, shards(): left_rows = lax.all_to_all(spread, 'row', 0, 0, tiled=True)  7.36 us
    ppermute x6, waiting for transfers between devices, by_row(): return lax.ppermute(x, 'row', [(r, r ^ k) for r in range(n_row)])  6.63 us
  transfers between devices with their start and end apart: 23, of which 11 were waited for; matrix products, arithmetic and copies ran while one was open for 3% of the time, Pallas kernels for 19%

profile of v3, /device:TPU:0, one launch (start us, length us, event | category | flops | bytes accessed | tf_op | source)
XLA Modules:
  0.0 160.1 jit_solution(13092856461935761757)
XLA Ops:
  7.2 0.0 all-gather.3.cloned.1.call-start
  7.2 4.2 %opm_inputs.1 = (bf16[2,13,32,128]{3,2,1,0:T(8,128)(2,1)}, bf16[33,32,96]{2,1,0:T(8,128)(2,1)}) custom-call(bf16[32,96,256]{2,1,0:T(8,128)(2,1)} %x_ref.1, s32[32,96]{1,0:T(8,128)} %mask_ref.1, f32[1,256]{1,0:T(1,128)} %bitcast.25, bf16[32,256]{1,0:T(8,128)(2,1)} %bitcast.19, bf16[32,256]{1,0:T(8,128)(2,1)} %bitcast.20), custom_call_target="tpu_custom_call" | custom-call | tf_op jit(solution)/shard_map/opm_inputs/pallas_call | solution.py:82
  11.4 0.0 all-gather.3.cloned.1.call-update
  11.5 23.4 %all_gather.9 = bf16[8,13,32,128]{3,2,1,0:T(8,128)(2,1)} all-gather(bf16[2,13,32,128]{3,2,1,0:T(8,128)(2,1)} %get-tuple-element.41), channel_id=1, replica_groups=mesh['row'=8,'col'=4] {'col'}, dimensions={0}, use_global_device_ids=true | all-gather | bytes 1064960 | tf_op jit(solution)/shard_map/all_gather | solution.py:344
  34.9 4.2 %all-to-all-start = ((bf16[8,13,32,128]{3,2,1,0:T(8,128)(2,1)}), bf16[8,13,32,128]{3,2,1,0:T(8,128)(2,1)}, u32[]{:S(2)}, u32[]{:S(2)}) async-start(bf16[8,13,32,128]{3,2,1,0:T(8,128)(2,1)} %all_gather.9), calls=%async_computation | async-start | bytes 1703936 | tf_op jit(solution)/shard_map/all_to_all | solution.py:345
  39.1 0.9 constant_dynamic-slice_fusion.5
  40.0 0.0 collective-permute-start
  40.0 2.4 %collective-permute-start.1 = (bf16[8,96,256]{2,1,0:T(8,128)(2,1)S(1)}, bf16[8,96,256]{2,1,0:T(8,128)(2,1)S(1)}, u32[]{:S(2)}, u32[]{:S(2)}) collective-permute-start(bf16[8,96,256]{2,1,0:T(8,128)(2,1)S(1)} %get-tuple-element.49), channel_id=1, source_target_pairs={{0,2},{1,3},{2,0},{3,1},{4,6},{5,7},{6,4},{7,5},{8,10},{9,11},{10,... | collective-permute-start | bytes 1179656 | tf_op jit(solution)/shard_map/ppermute | solution.py:297
  42.4 1.2 copy.19
  43.8 0.1 reshape.28
  43.9 0.6 reshape.30.refs_1_
  44.5 0.6 pad_add_fusion.mine_ref
  45.1 7.4 %all-to-all-done.left_ref = bf16[8,13,32,128]{3,2,1,0:T(8,128)(2,1)} async-done(((bf16[8,13,32,128]{3,2,1,0:T(8,128)(2,1)}), bf16[8,13,32,128]{3,2,1,0:T(8,128)(2,1)}, u32[]{:S(2)}, u32[]{:S(2)}) %all-to-all-start) | async-done | bytes 852000 | tf_op jit(solution)/shard_map/all_to_all | solution.py:345
  52.4 11.8 %pair_tile.1 = (f32[48,96,128]{2,1,0:T(8,128)}, bf16[8,48,96]{2,1,0:T(8,128)(2,1)}) custom-call(s32[3]{0:T(128)} %pad_add_fusion.mine_ref, bf16[8,13,32,128]{3,2,1,0:T(8,128)(2,1)} %all-to-all-done.left_ref, bf16[8,33,32,96]{3,2,1,0:T(8,128)(2,1)} %bitcast.17, f32[48,96,128]{2,1,0:T(8,128)} %refs_0_.1, s32[1,384]{1,0:T(1,128)} %reshape.30.refs_1_, ...), custom_call_target="tpu_custom_call" | custom-call | tf_op jit(solution)/shard_map/pair_tile/pallas_call | solution.py:174
  64.2 0.0 collective-permute-done.refs_1_
  64.3 0.0 collective-permute-done.1.refs_2_
  64.3 0.2 collective-permute-start.2
  64.5 2.4 %collective-permute-start.3 = (bf16[8,48,96]{2,1,0:T(8,128)(2,1)}, bf16[8,48,96]{2,1,0:T(8,128)(2,1)S(1)}, u32[]{:S(2)}, u32[]{:S(2)}) collective-permute-start(bf16[8,48,96]{2,1,0:T(8,128)(2,1)} %get-tuple-element.54), channel_id=1, source_target_pairs={{0,2},{1,3},{2,0},{3,1},{4,6},{5,7},{6,4},{7,5},{8,10},{9,11},{10,... | collective-permute-start | bytes 221192 | tf_op jit(solution)/shard_map/ppermute | solution.py:297
  66.9 1.8 %collective-permute-start.4 = (bf16[8,48,96]{2,1,0:T(8,128)(2,1)}, bf16[8,48,96]{2,1,0:T(8,128)(2,1)S(1)}, u32[]{:S(2)}, u32[]{:S(2)}) collective-permute-start(bf16[8,48,96]{2,1,0:T(8,128)(2,1)} %get-tuple-element.54), channel_id=1, source_target_pairs={{0,3},{1,2},{2,1},{3,0},{4,7},{5,6},{6,5},{7,4},{8,11},{9,10},{10,... | collective-permute-start | bytes 221192 | tf_op jit(solution)/shard_map/ppermute | solution.py:297
  68.7 2.5 %collective-permute-done.2 = bf16[8,48,96]{2,1,0:T(8,128)(2,1)S(1)} collective-permute-done((bf16[8,48,96]{2,1,0:T(8,128)(2,1)}, bf16[8,48,96]{2,1,0:T(8,128)(2,1)S(1)}, u32[]{:S(2)}, u32[]{:S(2)}) %collective-permute-start.2) | collective-permute-done | bytes 73760 | tf_op jit(solution)/shard_map/ppermute | solution.py:297
  71.3 0.0 collective-permute-done.3
  71.3 2.4 %collective-permute-done.4 = bf16[8,48,96]{2,1,0:T(8,128)(2,1)S(1)} collective-permute-done((bf16[8,48,96]{2,1,0:T(8,128)(2,1)}, bf16[8,48,96]{2,1,0:T(8,128)(2,1)S(1)}, u32[]{:S(2)}, u32[]{:S(2)}) %collective-permute-start.4) | collective-permute-done | bytes 73760 | tf_op jit(solution)/shard_map/ppermute | solution.py:297
  73.6 0.8 fusion
  74.5 0.1 maximum_bitcast_fusion.1
  74.7 0.6 collective-permute-start.7
  75.3 0.1 maximum_bitcast_fusion
  75.4 2.4 %collective-permute-start.5 = (bf16[1,4,48,384]{3,2,1,0:T(8,128)(2,1)S(1)}, bf16[1,4,48,384]{3,2,1,0:T(8,128)(2,1)S(1)}, u32[]{:S(2)}, u32[]{:S(2)}) collective-permute-start(bf16[1,4,48,384]{3,2,1,0:T(8,128)(2,1)S(1)} %maximum_bitcast_fusion), channel_id=1, source_target_pairs={{0,8},{4,12},{8,0},{12,4},{16,24},{20,28},{24,16},{28,20},{1,9},{5... | collective-permute-start | bytes 442376 | tf_op jit(solution)/shard_map/ppermute | solution.py:294
  77.8 2.1 %collective-permute-done.7 = bf16[1,4,48,384]{3,2,1,0:T(8,128)(2,1)S(1)} collective-permute-done((bf16[1,4,48,384]{3,2,1,0:T(8,128)(2,1)S(1)}, bf16[1,4,48,384]{3,2,1,0:T(8,128)(2,1)S(1)}, u32[]{:S(2)}, u32[]{:S(2)}) %collective-permute-start.7) | collective-permute-done | bytes 147488 | tf_op jit(solution)/shard_map/ppermute | solution.py:294
  79.9 2.5 %collective-permute-start.8 = (bf16[2,4,48,384]{3,2,1,0:T(8,128)(2,1)S(1)}, bf16[2,4,48,384]{3,2,1,0:T(8,128)(2,1)S(1)}, u32[]{:S(2)}, u32[]{:S(2)}) collective-permute-start(bf16[2,4,48,384]{3,2,1,0:T(8,128)(2,1)S(1)} %pad_maximum_fusion.3), channel_id=1, source_target_pairs={{0,8},{4,12},{8,0},{12,4},{16,24},{20,28},{24,16},{28,20},{1,9},{5... | collective-permute-start | bytes 884744 | tf_op jit(solution)/shard_map/ppermute | solution.py:294
  82.4 0.0 collective-permute-done.5
  82.5 1.6 collective-permute-start.6
  84.0 2.3 %collective-permute-start.9 = (bf16[8,96,256]{2,1,0:T(8,128)(2,1)S(1)}, bf16[8,96,256]{2,1,0:T(8,128)(2,1)S(1)}, u32[]{:S(2)}, u32[]{:S(2)}) collective-permute-start(bf16[8,96,256]{2,1,0:T(8,128)(2,1)S(1)} %get-tuple-element.58), channel_id=1, source_target_pairs={{0,3},{1,2},{2,1},{3,0},{4,7},{5,6},{6,5},{7,4},{8,11},{9,10},{10,... | collective-permute-start | bytes 1179656 | tf_op jit(solution)/shard_map/ppermute | solution.py:297
  86.3 0.9 collective-permute-done.8
  87.2 0.1 pad_maximum_fusion.1.refs_6_
  87.3 1.9 %collective-permute-done.6 = bf16[2,4,48,384]{3,2,1,0:T(8,128)(2,1)S(1)} collective-permute-done((bf16[2,4,48,384]{3,2,1,0:T(8,128)(2,1)S(1)}, bf16[2,4,48,384]{3,2,1,0:T(8,128)(2,1)S(1)}, u32[]{:S(2)}, u32[]{:S(2)}) %collective-permute-start.6) | collective-permute-done | bytes 294944 | tf_op jit(solution)/shard_map/ppermute | solution.py:294
  89.3 0.1 pad_maximum_fusion.refs_4_
  89.3 0.0 copy-start.1
  89.3 4.4 %collective-permute-done.9.refs_3_ = bf16[8,96,256]{2,1,0:T(8,128)(2,1)S(1)} collective-permute-done((bf16[8,96,256]{2,1,0:T(8,128)(2,1)S(1)}, bf16[8,96,256]{2,1,0:T(8,128)(2,1)S(1)}, u32[]{:S(2)}, u32[]{:S(2)}) %collective-permute-start.9) | collective-permute-done | bytes 393248 | tf_op jit(solution)/shard_map/ppermute | solution.py:297
  93.7 0.0 collective-permute-start.10
  93.7 0.5 collective-permute-start.11
  94.2 0.6 copy.21.mask_ref
  94.8 0.9 collective-permute-done.10.refs_5_
  95.7 0.8 collective-permute-done.11.refs_7_
  96.6 0.8 copy-done.4
  97.4 10.5 %attend.3 = (bf16[3,96,256]{2,1,0:T(8,128)(2,1)}, bf16[3,96,256]{2,1,0:T(8,128)(2,1)}, bf16[3,96,256]{2,1,0:T(8,128)(2,1)}, bf16[3,96,256]{2,1,0:T(8,128)(2,1)}) custom-call(s32[3]{0:T(128)} %pad_add_fusion.mine_ref, f32[1,256]{1,0:T(1,128)} %bitcast.21, bf16[256,1024]{1,0:T(8,128)(2,1)} %kernel_ref.5, bf16[8,1,384]{2,1,0:T(2,128)(2,1)} %copy.21.mask_ref, ...), custom_call_target="tpu_custom_call" | custom-call | tf_op jit(solution)/shard_map/attend/pallas_call | solution.py:269
  107.9 7.4 %collective-permute-start.12 = (bf16[3,96,256]{2,1,0:T(8,128)(2,1)}, bf16[3,96,256]{2,1,0:T(8,128)(2,1)S(1)}, u32[]{:S(2)}, u32[]{:S(2)}) collective-permute-start(bf16[3,96,256]{2,1,0:T(8,128)(2,1)} %get-tuple-element.63), channel_id=1, source_target_pairs={{0,1},{1,0},{2,3},{3,2},{4,5},{5,4},{6,7},{7,6},{8,9},{9,8},{10,11... | collective-permute-start | bytes 442376 | tf_op jit(solution)/shard_map/ppermute | solution.py:297
  115.3 0.2 collective-permute-start.13
  115.5 2.2 %collective-permute-start.14 = (bf16[3,96,256]{2,1,0:T(8,128)(2,1)}, bf16[3,96,256]{2,1,0:T(8,128)(2,1)S(1)}, u32[]{:S(2)}, u32[]{:S(2)}) collective-permute-start(bf16[3,96,256]{2,1,0:T(8,128)(2,1)} %get-tuple-element.65), channel_id=1, source_target_pairs={{0,3},{1,2},{2,1},{3,0},{4,7},{5,6},{6,5},{7,4},{8,11},{9,10},{10,... | collective-permute-start | bytes 442376 | tf_op jit(solution)/shard_map/ppermute | solution.py:297
  117.7 10.5 %attend.4 = (bf16[3,96,256]{2,1,0:T(8,128)(2,1)}, bf16[3,96,256]{2,1,0:T(8,128)(2,1)}, bf16[3,96,256]{2,1,0:T(8,128)(2,1)}, bf16[3,96,256]{2,1,0:T(8,128)(2,1)}) custom-call(s32[3]{0:T(128)} %pad_add_fusion.mine_ref, f32[1,256]{1,0:T(1,128)} %bitcast.22, bf16[256,1024]{1,0:T(8,128)(2,1)} %kernel_ref.5, bf16[8,1,384]{2,1,0:T(2,128)(2,1)} %copy.21.mask_ref, ...), custom_call_target="tpu_custom_call" | custom-call | tf_op jit(solution)/shard_map/attend/pallas_call | solution.py:269
  128.2 1.1 collective-permute-start.15
  129.3 1.1 collective-permute-start.16
  130.4 2.2 %collective-permute-start.17 = (bf16[3,96,256]{2,1,0:T(8,128)(2,1)}, bf16[3,96,256]{2,1,0:T(8,128)(2,1)S(1)}, u32[]{:S(2)}, u32[]{:S(2)}) collective-permute-start(bf16[3,96,256]{2,1,0:T(8,128)(2,1)} %get-tuple-element.73), channel_id=1, source_target_pairs={{0,3},{1,2},{2,1},{3,0},{4,7},{5,6},{6,5},{7,4},{8,11},{9,10},{10,... | collective-permute-start | bytes 442376 | tf_op jit(solution)/shard_map/ppermute | solution.py:297
  132.6 0.6 copy.23.mask_ref
  133.3 8.1 %attend.5 = (bf16[2,96,256]{2,1,0:T(8,128)(2,1)}, bf16[2,96,256]{2,1,0:T(8,128)(2,1)}, bf16[2,96,256]{2,1,0:T(8,128)(2,1)}, bf16[2,96,256]{2,1,0:T(8,128)(2,1)}) custom-call(s32[3]{0:T(128)} %pad_add_fusion.mine_ref, f32[1,256]{1,0:T(1,128)} %bitcast.23, bf16[256,1024]{1,0:T(8,128)(2,1)} %kernel_ref.5, bf16[8,1,384]{2,1,0:T(2,128)(2,1)} %copy.23.mask_ref, ...), custom_call_target="tpu_custom_call" | custom-call | tf_op jit(solution)/shard_map/attend/pallas_call | solution.py:269
  141.4 0.2 collective-permute-start.18
  141.6 2.0 %collective-permute-start.19 = (bf16[2,96,256]{2,1,0:T(8,128)(2,1)}, bf16[2,96,256]{2,1,0:T(8,128)(2,1)S(1)}, u32[]{:S(2)}, u32[]{:S(2)}) collective-permute-start(bf16[2,96,256]{2,1,0:T(8,128)(2,1)} %get-tuple-element.77), channel_id=1, source_target_pairs={{0,2},{1,3},{2,0},{3,1},{4,6},{5,7},{6,4},{7,5},{8,10},{9,11},{10,... | collective-permute-start | bytes 294920 | tf_op jit(solution)/shard_map/ppermute | solution.py:297
  143.7 0.2 broadcast_in_dim.9
  144.0 0.0 collective-permute-done.15
  144.0 2.3 %collective-permute-start.20 = (bf16[2,96,256]{2,1,0:T(8,128)(2,1)S(1)}, bf16[2,96,256]{2,1,0:T(8,128)(2,1)S(1)}, u32[]{:S(2)}, u32[]{:S(2)}) collective-permute-start(bf16[2,96,256]{2,1,0:T(8,128)(2,1)S(1)} %copy-done.13), channel_id=1, source_target_pairs={{0,3},{1,2},{2,1},{3,0},{4,7},{5,6},{6,5},{7,4},{8,11},{9,10},{10,... | collective-permute-start | bytes 294920 | tf_op jit(solution)/shard_map/ppermute | solution.py:297
  146.4 0.0 collective-permute-done.17
  146.4 0.5 collective-permute-done.18
  146.9 5.1 %collective-permute-done.19 = bf16[2,96,256]{2,1,0:T(8,128)(2,1)S(1)} collective-permute-done((bf16[2,96,256]{2,1,0:T(8,128)(2,1)}, bf16[2,96,256]{2,1,0:T(8,128)(2,1)S(1)}, u32[]{:S(2)}, u32[]{:S(2)}) %collective-permute-start.19) | collective-permute-done | bytes 98336 | tf_op jit(solution)/shard_map/ppermute | solution.py:297
  152.1 0.0 copy-start.8
  152.1 1.1 copy-done.8
  (50 shorter events, 0.4 us)
Async XLA Ops:
  7.2 45.3 %all-gather.3.cloned.1.call-start = ((), (), s32[]{:S(2)}) async-start(), calls=%async_computation.1 | async-start | bytes 2433024 | tf_op jit(solution)/shard_map/all_gather | solution.py:343
  11.4 27.7 %copy-start.2 = (bf16[32,96,256]{2,1,0:T(8,128)(2,1)S(1)}, bf16[32,96,256]{2,1,0:T(8,128)(2,1)}, u32[]{:S(2)}) copy-start(bf16[32,96,256]{2,1,0:T(8,128)(2,1)} %x_ref.1) | copy-start | bytes 4718596
  34.9 17.5 %all-to-all-start = ((bf16[8,13,32,128]{3,2,1,0:T(8,128)(2,1)}), bf16[8,13,32,128]{3,2,1,0:T(8,128)(2,1)}, u32[]{:S(2)}, u32[]{:S(2)}) async-start(bf16[8,13,32,128]{3,2,1,0:T(8,128)(2,1)} %all_gather.9), calls=%async_computation | async-start | bytes 1703936 | tf_op jit(solution)/shard_map/all_to_all | solution.py:345
  40.0 3.9 %copy-start.12 = (s32[384]{0:T(512)S(1)}, s32[384]{0:T(512)}, u32[]{:S(2)}) copy-start(s32[384]{0:T(512)} %param.15) | copy-start | bytes 4612
  40.0 24.2 %collective-permute-start = (bf16[8,96,256]{2,1,0:T(8,128)(2,1)S(1)}, bf16[8,96,256]{2,1,0:T(8,128)(2,1)S(1)}, u32[]{:S(2)}, u32[]{:S(2)}) collective-permute-start(bf16[8,96,256]{2,1,0:T(8,128)(2,1)S(1)} %get-tuple-element.48), channel_id=1, source_target_pairs={{0,1},{1,0},{2,3},{3,2},{4,5},{5,4},{6,7},{7,6},{8,9},{9,8},{10,11... | collective-permute-start | bytes 1179656 | tf_op jit(solution)/shard_map/ppermute | solution.py:297
  40.0 24.2 %collective-permute-start.1 = (bf16[8,96,256]{2,1,0:T(8,128)(2,1)S(1)}, bf16[8,96,256]{2,1,0:T(8,128)(2,1)S(1)}, u32[]{:S(2)}, u32[]{:S(2)}) collective-permute-start(bf16[8,96,256]{2,1,0:T(8,128)(2,1)S(1)} %get-tuple-element.49), channel_id=1, source_target_pairs={{0,2},{1,3},{2,0},{3,1},{4,6},{5,7},{6,4},{7,5},{8,10},{9,11},{10,... | collective-permute-start | bytes 1179656 | tf_op jit(solution)/shard_map/ppermute | solution.py:297
  64.3 23.1 %copy-start.5 = (bf16[8,96,256]{2,1,0:T(8,128)(2,1)}, bf16[8,96,256]{2,1,0:T(8,128)(2,1)S(1)}, u32[]{:S(2)}) copy-start(bf16[8,96,256]{2,1,0:T(8,128)(2,1)S(1)} %collective-permute-done.refs_1_) | copy-start | bytes 1179652
  64.3 23.0 %copy-start.6 = (bf16[8,96,256]{2,1,0:T(8,128)(2,1)}, bf16[8,96,256]{2,1,0:T(8,128)(2,1)S(1)}, u32[]{:S(2)}) copy-start(bf16[8,96,256]{2,1,0:T(8,128)(2,1)S(1)} %collective-permute-done.1.refs_2_) | copy-start | bytes 1179652
  64.3 7.0 %collective-permute-start.2 = (bf16[8,48,96]{2,1,0:T(8,128)(2,1)}, bf16[8,48,96]{2,1,0:T(8,128)(2,1)S(1)}, u32[]{:S(2)}, u32[]{:S(2)}) collective-permute-start(bf16[8,48,96]{2,1,0:T(8,128)(2,1)} %get-tuple-element.54), channel_id=1, source_target_pairs={{0,1},{1,0},{2,3},{3,2},{4,5},{5,4},{6,7},{7,6},{8,9},{9,8},{10,11... | collective-permute-start | bytes 221192 | tf_op jit(solution)/shard_map/ppermute | solution.py:297
  64.5 6.8 %collective-permute-start.3 = (bf16[8,48,96]{2,1,0:T(8,128)(2,1)}, bf16[8,48,96]{2,1,0:T(8,128)(2,1)S(1)}, u32[]{:S(2)}, u32[]{:S(2)}) collective-permute-start(bf16[8,48,96]{2,1,0:T(8,128)(2,1)} %get-tuple-element.54), channel_id=1, source_target_pairs={{0,2},{1,3},{2,0},{3,1},{4,6},{5,7},{6,4},{7,5},{8,10},{9,11},{10,... | collective-permute-start | bytes 221192 | tf_op jit(solution)/shard_map/ppermute | solution.py:297
  66.9 6.7 %collective-permute-start.4 = (bf16[8,48,96]{2,1,0:T(8,128)(2,1)}, bf16[8,48,96]{2,1,0:T(8,128)(2,1)S(1)}, u32[]{:S(2)}, u32[]{:S(2)}) collective-permute-start(bf16[8,48,96]{2,1,0:T(8,128)(2,1)} %get-tuple-element.54), channel_id=1, source_target_pairs={{0,3},{1,2},{2,1},{3,0},{4,7},{5,6},{6,5},{7,4},{8,11},{9,10},{10,... | collective-permute-start | bytes 221192 | tf_op jit(solution)/shard_map/ppermute | solution.py:297
  74.7 5.2 %collective-permute-start.7 = (bf16[1,4,48,384]{3,2,1,0:T(8,128)(2,1)S(1)}, bf16[1,4,48,384]{3,2,1,0:T(8,128)(2,1)S(1)}, u32[]{:S(2)}, u32[]{:S(2)}) collective-permute-start(bf16[1,4,48,384]{3,2,1,0:T(8,128)(2,1)S(1)} %maximum_bitcast_fusion.1), channel_id=1, source_target_pairs={{0,16},{4,20},{8,24},{12,28},{16,0},{20,4},{24,8},{28,12},{1,17},{... | collective-permute-start | bytes 442376 | tf_op jit(solution)/shard_map/ppermute | solution.py:294
  75.4 7.0 %collective-permute-start.5 = (bf16[1,4,48,384]{3,2,1,0:T(8,128)(2,1)S(1)}, bf16[1,4,48,384]{3,2,1,0:T(8,128)(2,1)S(1)}, u32[]{:S(2)}, u32[]{:S(2)}) collective-permute-start(bf16[1,4,48,384]{3,2,1,0:T(8,128)(2,1)S(1)} %maximum_bitcast_fusion), channel_id=1, source_target_pairs={{0,8},{4,12},{8,0},{12,4},{16,24},{20,28},{24,16},{28,20},{1,9},{5... | collective-permute-start | bytes 442376 | tf_op jit(solution)/shard_map/ppermute | solution.py:294
  79.9 7.3 %collective-permute-start.8 = (bf16[2,4,48,384]{3,2,1,0:T(8,128)(2,1)S(1)}, bf16[2,4,48,384]{3,2,1,0:T(8,128)(2,1)S(1)}, u32[]{:S(2)}, u32[]{:S(2)}) collective-permute-start(bf16[2,4,48,384]{3,2,1,0:T(8,128)(2,1)S(1)} %pad_maximum_fusion.3), channel_id=1, source_target_pairs={{0,8},{4,12},{8,0},{12,4},{16,24},{20,28},{24,16},{28,20},{1,9},{5... | collective-permute-start | bytes 884744 | tf_op jit(solution)/shard_map/ppermute | solution.py:294
  82.5 6.8 %collective-permute-start.6 = (bf16[2,4,48,384]{3,2,1,0:T(8,128)(2,1)S(1)}, bf16[2,4,48,384]{3,2,1,0:T(8,128)(2,1)S(1)}, u32[]{:S(2)}, u32[]{:S(2)}) collective-permute-start(bf16[2,4,48,384]{3,2,1,0:T(8,128)(2,1)S(1)} %pad_maximum_fusion.2), channel_id=1, source_target_pairs={{0,16},{4,20},{8,24},{12,28},{16,0},{20,4},{24,8},{28,12},{1,17},{... | collective-permute-start | bytes 884744 | tf_op jit(solution)/shard_map/ppermute | solution.py:294
  84.0 9.7 %collective-permute-start.9 = (bf16[8,96,256]{2,1,0:T(8,128)(2,1)S(1)}, bf16[8,96,256]{2,1,0:T(8,128)(2,1)S(1)}, u32[]{:S(2)}, u32[]{:S(2)}) collective-permute-start(bf16[8,96,256]{2,1,0:T(8,128)(2,1)S(1)} %get-tuple-element.58), channel_id=1, source_target_pairs={{0,3},{1,2},{2,1},{3,0},{4,7},{5,6},{6,5},{7,4},{8,11},{9,10},{10,... | collective-permute-start | bytes 1179656 | tf_op jit(solution)/shard_map/ppermute | solution.py:297
  87.3 9.3 %copy-start = (bf16[4,4,48,384]{3,2,1,0:T(8,128)(2,1)}, bf16[4,4,48,384]{3,2,1,0:T(8,128)(2,1)S(1)}, u32[]{:S(2)}) copy-start(bf16[4,4,48,384]{3,2,1,0:T(8,128)(2,1)S(1)} %pad_maximum_fusion.1.refs_6_) | copy-start | bytes 1769476
  89.3 7.3 %copy-start.1 = (bf16[4,4,48,384]{3,2,1,0:T(8,128)(2,1)}, bf16[4,4,48,384]{3,2,1,0:T(8,128)(2,1)S(1)}, u32[]{:S(2)}) copy-start(bf16[4,4,48,384]{3,2,1,0:T(8,128)(2,1)S(1)} %pad_maximum_fusion.refs_4_) | copy-start | bytes 1769476
  93.7 2.9 %copy-start.7 = (bf16[8,96,256]{2,1,0:T(8,128)(2,1)}, bf16[8,96,256]{2,1,0:T(8,128)(2,1)S(1)}, u32[]{:S(2)}) copy-start(bf16[8,96,256]{2,1,0:T(8,128)(2,1)S(1)} %collective-permute-done.9.refs_3_) | copy-start | bytes 1179652
  93.7 2.0 %collective-permute-start.10 = (bf16[4,4,48,384]{3,2,1,0:T(8,128)(2,1)S(1)}, bf16[4,4,48,384]{3,2,1,0:T(8,128)(2,1)S(1)}, u32[]{:S(2)}, u32[]{:S(2)}) collective-permute-start(bf16[4,4,48,384]{3,2,1,0:T(8,128)(2,1)S(1)} %pad_maximum_fusion.refs_4_), channel_id=1, source_target_pairs={{0,4},{4,0},{8,12},{12,8},{16,20},{20,16},{24,28},{28,24},{1,5},{5... | collective-permute-start | bytes 1769480 | tf_op jit(solution)/shard_map/ppermute | solution.py:294
  93.7 2.8 %collective-permute-start.11 = (bf16[4,4,48,384]{3,2,1,0:T(8,128)(2,1)S(1)}, bf16[4,4,48,384]{3,2,1,0:T(8,128)(2,1)S(1)}, u32[]{:S(2)}, u32[]{:S(2)}) collective-permute-start(bf16[4,4,48,384]{3,2,1,0:T(8,128)(2,1)S(1)} %pad_maximum_fusion.1.refs_6_), channel_id=1, source_target_pairs={{0,4},{4,0},{8,12},{12,8},{16,20},{20,16},{24,28},{28,24},{1,5},{5... | collective-permute-start | bytes 1769480 | tf_op jit(solution)/shard_map/ppermute | solution.py:294
  95.7 0.9 copy-start.3
  96.6 0.8 copy-start.4
  107.9 22.6 %collective-permute-start.12 = (bf16[3,96,256]{2,1,0:T(8,128)(2,1)}, bf16[3,96,256]{2,1,0:T(8,128)(2,1)S(1)}, u32[]{:S(2)}, u32[]{:S(2)}) collective-permute-start(bf16[3,96,256]{2,1,0:T(8,128)(2,1)} %get-tuple-element.63), channel_id=1, source_target_pairs={{0,1},{1,0},{2,3},{3,2},{4,5},{5,4},{6,7},{7,6},{8,9},{9,8},{10,11... | collective-permute-start | bytes 442376 | tf_op jit(solution)/shard_map/ppermute | solution.py:297
  115.3 17.4 %collective-permute-start.13 = (bf16[3,96,256]{2,1,0:T(8,128)(2,1)}, bf16[3,96,256]{2,1,0:T(8,128)(2,1)S(1)}, u32[]{:S(2)}, u32[]{:S(2)}) collective-permute-start(bf16[3,96,256]{2,1,0:T(8,128)(2,1)} %get-tuple-element.64), channel_id=1, source_target_pairs={{0,2},{1,3},{2,0},{3,1},{4,6},{5,7},{6,4},{7,5},{8,10},{9,11},{10,... | collective-permute-start | bytes 442376 | tf_op jit(solution)/shard_map/ppermute | solution.py:297
  115.5 17.2 %collective-permute-start.14 = (bf16[3,96,256]{2,1,0:T(8,128)(2,1)}, bf16[3,96,256]{2,1,0:T(8,128)(2,1)S(1)}, u32[]{:S(2)}, u32[]{:S(2)}) collective-permute-start(bf16[3,96,256]{2,1,0:T(8,128)(2,1)} %get-tuple-element.65), channel_id=1, source_target_pairs={{0,3},{1,2},{2,1},{3,0},{4,7},{5,6},{6,5},{7,4},{8,11},{9,10},{10,... | collective-permute-start | bytes 442376 | tf_op jit(solution)/shard_map/ppermute | solution.py:297
  128.2 15.8 %collective-permute-start.15 = (bf16[3,96,256]{2,1,0:T(8,128)(2,1)}, bf16[3,96,256]{2,1,0:T(8,128)(2,1)S(1)}, u32[]{:S(2)}, u32[]{:S(2)}) collective-permute-start(bf16[3,96,256]{2,1,0:T(8,128)(2,1)} %get-tuple-element.71), channel_id=1, source_target_pairs={{0,1},{1,0},{2,3},{3,2},{4,5},{5,4},{6,7},{7,6},{8,9},{9,8},{10,11... | collective-permute-start | bytes 442376 | tf_op jit(solution)/shard_map/ppermute | solution.py:297
  129.3 17.0 %collective-permute-start.16 = (bf16[3,96,256]{2,1,0:T(8,128)(2,1)}, bf16[3,96,256]{2,1,0:T(8,128)(2,1)S(1)}, u32[]{:S(2)}, u32[]{:S(2)}) collective-permute-start(bf16[3,96,256]{2,1,0:T(8,128)(2,1)} %get-tuple-element.72), channel_id=1, source_target_pairs={{0,2},{1,3},{2,0},{3,1},{4,6},{5,7},{6,4},{7,5},{8,10},{9,11},{10,... | collective-permute-start | bytes 442376 | tf_op jit(solution)/shard_map/ppermute | solution.py:297
  130.4 15.9 %collective-permute-start.17 = (bf16[3,96,256]{2,1,0:T(8,128)(2,1)}, bf16[3,96,256]{2,1,0:T(8,128)(2,1)S(1)}, u32[]{:S(2)}, u32[]{:S(2)}) collective-permute-start(bf16[3,96,256]{2,1,0:T(8,128)(2,1)} %get-tuple-element.73), channel_id=1, source_target_pairs={{0,3},{1,2},{2,1},{3,0},{4,7},{5,6},{6,5},{7,4},{8,11},{9,10},{10,... | collective-permute-start | bytes 442376 | tf_op jit(solution)/shard_map/ppermute | solution.py:297
  141.4 2.5 %copy-start.9 = (bf16[3,96,256]{2,1,0:T(8,128)(2,1)S(1)}, bf16[3,96,256]{2,1,0:T(8,128)(2,1)}, u32[]{:S(2)}) copy-start(bf16[3,96,256]{2,1,0:T(8,128)(2,1)} %get-tuple-element.66) | copy-start | bytes 442372
  141.4 2.6 %copy-start.10 = (bf16[3,96,256]{2,1,0:T(8,128)(2,1)S(1)}, bf16[3,96,256]{2,1,0:T(8,128)(2,1)}, u32[]{:S(2)}) copy-start(bf16[3,96,256]{2,1,0:T(8,128)(2,1)} %get-tuple-element.70) | copy-start | bytes 442372
  141.4 2.6 %copy-start.13 = (bf16[2,96,256]{2,1,0:T(8,128)(2,1)S(1)}, bf16[2,96,256]{2,1,0:T(8,128)(2,1)}, u32[]{:S(2)}) copy-start(bf16[2,96,256]{2,1,0:T(8,128)(2,1)} %get-tuple-element.78) | copy-start | bytes 294916
  141.4 5.5 %collective-permute-start.18 = (bf16[2,96,256]{2,1,0:T(8,128)(2,1)}, bf16[2,96,256]{2,1,0:T(8,128)(2,1)S(1)}, u32[]{:S(2)}, u32[]{:S(2)}) collective-permute-start(bf16[2,96,256]{2,1,0:T(8,128)(2,1)} %get-tuple-element.76), channel_id=1, source_target_pairs={{0,1},{1,0},{2,3},{3,2},{4,5},{5,4},{6,7},{7,6},{8,9},{9,8},{10,11... | collective-permute-start | bytes 294920 | tf_op jit(solution)/shard_map/ppermute | solution.py:297
  141.6 10.4 %collective-permute-start.19 = (bf16[2,96,256]{2,1,0:T(8,128)(2,1)}, bf16[2,96,256]{2,1,0:T(8,128)(2,1)S(1)}, u32[]{:S(2)}, u32[]{:S(2)}) collective-permute-start(bf16[2,96,256]{2,1,0:T(8,128)(2,1)} %get-tuple-element.77), channel_id=1, source_target_pairs={{0,2},{1,3},{2,0},{3,1},{4,6},{5,7},{6,4},{7,5},{8,10},{9,11},{10,... | collective-permute-start | bytes 294920 | tf_op jit(solution)/shard_map/ppermute | solution.py:297
  143.9 2.5 %copy-start.11 = (bf16[2,96,256]{2,1,0:T(8,128)(2,1)S(1)}, bf16[2,96,256]{2,1,0:T(8,128)(2,1)}, u32[]{:S(2)}) copy-start(bf16[2,96,256]{2,1,0:T(8,128)(2,1)} %get-tuple-element.75) | copy-start | bytes 294916
  144.0 8.0 %collective-permute-start.20 = (bf16[2,96,256]{2,1,0:T(8,128)(2,1)S(1)}, bf16[2,96,256]{2,1,0:T(8,128)(2,1)S(1)}, u32[]{:S(2)}, u32[]{:S(2)}) collective-permute-start(bf16[2,96,256]{2,1,0:T(8,128)(2,1)S(1)} %copy-done.13), channel_id=1, source_target_pairs={{0,3},{1,2},{2,1},{3,0},{4,7},{5,6},{6,5},{7,4},{8,11},{9,10},{10,... | collective-permute-start | bytes 294920 | tf_op jit(solution)/shard_map/ppermute | solution.py:297
  152.1 1.1 copy-start.8
Sparse Core Ops, SparseCore 0:
  11.6 30.8 all-gather.2

commit v4 on v3

--- a/solution.py
+++ b/solution.py
@@ -194,7 +194,7 @@
     )(mine, *operands)
 
 
-def attend(mine, pieces, gain, kernel, mask, low, high, closing, first, count):
+def attend(mine, pieces, starts, gain, kernel, mask, low, high, closing, first, count):
     cols = len(pieces)
     residues, channels = pieces[0].shape[1:]
     arrays = [array for array, offsets in (*low, *high)]
@@ -276,7 +276,7 @@
             pl.BlockSpec((1, 1, total), lambda s: (s + first, 0, 0)),
             whole(closing),
         ]
-        + [pl.BlockSpec((1, residues, channels), lambda s: (s + first, 0, 0))] * cols
+        + [pl.BlockSpec((1, residues, channels), lambda s, at=at: (s + at, 0, 0)) for at in starts]
         + [whole(array) for array in arrays],
         out_specs=[pl.BlockSpec((1, residues, channels), lambda s: (s, 0, 0))] * cols,
         out_shape=[jax.ShapeDtypeStruct((count, residues, channels), bf16)] * cols,
@@ -368,7 +368,9 @@
         tiles = [tile] + [by_col(tile, k) for k in range(1, n_col)]
         cut = tile.shape[0] // 2
         tiles, x[soon:] = lax.optimization_barrier((tiles, x[soon:]))
-        x[soon:] = [by_col(piece, k) for k, piece in enumerate(x[soon:], soon)]
+        lead = chunks(share)[0]
+        rest = [by_col(piece[lead:], k) for k, piece in enumerate(x[soon:], soon)] if lead < share else []
+        x[soon:] = [by_col(piece[:lead], k) for k, piece in enumerate(x[soon:], soon)]
         low, high, x[soon:] = gather_rows(
             jnp.concatenate([t[:cut] for t in tiles], 2), jnp.concatenate([t[cut:] for t in tiles], 2), x[soon:]
         )
@@ -376,10 +378,12 @@
         first = 0
         for count in chunks(share):
             held = rows_mask
+            now = [*x[:soon], *(x[soon:] if not first else rest)]
+            starts = [first] * soon + [max(first - lead, 0)] * (n_col - soon)
             if len(sent) > 1:
                 held, sent[-2] = lax.optimization_barrier((rows_mask, sent[-2]))
             outs = attend(
-                mine, x, lineup_gain, projection_kernel, held, low, high, closing_kernel, first, count
+                mine, now, starts, lineup_gain, projection_kernel, held, low, high, closing_kernel, first, count
             )
             sent.append([by_col(piece, k) if k else piece for k, piece in enumerate(outs)])
             first += count

time: 161 us -> 153 us (0.950)
  waiting for transfers between devices: 28.9 us -> 23.4 us
  starting transfers between devices: 39.8 us -> 36.8 us
    ppermute x15 -> x16, waiting for transfers between devices: 14.9 us -> 11.2 us  [by_col(): return lax.ppermute(x, 'col', [(c, c ^ k) for c in range(n_col)])]
    ppermute x15 -> x16, starting transfers between devices: 27.9 us -> 25 us  [by_col(): return lax.ppermute(x, 'col', [(c, c ^ k) for c in range(n_col)])]
    ppermute x6, waiting for transfers between devices: 6.63 us -> 4.83 us  [by_row(): return lax.ppermute(x, 'row', [(r, r ^ k) for r in range(n_row)])]
  transfers between devices with their start and end apart: 23 -> 24, of which waited for: 11 -> 8; matrix products, arithmetic and copies ran while one was open for 3% -> 4% of each run, Pallas kernels for 19% -> 27%
where the time goes in v4:
time: 153 us
  Pallas kernels  45.2 us (30%)
  starting transfers between devices  36.8 us (24%)
  waiting for transfers between devices  23.4 us (15%)
  blocking collectives  23.4 us (15%)
  between operations  14.5 us (9%)
  local copies, waits for them, and re-layouts  8.15 us (5%)
    pallas_call x3, Pallas kernels, attend(): pl.pallas_call(body, grid=(count,), in_specs=[SMEM, whole(gain), whole(ke...  29.2 us
    ppermute x16, starting transfers between devices, by_col(): return lax.ppermute(x, 'col', [(c, c ^ k) for c in range(n_col)])  25 us
    all_gather x1, blocking collectives, shards(): spread = lax.all_gather(left, 'col', axis=0, tiled=True)  23.4 us
    pallas_call x1, Pallas kernels, pair_tile(): pl.pallas_call(body, grid=(rows // block,), in_specs=[SMEM, *specs], out_...  11.8 us
    ppermute x16, waiting for transfers between devices, by_col(): return lax.ppermute(x, 'col', [(c, c ^ k) for c in range(n_col)])  11.2 us
    ppermute x6, starting transfers between devices, by_row(): return lax.ppermute(x, 'row', [(r, r ^ k) for r in range(n_row)])  7.6 us
    all_to_all x1, waiting for transfers between devices, shards(): left_rows = lax.all_to_all(spread, 'row', 0, 0, tiled=True)  7.34 us
    ppermute x6, waiting for transfers between devices, by_row(): return lax.ppermute(x, 'row', [(r, r ^ k) for r in range(n_row)])  4.83 us
  transfers between devices with their start and end apart: 24, of which 8 were waited for; matrix products, arithmetic and copies ran while one was open for 4% of the time, Pallas kernels for 27%

profile of v4, /device:TPU:0, one launch (start us, length us, event | category | flops | bytes accessed | tf_op | source)
XLA Modules:
  0.0 152.7 jit_solution(15231577838371516029)
XLA Ops:
  7.2 0.0 all-gather.3.cloned.1.call-start
  7.2 4.2 %opm_inputs.1 = (bf16[2,13,32,128]{3,2,1,0:T(8,128)(2,1)}, bf16[33,32,96]{2,1,0:T(8,128)(2,1)}) custom-call(bf16[32,96,256]{2,1,0:T(8,128)(2,1)} %x_ref.1, s32[32,96]{1,0:T(8,128)} %mask_ref.1, f32[1,256]{1,0:T(1,128)} %bitcast.25, bf16[32,256]{1,0:T(8,128)(2,1)} %bitcast.19, bf16[32,256]{1,0:T(8,128)(2,1)} %bitcast.20), custom_call_target="tpu_custom_call" | custom-call | tf_op jit(solution)/shard_map/opm_inputs/pallas_call | solution.py:82
  11.4 0.0 all-gather.3.cloned.1.call-update
  11.5 23.4 %all_gather.9 = bf16[8,13,32,128]{3,2,1,0:T(8,128)(2,1)} all-gather(bf16[2,13,32,128]{3,2,1,0:T(8,128)(2,1)} %get-tuple-element.41), channel_id=1, replica_groups=mesh['row'=8,'col'=4] {'col'}, dimensions={0}, use_global_device_ids=true | all-gather | bytes 1064960 | tf_op jit(solution)/shard_map/all_gather | solution.py:344
  34.9 4.2 %all-to-all-start = ((bf16[8,13,32,128]{3,2,1,0:T(8,128)(2,1)}), bf16[8,13,32,128]{3,2,1,0:T(8,128)(2,1)}, u32[]{:S(2)}, u32[]{:S(2)}) async-start(bf16[8,13,32,128]{3,2,1,0:T(8,128)(2,1)} %all_gather.9), calls=%async_computation | async-start | bytes 1703936 | tf_op jit(solution)/shard_map/all_to_all | solution.py:345
  39.2 0.9 constant_dynamic-slice_fusion.5
  40.0 2.4 %collective-permute-start.1 = (bf16[8,96,256]{2,1,0:T(8,128)(2,1)S(1)}, bf16[8,96,256]{2,1,0:T(8,128)(2,1)S(1)}, u32[]{:S(2)}, u32[]{:S(2)}) collective-permute-start(bf16[8,96,256]{2,1,0:T(8,128)(2,1)S(1)} %get-tuple-element.49), channel_id=1, source_target_pairs={{0,2},{1,3},{2,0},{3,1},{4,6},{5,7},{6,4},{7,5},{8,10},{9,11},{10,... | collective-permute-start | bytes 1179656 | tf_op jit(solution)/shard_map/ppermute | solution.py:297
  42.4 1.2 copy.19
  43.8 0.1 reshape.28
  43.9 0.6 reshape.30.refs_1_
  44.5 0.6 pad_add_fusion.mine_ref
  45.1 7.3 %all-to-all-done.left_ref = bf16[8,13,32,128]{3,2,1,0:T(8,128)(2,1)} async-done(((bf16[8,13,32,128]{3,2,1,0:T(8,128)(2,1)}), bf16[8,13,32,128]{3,2,1,0:T(8,128)(2,1)}, u32[]{:S(2)}, u32[]{:S(2)}) %all-to-all-start) | async-done | bytes 852000 | tf_op jit(solution)/shard_map/all_to_all | solution.py:345
  52.4 11.8 %pair_tile.1 = (f32[48,96,128]{2,1,0:T(8,128)}, bf16[8,48,96]{2,1,0:T(8,128)(2,1)}) custom-call(s32[3]{0:T(128)} %pad_add_fusion.mine_ref, bf16[8,13,32,128]{3,2,1,0:T(8,128)(2,1)} %all-to-all-done.left_ref, bf16[8,33,32,96]{3,2,1,0:T(8,128)(2,1)} %bitcast.17, f32[48,96,128]{2,1,0:T(8,128)} %refs_0_.1, s32[1,384]{1,0:T(1,128)} %reshape.30.refs_1_, ...), custom_call_target="tpu_custom_call" | custom-call | tf_op jit(solution)/shard_map/pair_tile/pallas_call | solution.py:174
  64.2 0.0 collective-permute-done.refs_1_
  64.3 0.0 collective-permute-done.1.refs_2_
  64.3 0.2 collective-permute-start.2
  64.5 2.4 %collective-permute-start.3 = (bf16[8,48,96]{2,1,0:T(8,128)(2,1)}, bf16[8,48,96]{2,1,0:T(8,128)(2,1)S(1)}, u32[]{:S(2)}, u32[]{:S(2)}) collective-permute-start(bf16[8,48,96]{2,1,0:T(8,128)(2,1)} %get-tuple-element.54), channel_id=1, source_target_pairs={{0,2},{1,3},{2,0},{3,1},{4,6},{5,7},{6,4},{7,5},{8,10},{9,11},{10,... | collective-permute-start | bytes 221192 | tf_op jit(solution)/shard_map/ppermute | solution.py:297
  66.9 1.8 %collective-permute-start.4 = (bf16[8,48,96]{2,1,0:T(8,128)(2,1)}, bf16[8,48,96]{2,1,0:T(8,128)(2,1)S(1)}, u32[]{:S(2)}, u32[]{:S(2)}) collective-permute-start(bf16[8,48,96]{2,1,0:T(8,128)(2,1)} %get-tuple-element.54), channel_id=1, source_target_pairs={{0,3},{1,2},{2,1},{3,0},{4,7},{5,6},{6,5},{7,4},{8,11},{9,10},{10,... | collective-permute-start | bytes 221192 | tf_op jit(solution)/shard_map/ppermute | solution.py:297
  68.7 2.5 %collective-permute-done.2 = bf16[8,48,96]{2,1,0:T(8,128)(2,1)S(1)} collective-permute-done((bf16[8,48,96]{2,1,0:T(8,128)(2,1)}, bf16[8,48,96]{2,1,0:T(8,128)(2,1)S(1)}, u32[]{:S(2)}, u32[]{:S(2)}) %collective-permute-start.2) | collective-permute-done | bytes 73760 | tf_op jit(solution)/shard_map/ppermute | solution.py:297
  71.3 0.0 collective-permute-done.3
  71.3 2.4 %collective-permute-done.4 = bf16[8,48,96]{2,1,0:T(8,128)(2,1)S(1)} collective-permute-done((bf16[8,48,96]{2,1,0:T(8,128)(2,1)}, bf16[8,48,96]{2,1,0:T(8,128)(2,1)S(1)}, u32[]{:S(2)}, u32[]{:S(2)}) %collective-permute-start.4) | collective-permute-done | bytes 73760 | tf_op jit(solution)/shard_map/ppermute | solution.py:297
  73.6 0.8 fusion
  74.5 0.1 maximum_bitcast_fusion.1
  74.7 0.6 collective-permute-start.7
  75.3 0.1 maximum_bitcast_fusion
  75.4 2.4 %collective-permute-start.5 = (bf16[1,4,48,384]{3,2,1,0:T(8,128)(2,1)S(1)}, bf16[1,4,48,384]{3,2,1,0:T(8,128)(2,1)S(1)}, u32[]{:S(2)}, u32[]{:S(2)}) collective-permute-start(bf16[1,4,48,384]{3,2,1,0:T(8,128)(2,1)S(1)} %maximum_bitcast_fusion), channel_id=1, source_target_pairs={{0,8},{4,12},{8,0},{12,4},{16,24},{20,28},{24,16},{28,20},{1,9},{5... | collective-permute-start | bytes 442376 | tf_op jit(solution)/shard_map/ppermute | solution.py:294
  77.8 2.1 %collective-permute-done.7 = bf16[1,4,48,384]{3,2,1,0:T(8,128)(2,1)S(1)} collective-permute-done((bf16[1,4,48,384]{3,2,1,0:T(8,128)(2,1)S(1)}, bf16[1,4,48,384]{3,2,1,0:T(8,128)(2,1)S(1)}, u32[]{:S(2)}, u32[]{:S(2)}) %collective-permute-start.7) | collective-permute-done | bytes 147488 | tf_op jit(solution)/shard_map/ppermute | solution.py:294
  79.9 2.5 %collective-permute-start.8 = (bf16[2,4,48,384]{3,2,1,0:T(8,128)(2,1)S(1)}, bf16[2,4,48,384]{3,2,1,0:T(8,128)(2,1)S(1)}, u32[]{:S(2)}, u32[]{:S(2)}) collective-permute-start(bf16[2,4,48,384]{3,2,1,0:T(8,128)(2,1)S(1)} %pad_maximum_fusion.3), channel_id=1, source_target_pairs={{0,8},{4,12},{8,0},{12,4},{16,24},{20,28},{24,16},{28,20},{1,9},{5... | collective-permute-start | bytes 884744 | tf_op jit(solution)/shard_map/ppermute | solution.py:294
  82.4 0.0 collective-permute-done.5
  82.5 1.6 %collective-permute-start.6 = (bf16[2,4,48,384]{3,2,1,0:T(8,128)(2,1)S(1)}, bf16[2,4,48,384]{3,2,1,0:T(8,128)(2,1)S(1)}, u32[]{:S(2)}, u32[]{:S(2)}) collective-permute-start(bf16[2,4,48,384]{3,2,1,0:T(8,128)(2,1)S(1)} %pad_maximum_fusion.2), channel_id=1, source_target_pairs={{0,16},{4,20},{8,24},{12,28},{16,0},{20,4},{24,8},{28,12},{1,17},{... | collective-permute-start | bytes 884744 | tf_op jit(solution)/shard_map/ppermute | solution.py:294
  84.1 2.4 %collective-permute-start.9 = (bf16[3,96,256]{2,1,0:T(8,128)(2,1)S(1)}, bf16[3,96,256]{2,1,0:T(8,128)(2,1)S(1)}, u32[]{:S(2)}, u32[]{:S(2)}) collective-permute-start(bf16[3,96,256]{2,1,0:T(8,128)(2,1)S(1)} %slice.42), channel_id=1, source_target_pairs={{0,3},{1,2},{2,1},{3,0},{4,7},{5,6},{6,5},{7,4},{8,11},{9,10},{10,... | collective-permute-start | bytes 442376 | tf_op jit(solution)/shard_map/ppermute | solution.py:297
  86.4 0.8 collective-permute-done.8
  87.2 0.1 pad_maximum_fusion.1.refs_6_
  87.3 1.9 %collective-permute-done.6 = bf16[2,4,48,384]{3,2,1,0:T(8,128)(2,1)S(1)} collective-permute-done((bf16[2,4,48,384]{3,2,1,0:T(8,128)(2,1)S(1)}, bf16[2,4,48,384]{3,2,1,0:T(8,128)(2,1)S(1)}, u32[]{:S(2)}, u32[]{:S(2)}) %collective-permute-start.6) | collective-permute-done | bytes 294944 | tf_op jit(solution)/shard_map/ppermute | solution.py:294
  89.3 0.1 pad_maximum_fusion.refs_4_
  89.3 0.0 copy-start.1
  89.4 1.8 %collective-permute-done.9.refs_3_ = bf16[3,96,256]{2,1,0:T(8,128)(2,1)S(1)} collective-permute-done((bf16[3,96,256]{2,1,0:T(8,128)(2,1)S(1)}, bf16[3,96,256]{2,1,0:T(8,128)(2,1)S(1)}, u32[]{:S(2)}, u32[]{:S(2)}) %collective-permute-start.9) | collective-permute-done | bytes 147488 | tf_op jit(solution)/shard_map/ppermute | solution.py:297
  91.2 0.0 collective-permute-start.10
  91.2 0.5 collective-permute-start.11
  91.7 2.4 %collective-permute-start.15 = (bf16[5,96,256]{2,1,0:T(8,128)(2,1)S(1)}, bf16[5,96,256]{2,1,0:T(8,128)(2,1)S(1)}, u32[]{:S(2)}, u32[]{:S(2)}) collective-permute-start(bf16[5,96,256]{2,1,0:T(8,128)(2,1)S(1)} %slice.43), channel_id=1, source_target_pairs={{0,3},{1,2},{2,1},{3,0},{4,7},{5,6},{6,5},{7,4},{8,11},{9,10},{10,... | collective-permute-start | bytes 737288 | tf_op jit(solution)/shard_map/ppermute | solution.py:297
  94.1 0.6 copy.21.mask_ref
  94.7 0.0 collective-permute-done.10.refs_5_
  94.7 0.0 collective-permute-done.11.refs_7_
  94.7 0.8 copy-done.3
  95.5 0.2 copy-done.4
  95.7 10.5 %attend.3 = (bf16[3,96,256]{2,1,0:T(8,128)(2,1)}, bf16[3,96,256]{2,1,0:T(8,128)(2,1)}, bf16[3,96,256]{2,1,0:T(8,128)(2,1)}, bf16[3,96,256]{2,1,0:T(8,128)(2,1)}) custom-call(s32[3]{0:T(128)} %pad_add_fusion.mine_ref, f32[1,256]{1,0:T(1,128)} %bitcast.21, bf16[256,1024]{1,0:T(8,128)(2,1)} %kernel_ref.5, bf16[8,1,384]{2,1,0:T(2,128)(2,1)} %copy.21.mask_ref, ...), custom_call_target="tpu_custom_call" | custom-call | tf_op jit(solution)/shard_map/attend/pallas_call | solution.py:269
  106.2 0.1 collective-permute-start.12
  106.3 2.1 %collective-permute-start.13 = (bf16[3,96,256]{2,1,0:T(8,128)(2,1)}, bf16[3,96,256]{2,1,0:T(8,128)(2,1)S(1)}, u32[]{:S(2)}, u32[]{:S(2)}) collective-permute-start(bf16[3,96,256]{2,1,0:T(8,128)(2,1)} %get-tuple-element.64), channel_id=1, source_target_pairs={{0,2},{1,3},{2,0},{3,1},{4,6},{5,7},{6,4},{7,5},{8,10},{9,11},{10,... | collective-permute-start | bytes 442376 | tf_op jit(solution)/shard_map/ppermute | solution.py:297
  108.3 2.3 %collective-permute-start.14 = (bf16[3,96,256]{2,1,0:T(8,128)(2,1)}, bf16[3,96,256]{2,1,0:T(8,128)(2,1)S(1)}, u32[]{:S(2)}, u32[]{:S(2)}) collective-permute-start(bf16[3,96,256]{2,1,0:T(8,128)(2,1)} %get-tuple-element.65), channel_id=1, source_target_pairs={{0,3},{1,2},{2,1},{3,0},{4,7},{5,6},{6,5},{7,4},{8,11},{9,10},{10,... | collective-permute-start | bytes 442376 | tf_op jit(solution)/shard_map/ppermute | solution.py:297
  110.6 0.7 copy-done.8
  111.3 10.5 %attend.4 = (bf16[3,96,256]{2,1,0:T(8,128)(2,1)}, bf16[3,96,256]{2,1,0:T(8,128)(2,1)}, bf16[3,96,256]{2,1,0:T(8,128)(2,1)}, bf16[3,96,256]{2,1,0:T(8,128)(2,1)}) custom-call(s32[3]{0:T(128)} %pad_add_fusion.mine_ref, f32[1,256]{1,0:T(1,128)} %bitcast.22, bf16[256,1024]{1,0:T(8,128)(2,1)} %kernel_ref.5, bf16[8,1,384]{2,1,0:T(2,128)(2,1)} %copy.21.mask_ref, ...), custom_call_target="tpu_custom_call" | custom-call | tf_op jit(solution)/shard_map/attend/pallas_call | solution.py:269
  121.9 0.1 collective-permute-start.16
  121.9 2.1 %collective-permute-start.17 = (bf16[3,96,256]{2,1,0:T(8,128)(2,1)}, bf16[3,96,256]{2,1,0:T(8,128)(2,1)S(1)}, u32[]{:S(2)}, u32[]{:S(2)}) collective-permute-start(bf16[3,96,256]{2,1,0:T(8,128)(2,1)} %get-tuple-element.72), channel_id=1, source_target_pairs={{0,2},{1,3},{2,0},{3,1},{4,6},{5,7},{6,4},{7,5},{8,10},{9,11},{10,... | collective-permute-start | bytes 442376 | tf_op jit(solution)/shard_map/ppermute | solution.py:297
  124.0 2.3 %collective-permute-start.18 = (bf16[3,96,256]{2,1,0:T(8,128)(2,1)}, bf16[3,96,256]{2,1,0:T(8,128)(2,1)S(1)}, u32[]{:S(2)}, u32[]{:S(2)}) collective-permute-start(bf16[3,96,256]{2,1,0:T(8,128)(2,1)} %get-tuple-element.73), channel_id=1, source_target_pairs={{0,3},{1,2},{2,1},{3,0},{4,7},{5,6},{6,5},{7,4},{8,11},{9,10},{10,... | collective-permute-start | bytes 442376 | tf_op jit(solution)/shard_map/ppermute | solution.py:297
  126.3 0.0 collective-permute-done.13
  126.3 0.6 copy.23.mask_ref
  126.9 8.2 %attend.5 = (bf16[2,96,256]{2,1,0:T(8,128)(2,1)}, bf16[2,96,256]{2,1,0:T(8,128)(2,1)}, bf16[2,96,256]{2,1,0:T(8,128)(2,1)}, bf16[2,96,256]{2,1,0:T(8,128)(2,1)}) custom-call(s32[3]{0:T(128)} %pad_add_fusion.mine_ref, f32[1,256]{1,0:T(1,128)} %bitcast.23, bf16[256,1024]{1,0:T(8,128)(2,1)} %kernel_ref.5, bf16[8,1,384]{2,1,0:T(2,128)(2,1)} %copy.23.mask_ref, ...), custom_call_target="tpu_custom_call" | custom-call | tf_op jit(solution)/shard_map/attend/pallas_call | solution.py:269
  135.1 0.1 collective-permute-start.19
  135.2 2.1 %collective-permute-start.20 = (bf16[2,96,256]{2,1,0:T(8,128)(2,1)}, bf16[2,96,256]{2,1,0:T(8,128)(2,1)S(1)}, u32[]{:S(2)}, u32[]{:S(2)}) collective-permute-start(bf16[2,96,256]{2,1,0:T(8,128)(2,1)} %get-tuple-element.77), channel_id=1, source_target_pairs={{0,2},{1,3},{2,0},{3,1},{4,6},{5,7},{6,4},{7,5},{8,10},{9,11},{10,... | collective-permute-start | bytes 294920 | tf_op jit(solution)/shard_map/ppermute | solution.py:297
  137.3 0.2 broadcast_in_dim.9
  137.7 2.3 %collective-permute-start.21 = (bf16[2,96,256]{2,1,0:T(8,128)(2,1)S(1)}, bf16[2,96,256]{2,1,0:T(8,128)(2,1)S(1)}, u32[]{:S(2)}, u32[]{:S(2)}) collective-permute-start(bf16[2,96,256]{2,1,0:T(8,128)(2,1)S(1)} %copy-done.14), channel_id=1, source_target_pairs={{0,3},{1,2},{2,1},{3,0},{4,7},{5,6},{6,5},{7,4},{8,11},{9,10},{10,... | collective-permute-start | bytes 294920 | tf_op jit(solution)/shard_map/ppermute | solution.py:297
  140.2 4.5 %collective-permute-done.20 = bf16[2,96,256]{2,1,0:T(8,128)(2,1)S(1)} collective-permute-done((bf16[2,96,256]{2,1,0:T(8,128)(2,1)}, bf16[2,96,256]{2,1,0:T(8,128)(2,1)S(1)}, u32[]{:S(2)}, u32[]{:S(2)}) %collective-permute-start.20) | collective-permute-done | bytes 98336 | tf_op jit(solution)/shard_map/ppermute | solution.py:297
  144.7 0.0 copy-start.7
  144.7 1.1 copy-done.7
  (56 shorter events, 0.4 us)
Async XLA Ops:
  7.2 45.3 %all-gather.3.cloned.1.call-start = ((), (), s32[]{:S(2)}) async-start(), calls=%async_computation.1 | async-start | bytes 2433024 | tf_op jit(solution)/shard_map/all_gather | solution.py:343
  11.4 27.7 %copy-start.2 = (bf16[32,96,256]{2,1,0:T(8,128)(2,1)S(1)}, bf16[32,96,256]{2,1,0:T(8,128)(2,1)}, u32[]{:S(2)}) copy-start(bf16[32,96,256]{2,1,0:T(8,128)(2,1)} %x_ref.1) | copy-start | bytes 4718596
  34.9 17.5 %all-to-all-start = ((bf16[8,13,32,128]{3,2,1,0:T(8,128)(2,1)}), bf16[8,13,32,128]{3,2,1,0:T(8,128)(2,1)}, u32[]{:S(2)}, u32[]{:S(2)}) async-start(bf16[8,13,32,128]{3,2,1,0:T(8,128)(2,1)} %all_gather.9), calls=%async_computation | async-start | bytes 1703936 | tf_op jit(solution)/shard_map/all_to_all | solution.py:345
  40.0 3.9 %copy-start.13 = (s32[384]{0:T(512)S(1)}, s32[384]{0:T(512)}, u32[]{:S(2)}) copy-start(s32[384]{0:T(512)} %param.15) | copy-start | bytes 4612
  40.0 24.2 %collective-permute-start = (bf16[8,96,256]{2,1,0:T(8,128)(2,1)S(1)}, bf16[8,96,256]{2,1,0:T(8,128)(2,1)S(1)}, u32[]{:S(2)}, u32[]{:S(2)}) collective-permute-start(bf16[8,96,256]{2,1,0:T(8,128)(2,1)S(1)} %get-tuple-element.48), channel_id=1, source_target_pairs={{0,1},{1,0},{2,3},{3,2},{4,5},{5,4},{6,7},{7,6},{8,9},{9,8},{10,11... | collective-permute-start | bytes 1179656 | tf_op jit(solution)/shard_map/ppermute | solution.py:297
  40.0 24.2 %collective-permute-start.1 = (bf16[8,96,256]{2,1,0:T(8,128)(2,1)S(1)}, bf16[8,96,256]{2,1,0:T(8,128)(2,1)S(1)}, u32[]{:S(2)}, u32[]{:S(2)}) collective-permute-start(bf16[8,96,256]{2,1,0:T(8,128)(2,1)S(1)} %get-tuple-element.49), channel_id=1, source_target_pairs={{0,2},{1,3},{2,0},{3,1},{4,6},{5,7},{6,4},{7,5},{8,10},{9,11},{10,... | collective-permute-start | bytes 1179656 | tf_op jit(solution)/shard_map/ppermute | solution.py:297
  64.3 23.0 %copy-start.5 = (bf16[8,96,256]{2,1,0:T(8,128)(2,1)}, bf16[8,96,256]{2,1,0:T(8,128)(2,1)S(1)}, u32[]{:S(2)}) copy-start(bf16[8,96,256]{2,1,0:T(8,128)(2,1)S(1)} %collective-permute-done.refs_1_) | copy-start | bytes 1179652
  64.3 23.0 %copy-start.6 = (bf16[8,96,256]{2,1,0:T(8,128)(2,1)}, bf16[8,96,256]{2,1,0:T(8,128)(2,1)S(1)}, u32[]{:S(2)}) copy-start(bf16[8,96,256]{2,1,0:T(8,128)(2,1)S(1)} %collective-permute-done.1.refs_2_) | copy-start | bytes 1179652
  64.3 7.0 %collective-permute-start.2 = (bf16[8,48,96]{2,1,0:T(8,128)(2,1)}, bf16[8,48,96]{2,1,0:T(8,128)(2,1)S(1)}, u32[]{:S(2)}, u32[]{:S(2)}) collective-permute-start(bf16[8,48,96]{2,1,0:T(8,128)(2,1)} %get-tuple-element.54), channel_id=1, source_target_pairs={{0,1},{1,0},{2,3},{3,2},{4,5},{5,4},{6,7},{7,6},{8,9},{9,8},{10,11... | collective-permute-start | bytes 221192 | tf_op jit(solution)/shard_map/ppermute | solution.py:297
  64.5 6.8 %collective-permute-start.3 = (bf16[8,48,96]{2,1,0:T(8,128)(2,1)}, bf16[8,48,96]{2,1,0:T(8,128)(2,1)S(1)}, u32[]{:S(2)}, u32[]{:S(2)}) collective-permute-start(bf16[8,48,96]{2,1,0:T(8,128)(2,1)} %get-tuple-element.54), channel_id=1, source_target_pairs={{0,2},{1,3},{2,0},{3,1},{4,6},{5,7},{6,4},{7,5},{8,10},{9,11},{10,... | collective-permute-start | bytes 221192 | tf_op jit(solution)/shard_map/ppermute | solution.py:297
  66.9 6.7 %collective-permute-start.4 = (bf16[8,48,96]{2,1,0:T(8,128)(2,1)}, bf16[8,48,96]{2,1,0:T(8,128)(2,1)S(1)}, u32[]{:S(2)}, u32[]{:S(2)}) collective-permute-start(bf16[8,48,96]{2,1,0:T(8,128)(2,1)} %get-tuple-element.54), channel_id=1, source_target_pairs={{0,3},{1,2},{2,1},{3,0},{4,7},{5,6},{6,5},{7,4},{8,11},{9,10},{10,... | collective-permute-start | bytes 221192 | tf_op jit(solution)/shard_map/ppermute | solution.py:297
  74.7 5.2 %collective-permute-start.7 = (bf16[1,4,48,384]{3,2,1,0:T(8,128)(2,1)S(1)}, bf16[1,4,48,384]{3,2,1,0:T(8,128)(2,1)S(1)}, u32[]{:S(2)}, u32[]{:S(2)}) collective-permute-start(bf16[1,4,48,384]{3,2,1,0:T(8,128)(2,1)S(1)} %maximum_bitcast_fusion.1), channel_id=1, source_target_pairs={{0,16},{4,20},{8,24},{12,28},{16,0},{20,4},{24,8},{28,12},{1,17},{... | collective-permute-start | bytes 442376 | tf_op jit(solution)/shard_map/ppermute | solution.py:294
  75.4 7.0 %collective-permute-start.5 = (bf16[1,4,48,384]{3,2,1,0:T(8,128)(2,1)S(1)}, bf16[1,4,48,384]{3,2,1,0:T(8,128)(2,1)S(1)}, u32[]{:S(2)}, u32[]{:S(2)}) collective-permute-start(bf16[1,4,48,384]{3,2,1,0:T(8,128)(2,1)S(1)} %maximum_bitcast_fusion), channel_id=1, source_target_pairs={{0,8},{4,12},{8,0},{12,4},{16,24},{20,28},{24,16},{28,20},{1,9},{5... | collective-permute-start | bytes 442376 | tf_op jit(solution)/shard_map/ppermute | solution.py:294
  79.9 7.3 %collective-permute-start.8 = (bf16[2,4,48,384]{3,2,1,0:T(8,128)(2,1)S(1)}, bf16[2,4,48,384]{3,2,1,0:T(8,128)(2,1)S(1)}, u32[]{:S(2)}, u32[]{:S(2)}) collective-permute-start(bf16[2,4,48,384]{3,2,1,0:T(8,128)(2,1)S(1)} %pad_maximum_fusion.3), channel_id=1, source_target_pairs={{0,8},{4,12},{8,0},{12,4},{16,24},{20,28},{24,16},{28,20},{1,9},{5... | collective-permute-start | bytes 884744 | tf_op jit(solution)/shard_map/ppermute | solution.py:294
  82.5 6.8 %collective-permute-start.6 = (bf16[2,4,48,384]{3,2,1,0:T(8,128)(2,1)S(1)}, bf16[2,4,48,384]{3,2,1,0:T(8,128)(2,1)S(1)}, u32[]{:S(2)}, u32[]{:S(2)}) collective-permute-start(bf16[2,4,48,384]{3,2,1,0:T(8,128)(2,1)S(1)} %pad_maximum_fusion.2), channel_id=1, source_target_pairs={{0,16},{4,20},{8,24},{12,28},{16,0},{20,4},{24,8},{28,12},{1,17},{... | collective-permute-start | bytes 884744 | tf_op jit(solution)/shard_map/ppermute | solution.py:294
  84.1 7.1 %collective-permute-start.9 = (bf16[3,96,256]{2,1,0:T(8,128)(2,1)S(1)}, bf16[3,96,256]{2,1,0:T(8,128)(2,1)S(1)}, u32[]{:S(2)}, u32[]{:S(2)}) collective-permute-start(bf16[3,96,256]{2,1,0:T(8,128)(2,1)S(1)} %slice.42), channel_id=1, source_target_pairs={{0,3},{1,2},{2,1},{3,0},{4,7},{5,6},{6,5},{7,4},{8,11},{9,10},{10,... | collective-permute-start | bytes 442376 | tf_op jit(solution)/shard_map/ppermute | solution.py:297
  87.3 7.4 %copy-start = (bf16[4,4,48,384]{3,2,1,0:T(8,128)(2,1)}, bf16[4,4,48,384]{3,2,1,0:T(8,128)(2,1)S(1)}, u32[]{:S(2)}) copy-start(bf16[4,4,48,384]{3,2,1,0:T(8,128)(2,1)S(1)} %pad_maximum_fusion.1.refs_6_) | copy-start | bytes 1769476
  89.3 5.4 %copy-start.1 = (bf16[4,4,48,384]{3,2,1,0:T(8,128)(2,1)}, bf16[4,4,48,384]{3,2,1,0:T(8,128)(2,1)S(1)}, u32[]{:S(2)}) copy-start(bf16[4,4,48,384]{3,2,1,0:T(8,128)(2,1)S(1)} %pad_maximum_fusion.refs_4_) | copy-start | bytes 1769476
  91.2 3.5 %copy-start.9 = (bf16[3,96,256]{2,1,0:T(8,128)(2,1)}, bf16[3,96,256]{2,1,0:T(8,128)(2,1)S(1)}, u32[]{:S(2)}) copy-start(bf16[3,96,256]{2,1,0:T(8,128)(2,1)S(1)} %collective-permute-done.9.refs_3_) | copy-start | bytes 442372
  91.2 3.5 %collective-permute-start.10 = (bf16[4,4,48,384]{3,2,1,0:T(8,128)(2,1)S(1)}, bf16[4,4,48,384]{3,2,1,0:T(8,128)(2,1)S(1)}, u32[]{:S(2)}, u32[]{:S(2)}) collective-permute-start(bf16[4,4,48,384]{3,2,1,0:T(8,128)(2,1)S(1)} %pad_maximum_fusion.refs_4_), channel_id=1, source_target_pairs={{0,4},{4,0},{8,12},{12,8},{16,20},{20,16},{24,28},{28,24},{1,5},{5... | collective-permute-start | bytes 1769480 | tf_op jit(solution)/shard_map/ppermute | solution.py:294
  91.2 3.5 %collective-permute-start.11 = (bf16[4,4,48,384]{3,2,1,0:T(8,128)(2,1)S(1)}, bf16[4,4,48,384]{3,2,1,0:T(8,128)(2,1)S(1)}, u32[]{:S(2)}, u32[]{:S(2)}) collective-permute-start(bf16[4,4,48,384]{3,2,1,0:T(8,128)(2,1)S(1)} %pad_maximum_fusion.1.refs_6_), channel_id=1, source_target_pairs={{0,4},{4,0},{8,12},{12,8},{16,20},{20,16},{24,28},{28,24},{1,5},{5... | collective-permute-start | bytes 1769480 | tf_op jit(solution)/shard_map/ppermute | solution.py:294
  91.7 18.9 %collective-permute-start.15 = (bf16[5,96,256]{2,1,0:T(8,128)(2,1)S(1)}, bf16[5,96,256]{2,1,0:T(8,128)(2,1)S(1)}, u32[]{:S(2)}, u32[]{:S(2)}) collective-permute-start(bf16[5,96,256]{2,1,0:T(8,128)(2,1)S(1)} %slice.43), channel_id=1, source_target_pairs={{0,3},{1,2},{2,1},{3,0},{4,7},{5,6},{6,5},{7,4},{8,11},{9,10},{10,... | collective-permute-start | bytes 737288 | tf_op jit(solution)/shard_map/ppermute | solution.py:297
  94.7 0.8 copy-start.3
  94.7 1.0 copy-start.4
  106.2 17.9 %collective-permute-start.12 = (bf16[3,96,256]{2,1,0:T(8,128)(2,1)}, bf16[3,96,256]{2,1,0:T(8,128)(2,1)S(1)}, u32[]{:S(2)}, u32[]{:S(2)}) collective-permute-start(bf16[3,96,256]{2,1,0:T(8,128)(2,1)} %get-tuple-element.63), channel_id=1, source_target_pairs={{0,1},{1,0},{2,3},{3,2},{4,5},{5,4},{6,7},{7,6},{8,9},{9,8},{10,11... | collective-permute-start | bytes 442376 | tf_op jit(solution)/shard_map/ppermute | solution.py:297
  106.3 20.0 %collective-permute-start.13 = (bf16[3,96,256]{2,1,0:T(8,128)(2,1)}, bf16[3,96,256]{2,1,0:T(8,128)(2,1)S(1)}, u32[]{:S(2)}, u32[]{:S(2)}) collective-permute-start(bf16[3,96,256]{2,1,0:T(8,128)(2,1)} %get-tuple-element.64), channel_id=1, source_target_pairs={{0,2},{1,3},{2,0},{3,1},{4,6},{5,7},{6,4},{7,5},{8,10},{9,11},{10,... | collective-permute-start | bytes 442376 | tf_op jit(solution)/shard_map/ppermute | solution.py:297
  108.3 18.0 %collective-permute-start.14 = (bf16[3,96,256]{2,1,0:T(8,128)(2,1)}, bf16[3,96,256]{2,1,0:T(8,128)(2,1)S(1)}, u32[]{:S(2)}, u32[]{:S(2)}) collective-permute-start(bf16[3,96,256]{2,1,0:T(8,128)(2,1)} %get-tuple-element.65), channel_id=1, source_target_pairs={{0,3},{1,2},{2,1},{3,0},{4,7},{5,6},{6,5},{7,4},{8,11},{9,10},{10,... | collective-permute-start | bytes 442376 | tf_op jit(solution)/shard_map/ppermute | solution.py:297
  110.6 0.7 copy-start.8
  121.9 15.8 %collective-permute-start.16 = (bf16[3,96,256]{2,1,0:T(8,128)(2,1)}, bf16[3,96,256]{2,1,0:T(8,128)(2,1)S(1)}, u32[]{:S(2)}, u32[]{:S(2)}) collective-permute-start(bf16[3,96,256]{2,1,0:T(8,128)(2,1)} %get-tuple-element.71), channel_id=1, source_target_pairs={{0,1},{1,0},{2,3},{3,2},{4,5},{5,4},{6,7},{7,6},{8,9},{9,8},{10,11... | collective-permute-start | bytes 442376 | tf_op jit(solution)/shard_map/ppermute | solution.py:297
  121.9 18.1 %collective-permute-start.17 = (bf16[3,96,256]{2,1,0:T(8,128)(2,1)}, bf16[3,96,256]{2,1,0:T(8,128)(2,1)S(1)}, u32[]{:S(2)}, u32[]{:S(2)}) collective-permute-start(bf16[3,96,256]{2,1,0:T(8,128)(2,1)} %get-tuple-element.72), channel_id=1, source_target_pairs={{0,2},{1,3},{2,0},{3,1},{4,6},{5,7},{6,4},{7,5},{8,10},{9,11},{10,... | collective-permute-start | bytes 442376 | tf_op jit(solution)/shard_map/ppermute | solution.py:297
  124.0 16.0 %collective-permute-start.18 = (bf16[3,96,256]{2,1,0:T(8,128)(2,1)}, bf16[3,96,256]{2,1,0:T(8,128)(2,1)S(1)}, u32[]{:S(2)}, u32[]{:S(2)}) collective-permute-start(bf16[3,96,256]{2,1,0:T(8,128)(2,1)} %get-tuple-element.73), channel_id=1, source_target_pairs={{0,3},{1,2},{2,1},{3,0},{4,7},{5,6},{6,5},{7,4},{8,11},{9,10},{10,... | collective-permute-start | bytes 442376 | tf_op jit(solution)/shard_map/ppermute | solution.py:297
  135.1 2.4 %copy-start.10 = (bf16[3,96,256]{2,1,0:T(8,128)(2,1)S(1)}, bf16[3,96,256]{2,1,0:T(8,128)(2,1)}, u32[]{:S(2)}) copy-start(bf16[3,96,256]{2,1,0:T(8,128)(2,1)} %get-tuple-element.66) | copy-start | bytes 442372
  135.1 2.5 %copy-start.11 = (bf16[3,96,256]{2,1,0:T(8,128)(2,1)S(1)}, bf16[3,96,256]{2,1,0:T(8,128)(2,1)}, u32[]{:S(2)}) copy-start(bf16[3,96,256]{2,1,0:T(8,128)(2,1)} %get-tuple-element.70) | copy-start | bytes 442372
  135.1 2.5 %copy-start.14 = (bf16[2,96,256]{2,1,0:T(8,128)(2,1)S(1)}, bf16[2,96,256]{2,1,0:T(8,128)(2,1)}, u32[]{:S(2)}) copy-start(bf16[2,96,256]{2,1,0:T(8,128)(2,1)} %get-tuple-element.78) | copy-start | bytes 294916
  135.1 5.0 %collective-permute-start.19 = (bf16[2,96,256]{2,1,0:T(8,128)(2,1)}, bf16[2,96,256]{2,1,0:T(8,128)(2,1)S(1)}, u32[]{:S(2)}, u32[]{:S(2)}) collective-permute-start(bf16[2,96,256]{2,1,0:T(8,128)(2,1)} %get-tuple-element.76), channel_id=1, source_target_pairs={{0,1},{1,0},{2,3},{3,2},{4,5},{5,4},{6,7},{7,6},{8,9},{9,8},{10,11... | collective-permute-start | bytes 294920 | tf_op jit(solution)/shard_map/ppermute | solution.py:297
  135.2 9.4 %collective-permute-start.20 = (bf16[2,96,256]{2,1,0:T(8,128)(2,1)}, bf16[2,96,256]{2,1,0:T(8,128)(2,1)S(1)}, u32[]{:S(2)}, u32[]{:S(2)}) collective-permute-start(bf16[2,96,256]{2,1,0:T(8,128)(2,1)} %get-tuple-element.77), channel_id=1, source_target_pairs={{0,2},{1,3},{2,0},{3,1},{4,6},{5,7},{6,4},{7,5},{8,10},{9,11},{10,... | collective-permute-start | bytes 294920 | tf_op jit(solution)/shard_map/ppermute | solution.py:297
  137.5 2.6 %copy-start.12 = (bf16[2,96,256]{2,1,0:T(8,128)(2,1)S(1)}, bf16[2,96,256]{2,1,0:T(8,128)(2,1)}, u32[]{:S(2)}) copy-start(bf16[2,96,256]{2,1,0:T(8,128)(2,1)} %get-tuple-element.75) | copy-start | bytes 294916
  137.7 7.0 %collective-permute-start.21 = (bf16[2,96,256]{2,1,0:T(8,128)(2,1)S(1)}, bf16[2,96,256]{2,1,0:T(8,128)(2,1)S(1)}, u32[]{:S(2)}, u32[]{:S(2)}) collective-permute-start(bf16[2,96,256]{2,1,0:T(8,128)(2,1)S(1)} %copy-done.14), channel_id=1, source_target_pairs={{0,3},{1,2},{2,1},{3,0},{4,7},{5,6},{6,5},{7,4},{8,11},{9,10},{10,... | collective-permute-start | bytes 294920 | tf_op jit(solution)/shard_map/ppermute | solution.py:297
  144.7 1.1 copy-start.7
Sparse Core Ops, SparseCore 0:
  11.6 30.8 all-gather.2
